TPU v7x, 512 devices: a whole 4x4x16 slice. The times are simulated.
512 devices in a mesh: dp: 16 (over z_lo, core), fsdp: 32 (over y, z_hi, x).
Axes of the slice: x: 4, y: 4, z: 16 (z_hi: 2, z_lo: 8; z = z_hi * 8 + z_lo), core: 2. Of those that a mesh axis runs over, the one named last changes fastest.
Arguments:
- queries: bfloat16 [2048, 4096], P('dp', 'fsdp'), as said below
- passages: bfloat16 [2048, 4096], P('dp', 'fsdp'), as said below
- positive: int32 [2048], P('dp'), may hold values from 0 to 2047, each once
- hidden_states: bfloat16 [262144, 4096], P(('dp', 'fsdp')), may hold values from -6 to 6
- lengths: int32 [2048], P(('dp', 'fsdp')), may hold values from 1 to 128, as said below
- w_down: bfloat16 [4096, 128], P('fsdp'), may hold values from -0.09375 to 0.09375
- w_up: bfloat16 [128, 4096], P(None, 'fsdp'), may hold values from -0.5 to 0.5
Outputs:
- grad_queries: bfloat16 [2048, 4096], P('dp', 'fsdp')
- grad_passages: bfloat16 [2048, 4096], P('dp', 'fsdp')
- sub_embed: bfloat16 [2048, 4096], P(('dp', 'fsdp'))
- grad_down: float32 [4096, 128], P('fsdp')
- grad_up: float32 [128, 4096], P(None, 'fsdp')
Inputs may be any that keep to these rules, and one draw needn't show every extreme that they name: `queries`: entries of the cached query embeddings lie within -0.2 to 0.2. `passages`: entries of the cached page embeddings lie within -0.25 to 0.25. `lengths`: in every draw some page has length 128 and some page has length 1.
All inputs are finite; a program needn't handle non-finite values.
Results may differ from a plain program's by a relative error of at most 0.022.
Values may be sent and summed in bfloat16 or wider, within the bound.
No kernel may reach another device: no remote copies, remote signals or barrier semaphores. Data moves between devices by JAX's collectives and lax.ppermute only.
A program may use at most 64 MiB of HBM per device.

v0:
```python
import jax
import jax.numpy as jnp
from jax import lax
from jax.sharding import PartitionSpec as P

inv_temp = 20.0
eps = 1e-06


def adapter_terms(block_x, block_len, block_cot, w_down, w_up):
    xf = block_x.astype(jnp.float32)
    mean_sq = jnp.mean(xf * xf, axis=-1, keepdims=True)
    normed = (xf * lax.rsqrt(mean_sq + eps)).astype(jnp.bfloat16)
    pre = jnp.dot(normed, w_down, preferred_element_type=jnp.float32)
    act = jax.nn.silu(pre).astype(jnp.bfloat16)
    out = xf + jnp.dot(act, w_up, preferred_element_type=jnp.float32)
    pages = block_len.shape[0]
    page_len = block_x.shape[0] // pages
    places = jnp.arange(page_len, dtype=jnp.int32)
    valid = (places[None, :] < block_len[:, None]).astype(jnp.float32)
    weight = valid / block_len.astype(jnp.float32)[:, None]
    out3 = out.reshape(pages, page_len, out.shape[1])
    embed = jnp.sum(weight[:, :, None] * out3, axis=1).astype(jnp.bfloat16)
    act3 = act.astype(jnp.float32).reshape(pages, page_len, act.shape[1])
    pooled = jnp.sum(weight[:, :, None] * act3, axis=1).astype(jnp.bfloat16)
    dout = (
        (weight[:, :, None] * block_cot.astype(jnp.float32)[:, None, :])
        .reshape(block_x.shape[0], -1)
        .astype(jnp.bfloat16)
    )
    dact = lax.dot_general(dout, w_up, (((1,), (1,)), ((), ())), preferred_element_type=jnp.float32)
    sig = jax.nn.sigmoid(pre)
    dpre = (dact * sig * (1.0 + pre * (1.0 - sig))).astype(jnp.bfloat16)
    down_part = lax.dot_general(
        normed, dpre, (((0,), (0,)), ((), ())), preferred_element_type=jnp.float32
    )
    return (embed, down_part, pooled)


def local(queries, passages, positive, hidden_states, lengths, w_down, w_up):
    groups = lax.axis_size("fsdp")
    all_passages = lax.all_gather(passages, "dp", axis=0, tiled=True)
    total_pages = all_passages.shape[0]
    partial_value = lax.dot_general(
        queries, all_passages, (((1,), (1,)), ((), ())), preferred_element_type=jnp.float32
    )
    scores = inv_temp * lax.psum(partial_value, "fsdp")
    probs = jax.nn.softmax(scores, axis=-1)
    columns = jnp.arange(total_pages, dtype=jnp.int32)
    onehot = (positive[:, None] == columns[None, :]).astype(jnp.float32)
    coeff = (probs - onehot).astype(jnp.bfloat16)
    grad_queries = (
        inv_temp * jnp.dot(coeff, all_passages, preferred_element_type=jnp.float32)
    ).astype(jnp.bfloat16)
    summed_rows = lax.psum_scatter(
        lax.dot_general(
            coeff, queries, (((0,), (0,)), ((), ())), preferred_element_type=jnp.float32
        ),
        "dp",
        scatter_dimension=0,
        tiled=True,
    )
    grad_passages = (inv_temp * summed_rows).astype(jnp.bfloat16)
    pages = lengths.shape[0]
    page_cot = lax.all_to_all(grad_passages, "fsdp", split_axis=0, concat_axis=1, tiled=True)
    full_down, full_up = (
        lax.all_gather(w_down, "fsdp", axis=0, tiled=True),
        lax.all_gather(w_up, "fsdp", axis=1, tiled=True),
    )
    sub_embed, down_part, pooled = adapter_terms(
        hidden_states, lengths, page_cot, full_down, full_up
    )
    group_pooled = lax.all_gather(pooled, "fsdp", axis=0, tiled=True)
    width = grad_passages.shape[1]
    pooled3 = group_pooled.reshape(groups, pages, group_pooled.shape[1])
    cot3 = grad_passages.reshape(groups, pages, width)
    terms = jnp.einsum("jsr,jsd->jrd", pooled3, cot3, preferred_element_type=jnp.float32)
    up_shard = jnp.sum(terms.astype(jnp.bfloat16).astype(jnp.float32), axis=0)
    down_rounded = down_part.astype(jnp.bfloat16).astype(jnp.float32)
    down_shard = lax.psum_scatter(down_rounded, "fsdp", scatter_dimension=0, tiled=True)
    grad_down, grad_up = lax.psum((down_shard, up_shard), "dp")
    return (grad_queries, grad_passages, sub_embed, grad_down, grad_up)


def solution(mesh):
    placed = (
        P("dp", "fsdp"),
        P("dp", "fsdp"),
        P("dp"),
        P(("dp", "fsdp"), None),
        P(("dp", "fsdp")),
        P("fsdp", None),
        P(None, "fsdp"),
    )
    return jax.shard_map(
        local,
        mesh=mesh,
        in_specs=placed,
        out_specs=(
            P("dp", "fsdp"),
            P("dp", "fsdp"),
            P(("dp", "fsdp"), None),
            P("fsdp", None),
            P(None, "fsdp"),
        ),
        check_vma=False,
    )
```

profile of v0, /device:TPU:1, one launch (start us, length us, event | category | flops | bytes accessed | tf_op | source)
XLA Modules:
  0.0 1466.3 jit_solution(10283782004232753234)
XLA Ops:
  7.2 0.0 copy-start
  7.2 0.0 copy-start.2
  7.2 0.0 all-reduce.4.cloned.1.call-start
  7.2 40.3 %all_gather.12 = bf16[2048,128]{1,0:T(8,128)(2,1)S(1)} all-gather(bf16[128,128]{1,0:T(8,128)(2,1)} %param.8), channel_id=1, replica_groups=mesh['dp'=16,'fsdp'=32] {'dp'}, dimensions={0}, use_global_device_ids=true | all-gather | bytes 557056 | tf_op jit(solution)/shard_map/all_gather | solution.py:42
  47.5 0.0 copy-done
  47.5 0.0 copy-start.3
  47.5 1.3 fusion.18
  48.8 0.0 all-reduce.4.cloned.1.call-update
  48.9 0.0 reduce-scatter.3.cloned.1.call-start
  48.9 553.5 %all-reduce.4.cloned.1.call-done = f32[128,2048]{1,0:T(8,128)} async-done(((f32[128,2048]{1,0:T(8,128)}), f32[128,2048]{1,0:T(8,128)}) %all-reduce.4.cloned.1.call-update) | async-done | bytes 1048592 | tf_op jit(solution)/shard_map/psum | solution.py:47
  602.4 1.4 multiply_reduce_fusion.1
  603.8 1.5 fusion.10
  605.3 0.0 copy-done.2
  605.3 1.6 subtract_convert_fusion
  607.0 1.4 fusion.19
  608.3 0.0 reduce-scatter.3.cloned.1.call-update
  608.4 0.0 all-gather.4.cloned.1.call-start
  608.4 0.7 all-gather.4.cloned.1.call-update
  609.1 0.0 all-gather.6.cloned.1.call-start
  609.1 0.5 all-gather.6.cloned.1.call-update
  609.7 0.0 copy-done.3
  609.7 3.1 fusion
  612.8 115.7 %reduce-scatter.3.cloned.1.call-done = f32[128,128]{1,0:T(8,128)} async-done(((f32[2048,128]{1,0:T(8,128)}), f32[128,128]{1,0:T(8,128)}) %reduce-scatter.3.cloned.1.call-update) | async-done | bytes 65552 | tf_op jit(solution)/shard_map/reduce_scatter | solution.py:55
  728.5 1.5 multiply_convert_fusion.1
  730.0 16.1 %all-to-all-start = ((bf16[32,4,128]{2,1,0:T(4,128)(2,1)}), bf16[32,4,128]{2,1,0:T(4,128)(2,1)S(1)}, u32[]{:S(2)}, u32[]{:S(2)}) async-start(bf16[32,4,128]{2,1,0:T(4,128)(2,1)} %bitcast.2), calls=%async_computation.1 | async-start | bytes 65536 | tf_op jit(solution)/shard_map/all_to_all | solution.py:65
  746.1 0.0 reduce-scatter.5.cloned.1.call-start
  746.1 0.1 fusion.17
  746.2 98.5 %all-gather.4.cloned.1.call-done = bf16[4096,128]{1,0:T(8,128)(2,1)} async-done(((bf16[128,128]{1,0:T(8,128)(2,1)}), bf16[4096,128]{1,0:T(8,128)(2,1)}) %all-gather.4.cloned.1.call-update) | async-done | bytes 1048592 | tf_op jit(solution)/shard_map/all_gather | solution.py:67
  844.7 3.8 fusion.11
  848.5 0.0 all-to-all-done
  848.5 3.0 fusion.2
  851.6 102.1 %all-gather.6.cloned.1.call-done = bf16[128,4096]{1,0:T(8,128)(2,1)} async-done(((bf16[128,128]{1,0:T(8,128)(2,1)}), bf16[128,4096]{1,0:T(8,128)(2,1)}) %all-gather.6.cloned.1.call-update) | async-done | bytes 1048592 | tf_op jit(solution)/shard_map/all_gather | solution.py:68
  953.7 9.5 fusion.3
  963.2 0.0 copy-start.1
  963.2 0.0 reduce-scatter.5.cloned.1.call-update
  963.2 0.0 all-reduce.6.cloned.1.call-start
  963.3 133.1 %all-gather = bf16[32,4,128]{2,1,0:T(4,128)(2,1)S(1)} all-gather(bf16[1,4,128]{2,1,0:T(4,128)(2,1)S(1)} %bitcast.32), channel_id=1, replica_groups=mesh['dp'=16,'fsdp'=32] {'fsdp'}, dimensions={0}, use_global_device_ids=true | all-gather | bytes 33792 | tf_op jit(solution)/shard_map/all_gather | solution.py:73
  1096.4 1.9 convert_reduce_fusion
  1098.3 146.6 %reduce-scatter.5.cloned.1.call-done = f32[128,128]{1,0:T(8,128)} async-done(((f32[4096,128]{1,0:T(8,128)}), f32[128,128]{1,0:T(8,128)}) %reduce-scatter.5.cloned.1.call-update) | async-done | bytes 65552 | tf_op jit(solution)/shard_map/reduce_scatter | solution.py:80
  1244.9 0.0 all-reduce.6.cloned.1.call-update
  1245.0 0.9 fusion.9
  1245.9 0.0 copy-done.1
  1245.9 4.3 multiply_reduce_fusion
  1250.2 206.3 %all-reduce.6.cloned.1.call-done = (f32[128,128]{1,0:T(8,128)}, f32[128,128]{1,0:T(8,128)}) async-done(((f32[128,128]{1,0:T(8,128)}, f32[128,128]{1,0:T(8,128)}), (f32[128,128]{1,0:T(8,128)}, f32[128,128]{1,0:T(8,128)})) %all-reduce.6.cloned.1.call-update) | async-done | bytes 131088 | tf_op jit(solution)/shard_map/psum | solution.py:81
  1456.5 1.5 copy.15
  1458.0 1.5 copy.16
  (3 shorter events, 0.0 us)
Async XLA Ops:
  7.2 40.3 %copy-start = (bf16[128,128]{1,0:T(8,128)(2,1)S(1)}, bf16[128,128]{1,0:T(8,128)(2,1)}, u32[]{:S(2)}) copy-start(bf16[128,128]{1,0:T(8,128)(2,1)} %param.7) | copy-start | bytes 98308
  7.2 598.2 %copy-start.2 = (s32[128]{0:T(128)S(1)}, s32[128]{0:T(128)}, u32[]{:S(2)}) copy-start(s32[128]{0:T(128)} %param.9) | copy-start | bytes 1540
  7.2 595.2 %all-reduce.4.cloned.1.call-start = ((), (), s32[]{:S(2)}) async-start(), calls=%async_computation.3 | async-start | bytes 2097152 | tf_op jit(solution)/shard_map/psum | solution.py:47
  47.5 562.2 %copy-start.3 = (s32[4]{0:T(128)S(1)}, s32[4]{0:T(128)}, u32[]{:S(2)}) copy-start(s32[4]{0:T(128)} %param.11) | copy-start | bytes 52
  48.9 679.7 %reduce-scatter.3.cloned.1.call-start = ((), (), s32[]{:S(2)}) async-start(), calls=%async_computation.4 | async-start | bytes 1114112 | tf_op jit(solution)/shard_map/reduce_scatter | solution.py:55
  608.4 236.3 %all-gather.4.cloned.1.call-start = ((), (), s32[]{:S(2)}) async-start(), calls=%async_computation.5 | async-start | bytes 1081344 | tf_op jit(solution)/shard_map/all_gather | solution.py:67
  609.1 344.6 %all-gather.6.cloned.1.call-start = ((), (), s32[]{:S(2)}) async-start(), calls=%async_computation.6 | async-start | bytes 1081344 | tf_op jit(solution)/shard_map/all_gather | solution.py:68
  730.0 118.5 %all-to-all-start = ((bf16[32,4,128]{2,1,0:T(4,128)(2,1)}), bf16[32,4,128]{2,1,0:T(4,128)(2,1)S(1)}, u32[]{:S(2)}, u32[]{:S(2)}) async-start(bf16[32,4,128]{2,1,0:T(4,128)(2,1)} %bitcast.2), calls=%async_computation.1 | async-start | bytes 65536 | tf_op jit(solution)/shard_map/all_to_all | solution.py:65
  746.1 498.9 %reduce-scatter.5.cloned.1.call-start = ((), (), s32[]{:S(2)}) async-start(), calls=%async_computation.7 | async-start | bytes 2162688 | tf_op jit(solution)/shard_map/reduce_scatter | solution.py:80
  963.2 282.6 %copy-start.1 = (bf16[128,4096]{1,0:T(8,128)(2,1)S(1)}, bf16[128,4096]{1,0:T(8,128)(2,1)}, u32[]{:S(2)}) copy-start(bf16[128,4096]{1,0:T(8,128)(2,1)} %all-gather.6.cloned.1.call-done) | copy-start | bytes 3145732
  963.2 493.2 %all-reduce.6.cloned.1.call-start = ((), (), s32[]{:S(2)}) async-start(), calls=%async_computation.8 | async-start | bytes 262144 | tf_op jit(solution)/shard_map/psum | solution.py:81
Sparse Core Ops, SparseCore 0:
  49.0 553.3 all-reduce.3
  608.5 120.0 reduce-scatter.2
  732.8 111.8 all-gather.3
  848.6 105.0 all-gather.5
  963.4 281.5 reduce-scatter.4
  1248.6 207.8 all-reduce.5
where the time goes:
time: 1470 us
  waiting for transfers between devices  1220 us (83%)
  blocking collectives  173 us (12%)
  matrix products  23.2 us (2%)
  starting transfers between devices  16.3 us (1%)
    psum x1, waiting for transfers between devices, local(): scores = inv_temp * lax.psum(partial_value, 'fsdp')  554 us
    psum x1, waiting for transfers between devices, local(): grad_down, grad_up = lax.psum((down_shard, up_shard), 'dp')  206 us
    reduce_scatter x1, waiting for transfers between devices, local(): lax.psum_scatter(down_rounded, 'fsdp', scatter_dimension=0, tiled=True)  147 us
    all_gather x1, blocking collectives, local(): group_pooled = lax.all_gather(pooled, 'fsdp', axis=0, tiled=True)  133 us
    reduce_scatter x1, waiting for transfers between devices, local(): lax.psum_scatter(lax.dot_general(coeff, queries, (((0,), (0,)), ((), ()))...  116 us
    all_gather x1, waiting for transfers between devices, local(): lax.all_gather(w_up, 'fsdp', axis=1, tiled=True)  102 us
    all_gather x1, waiting for transfers between devices, local(): lax.all_gather(w_down, 'fsdp', axis=0, tiled=True)  98.5 us
    all_gather x1, blocking collectives, local(): all_passages = lax.all_gather(passages, 'dp', axis=0, tiled=True)  40.3 us
  transfers between devices with their start and end apart: 7, of which 6 were waited for; matrix products, arithmetic and copies ran while one was open for 1% of the time, Pallas kernels for 0%

commit v1 on v0

v1 whole, which is shorter than its diff:
```python
import jax
import jax.numpy as jnp
import numpy as np
from jax import lax
from jax.sharding import Mesh, PartitionSpec as P

inv_temp = 20.0
eps = 1e-06
bf16 = jnp.bfloat16
f32 = jnp.float32


def exchange(x, axes):
    return lax.all_to_all(x, axes, split_axis=0, concat_axis=0, tiled=False)


def spread(x, count):
    return jnp.broadcast_to(x[None], (count,) + x.shape)


def swap(x, axis):
    return lax.ppermute(x, axis, [(0, 1), (1, 0)])


def in_order(first, mine, other):
    return jnp.where(first, jnp.stack([mine, other]), jnp.stack([other, mine]))


def local(queries, passages, positive, hidden, lengths, w_down, w_up):
    zl_n, y_n, x_n = lax.axis_size("zl"), lax.axis_size("y"), lax.axis_size("x")
    c, y, h, x = (lax.axis_index(a) for a in ("c", "y", "h", "x"))
    plane = y_n * x_n
    rows, width = queries.shape
    pages, rank = lengths.shape[0], w_down.shape[1]
    tokens = hidden.shape[0]
    half = plane * pages

    pack = jnp.concatenate([queries, w_up, w_down], axis=0)
    both = in_order(h == 0, pack, swap(pack, "h"))
    q_mine = both[:, :rows]
    up2 = both[:, rows : rows + rank]
    down2 = both[:, rows + rank :]
    q_both = in_order(c == 0, q_mine, swap(q_mine, "c"))
    q_all = q_both.transpose(0, 2, 1, 3).reshape(2 * rows, 2 * width)

    p_sub = passages.reshape(y_n, 2, x_n * pages, width).transpose(1, 0, 2, 3)
    p_sub = p_sub.reshape(2, half, width)
    p_got = exchange(spread(p_sub, zl_n).reshape(zl_n * 2, half, width), ("zl", "h"))
    p_all = p_got.reshape(zl_n, 2, half, width).transpose(0, 2, 1, 3)
    p_all = p_all.reshape(zl_n * half, 2 * width)
    cols = zl_n * half

    part = lax.dot_general(q_all, p_all, (((1,), (1,)), ((), ())), preferred_element_type=f32)
    q_c = jnp.where(c == 0, q_all[:, :width], q_all[:, width:])
    up_c = jnp.where(c == 0, up2[0], up2[1])
    qw_part = lax.dot_general(q_c, up_c, (((1,), (1,)), ((), ())), preferred_element_type=f32)
    own = 2 * rows // (2 * plane)
    sent = jnp.concatenate([part, qw_part], axis=1).reshape(2 * plane, own, cols + rank)
    got = jnp.sum(exchange(sent, ("c", "y", "x")).reshape(2, plane, own, cols + rank), axis=1)
    scores = inv_temp * got[:, :, :cols]
    qw = got[0, :, cols:] + got[1, :, cols:]
    top = jnp.max(scores, axis=(0, 2))
    e = jnp.exp(scores - top[None, :, None])
    total = jnp.sum(e, axis=(0, 2))
    lane = lax.broadcasted_iota(jnp.int32, (own, 128), 1)
    stats = swap(jnp.where(lane < 64, top[:, None], total[:, None]), "h")
    top_o, total_o = stats[:, 0], stats[:, 64]
    top_a = jnp.maximum(top, top_o)
    scale = jnp.exp(top - top_a)
    z = total * scale + total_o * jnp.exp(top_o - top_a)
    probs = e * (scale / z)[None, :, None]
    k = np.arange(cols)
    base = k // half * (4 * half) + k % half // (x_n * pages) * (2 * x_n * pages) + k % (x_n * pages)
    base = np.stack([base, base + 2 * half]).astype(np.int32)
    target = lax.dynamic_slice(positive, ((y * x_n + x) * own,), (own,)) - h * (x_n * pages)
    onehot = (target[None, :, None] == base[:, None, :]).astype(f32)
    coeff_own = (probs - onehot).astype(bf16)
    qw_b = jnp.broadcast_to(qw.astype(bf16)[None], (2, own, rank))
    sent = jnp.concatenate([coeff_own, qw_b], axis=2)
    sent = jnp.broadcast_to(sent[:, None], (2, plane, own, cols + rank))
    got = exchange(sent.reshape(2 * plane, own, cols + rank), ("c", "y", "x"))
    got = got.reshape(2 * rows, cols + rank)
    coeff, qw_all = got[:, :cols], got[:, cols:]

    c_mine = coeff.reshape(2 * rows, zl_n, plane, pages)
    c_mine = lax.dynamic_slice_in_dim(c_mine, y * x_n + x, 1, axis=2)[:, :, 0]
    dact_part = lax.dot_general(
        c_mine.reshape(2 * rows, zl_n * pages), qw_all, (((0,), (0,)), ((), ())), preferred_element_type=f32
    )
    dact = inv_temp * jnp.sum(exchange(dact_part.reshape(zl_n, pages, rank), ("zl",)), axis=0)

    wd = exchange(spread(down2, plane), ("y", "x"))
    wd = wd.reshape(y_n, x_n, 2, width, rank).transpose(0, 2, 1, 3, 4).reshape(-1, rank)
    xf = hidden.astype(f32)
    rs = lax.rsqrt(jnp.mean(xf * xf, axis=-1, keepdims=True) + eps)
    normed = (xf * rs).astype(bf16)
    pre = jnp.dot(normed, wd, preferred_element_type=f32)
    sig = jax.nn.sigmoid(pre)
    act = (pre * sig).astype(bf16)
    span = tokens // pages
    place = jnp.arange(tokens, dtype=jnp.int32)
    page_of, at = place // span, place % span
    mask = (page_of[None, :] == jnp.arange(pages)[:, None]) & (at[None, :] < lengths[:, None])
    mask = mask.astype(bf16)
    inv_len = 1.0 / lengths.astype(f32)
    x_mean = jnp.dot(mask, hidden, preferred_element_type=f32) * inv_len[:, None]
    pooled = (jnp.dot(mask, act, preferred_element_type=f32) * inv_len[:, None]).astype(bf16)
    weight = (at.reshape(pages, span) < lengths[:, None]).astype(f32) * inv_len[:, None]
    g = (sig * (1.0 + pre * (1.0 - sig)) * rs).reshape(pages, span, rank) * weight[:, :, None]

    pooled_xy = exchange(spread(pooled, plane), ("y", "x")).reshape(half, rank)
    pooled_all = exchange(spread(pooled_xy, zl_n), ("zl",)).reshape(cols, rank)
    lift = jnp.einsum("pr,hrf->phf", pooled_xy, up2, preferred_element_type=f32)
    lift = exchange(lift.reshape(plane, pages, 2 * width), ("y", "x"))
    lift = lift.reshape(y_n, x_n, pages, 2, width).transpose(2, 0, 3, 1, 4).reshape(pages, -1)
    sub_embed = (x_mean + lift).astype(bf16)

    gp = lax.dot_general(coeff, q_all, (((0,), (0,)), ((), ())), preferred_element_type=f32)
    gp = gp.astype(bf16).reshape(zl_n, half, 2, width).transpose(0, 2, 1, 3)
    gp = exchange(gp.reshape(zl_n * 2, half, width), ("zl", "h")).astype(f32)
    gp = inv_temp * jnp.sum(gp.reshape(zl_n, 2, half, width), axis=0)
    grad_passages = gp.reshape(2, y_n, x_n * pages, width).transpose(1, 0, 2, 3)
    grad_passages = grad_passages.reshape(-1, width).astype(bf16)
    gq = jnp.dot(coeff, p_all, preferred_element_type=f32)
    gq = gq.reshape(2, rows, 2, width).transpose(0, 2, 1, 3).astype(bf16)
    gq = exchange(gq.reshape(4, rows, width), ("c", "h")).astype(f32)
    grad_queries = (inv_temp * jnp.sum(gq, axis=0)).astype(bf16)

    u = (inv_temp * jnp.dot(coeff, pooled_all, preferred_element_type=f32)).astype(bf16)
    up_part = lax.dot_general(u, q_all, (((0,), (0,)), ((), ())), preferred_element_type=f32)
    up_part = up_part.astype(bf16).reshape(zl_n, rank // zl_n, 2, width).transpose(0, 2, 1, 3)
    dpre = (g * dact[:, None, :]).astype(bf16).reshape(tokens, rank)
    down = lax.dot_general(dpre, hidden, (((0,), (0,)), ((), ())), preferred_element_type=f32)
    down = down.astype(bf16).reshape(2, rank // 2, y_n, 2, x_n, width).transpose(0, 2, 4, 3, 1, 5)
    down = exchange(down.reshape(2 * plane, 2, rank // 2, width), ("c", "y", "x")).astype(f32)
    down = jnp.sum(down, axis=0).astype(bf16)
    down = down.reshape(2, zl_n, rank // 2 // zl_n, width).transpose(1, 0, 2, 3)
    sent = jnp.concatenate([down, up_part], axis=2)
    step = sent.shape[2]
    got = exchange(sent.reshape(zl_n * 2, step, width), ("zl", "h")).astype(f32)
    got = exchange(spread(jnp.sum(got, axis=0), zl_n * 2), ("zl", "c"))
    got = got.reshape(zl_n, 2, step, width)
    n = rank // 2 // zl_n
    grad_down = got[:, :, :n].transpose(1, 0, 2, 3).reshape(rank, width).T
    grad_up = jnp.sum(got[:, :, n:], axis=1).reshape(rank, width)
    return (grad_queries, grad_passages, sub_embed, grad_down, grad_up)


def solution(mesh):
    dp, fsdp = ("zl", "c"), ("y", "h", "x")
    shape = (mesh.shape["dp"] // 2, 2, 4, 2, mesh.shape["fsdp"] // 8)
    inner = Mesh(mesh.devices.reshape(shape), dp + fsdp)
    both = dp + fsdp
    return jax.shard_map(
        local,
        mesh=inner,
        in_specs=(P(dp, fsdp), P(dp, fsdp), P(dp), P(both, None), P(both), P(fsdp, None), P(None, fsdp)),
        out_specs=(P(dp, fsdp), P(dp, fsdp), P(both, None), P(fsdp, None), P(None, fsdp)),
        check_vma=False,
    )
```

time: 1470 us -> 288 us (0.20)
  waiting for transfers between devices: 1220 us -> 136 us
  blocking collectives: 173 us -> 21.9 us
  starting transfers between devices: 16.3 us -> 95.2 us
    psum x2 -> x0, waiting for transfers between devices: 760 us -> none  [the longest x1 554 us: local(): scores = inv_temp * lax.psum(partial_value, 'fsdp')]
    reduce_scatter x2 -> x0, waiting for transfers between devices: 262 us -> none  [the longest x1 147 us: local(): lax.psum_scatter(down_rounded, 'fsdp', scatter_dimension=0, tiled=True)]
    all_gather x2 -> x0, waiting for transfers between devices: 201 us -> none  [the longest x1 102 us: local(): lax.all_gather(w_up, 'fsdp', axis=1, tiled=True)]
    all_gather x2 -> x0, blocking collectives: 173 us -> none  [the longest x1 133 us: local(): group_pooled = lax.all_gather(pooled, 'fsdp', axis=0, tiled=True)]
    all_to_all x1 -> x11, waiting for transfers between devices: 0.01 us -> 108 us  [exchange(): return lax.all_to_all(x, axes, split_axis=0, concat_axis=0, tiled=False)]
    all_to_all x1 -> x11, starting transfers between devices: 16.1 us -> 74.8 us  [exchange(): return lax.all_to_all(x, axes, split_axis=0, concat_axis=0, tiled=False)]
    ppermute x0 -> x3, waiting for transfers between devices: none -> 27.7 us  [swap(): return lax.ppermute(x, axis, [(0, 1), (1, 0)])]
    all_to_all x0 -> x2, blocking collectives: none -> 21.9 us  [exchange(): return lax.all_to_all(x, axes, split_axis=0, concat_axis=0, tiled=False)]
  transfers between devices with their start and end apart: 7 -> 14, of which waited for: 6 -> 13; matrix products, arithmetic and copies ran while one was open for 1% -> 7% of each run, Pallas kernels for 0% -> 0%
where the time goes in v1:
time: 288 us; the launch traced here: 286 us
  waiting for transfers between devices  136 us (47%)
  starting transfers between devices  95.2 us (33%)
  blocking collectives  21.9 us (8%)
  matrix products  13 us (5%)
  local copies, waits for them, and re-layouts  12.7 us (4%)
  other arithmetic  6.92 us (2%)
    all_to_all x11, waiting for transfers between devices, exchange(): return lax.all_to_all(x, axes, split_axis=0, concat_axis=0, tiled=False)  108 us
    all_to_all x11, starting transfers between devices, exchange(): return lax.all_to_all(x, axes, split_axis=0, concat_axis=0, tiled=False)  74.8 us
    ppermute x3, waiting for transfers between devices, swap(): return lax.ppermute(x, axis, [(0, 1), (1, 0)])  27.7 us
    all_to_all x2, blocking collectives, exchange(): return lax.all_to_all(x, axes, split_axis=0, concat_axis=0, tiled=False)  21.9 us
    ppermute x3, starting transfers between devices, swap(): return lax.ppermute(x, axis, [(0, 1), (1, 0)])  20.3 us
  transfers between devices with their start and end apart: 14, of which 13 were waited for; matrix products, arithmetic and copies ran while one was open for 7% of the time, Pallas kernels for 0%

profile of v1, /device:TPU:1, one launch (start us, length us, event | category | flops | bytes accessed | tf_op | source)
XLA Modules:
  0.0 286.4 jit_solution(6525402548918429517)
XLA Ops:
  0.7 0.8 copy.49
  1.4 0.7 broadcast_in_dim.37
  2.2 15.7 %all-to-all-start = ((bf16[16,64,128]{2,1,0:T(8,128)(2,1)}), bf16[16,64,128]{2,1,0:T(8,128)(2,1)S(1)}, u32[]{:S(2)}, u32[]{:S(2)}) async-start(bf16[16,64,128]{2,1,0:T(8,128)(2,1)} %bitcast.8), calls=%async_computation | async-start | bytes 524288 | tf_op jit(solution)/shard_map/all_to_all | solution.py:14
  17.9 0.8 constant_dynamic-update-slice_fusion.2
  18.7 0.8 constant_dynamic-update-slice_fusion.1
  19.4 0.8 constant_dynamic-update-slice_fusion
  20.2 12.0 %collective-permute-start = (bf16[384,128]{1,0:T(8,128)(2,1)S(1)}, bf16[384,128]{1,0:T(8,128)(2,1)S(1)}, u32[]{:S(2)}, u32[]{:S(2)}) collective-permute-start(bf16[384,128]{1,0:T(8,128)(2,1)S(1)} %constant_dynamic-update-slice_fusion), channel_id=1, source_target_pairs={{0,4},{4,0},{1,5},{5,1},{2,6},{6,2},{3,7},{7,3},{8,12},{12,8},{9,1... | collective-permute-start | bytes 294920 | tf_op jit(solution)/shard_map/ppermute | solution.py:22
  32.2 16.1 %collective-permute-done = bf16[384,128]{1,0:T(8,128)(2,1)S(1)} collective-permute-done((bf16[384,128]{1,0:T(8,128)(2,1)S(1)}, bf16[384,128]{1,0:T(8,128)(2,1)S(1)}, u32[]{:S(2)}, u32[]{:S(2)}) %collective-permute-start) | collective-permute-done | bytes 98336 | tf_op jit(solution)/shard_map/ppermute | solution.py:22
  48.4 3.1 %collective-permute-start.1 = (bf16[2,128,128]{2,1,0:T(8,128)(2,1)S(1)}, bf16[2,128,128]{2,1,0:T(8,128)(2,1)S(1)}, u32[]{:S(2)}, u32[]{:S(2)}) collective-permute-start(bf16[2,128,128]{2,1,0:T(8,128)(2,1)S(1)} %get-tuple-element.23), channel_id=1, source_target_pairs={{0,32},{32,0},{1,33},{33,1},{2,34},{34,2},{3,35},{35,3},{4,36},{36... | collective-permute-start | bytes 196616 | tf_op jit(solution)/shard_map/ppermute | solution.py:22
  51.5 0.9 collective-permute-done.1
  53.3 0.9 maximum_bitcast_fusion
  54.2 7.4 %all-to-all-start.1 = ((f32[32,8,640]{2,1,0:T(8,128)}), f32[32,8,640]{2,1,0:T(8,128)S(1)}, u32[]{:S(2)}, u32[]{:S(2)}) async-start(f32[32,8,640]{2,1,0:T(8,128)} %maximum_bitcast_fusion), calls=%async_computation.1 | async-start | bytes 1310720 | tf_op jit(solution)/shard_map/all_to_all | solution.py:14
  61.7 12.2 %all-to-all-done.1 = f32[32,8,640]{2,1,0:T(8,128)S(1)} async-done(((f32[32,8,640]{2,1,0:T(8,128)}), f32[32,8,640]{2,1,0:T(8,128)S(1)}, u32[]{:S(2)}, u32[]{:S(2)}) %all-to-all-start.1) | async-done | bytes 655392 | tf_op jit(solution)/shard_map/all_to_all | solution.py:14
  74.4 5.3 %collective-permute-start.2 = (f32[8,128]{0,1:T(8,128)S(1)}, f32[8,128]{0,1:T(8,128)S(1)}, u32[]{:S(2)}, u32[]{:S(2)}) collective-permute-start(f32[8,128]{0,1:T(8,128)S(1)} %broadcast_select_fusion), channel_id=1, source_target_pairs={{0,4},{4,0},{1,5},{5,1},{2,6},{6,2},{3,7},{7,3},{8,12},{12,8},{9,1... | collective-permute-start | bytes 12296 | tf_op jit(solution)/shard_map/ppermute | solution.py:22
  79.7 10.7 %collective-permute-done.2 = f32[8,128]{0,1:T(8,128)S(1)} collective-permute-done((f32[8,128]{0,1:T(8,128)S(1)}, f32[8,128]{0,1:T(8,128)S(1)}, u32[]{:S(2)}, u32[]{:S(2)}) %collective-permute-start.2) | collective-permute-done | bytes 4128 | tf_op jit(solution)/shard_map/ppermute | solution.py:22
  90.6 12.7 %all_to_all.65 = bf16[32,8,640]{2,1,0:T(8,128)(2,1)S(1)} all-to-all(bf16[32,8,640]{2,1,0:T(8,128)(2,1)S(1)} %bitcast.148), channel_id=1, replica_groups=mesh['zl'=8,'c'=2,'y'=4,'h'=2,'x'=4] {'c','y','x'}, dimensions={0} | all-to-all | bytes 655360 | tf_op jit(solution)/shard_map/all_to_all | solution.py:14
  103.2 1.2 broadcast_in_dim.43
  104.5 3.8 %all-to-all-start.5 = ((bf16[16,2,128,128]{3,2,1,0:T(8,128)(2,1)}), bf16[16,2,128,128]{3,2,1,0:T(8,128)(2,1)S(1)}, u32[]{:S(2)}, u32[]{:S(2)}) async-start(bf16[16,2,128,128]{3,2,1,0:T(8,128)(2,1)} %broadcast_in_dim.43), calls=%async_computation.5 | async-start | bytes 2097152 | tf_op jit(solution)/shard_map/all_to_all | solution.py:14
  108.3 3.1 %fusion = f32[512]{0:T(512)S(1)} fusion(bf16[512,4096]{1,0:T(8,128)(2,1)} %param.11), kind=kLoop, calls=%fused_computation.2 | loop fusion | flops 6290944 | bytes 4196352 | tf_op jit(solution)/shard_map/reduce_sum | solution.py:95
  111.7 0.7 fusion.14
  112.5 11.6 %all-to-all-done.5 = bf16[16,2,128,128]{3,2,1,0:T(8,128)(2,1)S(1)} async-done(((bf16[16,2,128,128]{3,2,1,0:T(8,128)(2,1)}), bf16[16,2,128,128]{3,2,1,0:T(8,128)(2,1)S(1)}, u32[]{:S(2)}, u32[]{:S(2)}) %all-to-all-start.5) | async-done | bytes 1048608 | tf_op jit(solution)/shard_map/all_to_all | solution.py:14
  124.1 3.3 %all-to-all-start.8 = ((f32[8,4,128]{2,1,0:T(4,128)}), f32[8,4,128]{2,1,0:T(4,128)S(1)}, u32[]{:S(2)}, u32[]{:S(2)}) async-start(f32[8,4,128]{2,1,0:T(4,128)} %fusion.14), calls=%async_computation.8 | async-start | bytes 32768 | tf_op jit(solution)/shard_map/all_to_all | solution.py:14
  127.6 9.2 %all-to-all-done.8 = f32[8,4,128]{2,1,0:T(4,128)S(1)} async-done(((f32[8,4,128]{2,1,0:T(4,128)}), f32[8,4,128]{2,1,0:T(4,128)S(1)}, u32[]{:S(2)}, u32[]{:S(2)}) %all-to-all-start.8) | async-done | bytes 16416 | tf_op jit(solution)/shard_map/all_to_all | solution.py:14
  136.8 3.5 %fusion.11 = (bf16[512,128]{1,0:T(8,128)(2,1)S(1)}, f32[512,128]{1,0:T(8,128)S(1)}) fusion(f32[4,128]{1,0:T(4,128)S(1)} %broadcast_multiply_fusion, f32[512]{0:T(512)S(1)} %get-tuple-element.26, f32[512]{0:T(512)S(1)} %get-tuple-element.27, bf16[4096,128]{1,0:T(8,128)(2,1)S(1)} %bitcast.140, bf16[512,4096]{1,0:T(8,128)(2,1)} %param.11), kind=kOutput, calls=%fused_computation.24 | convolution fusion | flops 543883264 | bytes 5642240 | tf_op jit(solution)/shard_map/dot_general | solution.py:97
  141.1 4.2 %all-to-all-start.6 = ((bf16[16,4,128]{2,1,0:T(4,128)(2,1)}), bf16[16,4,128]{2,1,0:T(4,128)(2,1)S(1)}, u32[]{:S(2)}, u32[]{:S(2)}) async-start(bf16[16,4,128]{2,1,0:T(4,128)(2,1)} %broadcast_in_dim.44), calls=%async_computation.6 | async-start | bytes 32768 | tf_op jit(solution)/shard_map/all_to_all | solution.py:14
  145.5 6.3 %all-to-all-done.6 = bf16[16,4,128]{2,1,0:T(4,128)(2,1)S(1)} async-done(((bf16[16,4,128]{2,1,0:T(4,128)(2,1)}), bf16[16,4,128]{2,1,0:T(4,128)(2,1)S(1)}, u32[]{:S(2)}, u32[]{:S(2)}) %all-to-all-start.6) | async-done | bytes 16416 | tf_op jit(solution)/shard_map/all_to_all | solution.py:14
  152.0 9.3 %all_to_all.66 = f32[16,4,256]{2,1,0:T(4,128)S(1)} all-to-all(f32[16,4,256]{2,1,0:T(4,128)S(1)} %copy.58), channel_id=1, replica_groups=mesh['zl'=8,'c'=2,'y'=4,'h'=2,'x'=4] {'y','x'}, dimensions={0} | all-to-all | bytes 131072 | tf_op jit(solution)/shard_map/all_to_all | solution.py:14
  161.2 0.7 broadcast_in_dim.46
  161.9 3.4 %all-to-all-start.10 = ((bf16[8,64,128]{2,1,0:T(8,128)(2,1)}), bf16[8,64,128]{2,1,0:T(8,128)(2,1)S(1)}, u32[]{:S(2)}, u32[]{:S(2)}) async-start(bf16[8,64,128]{2,1,0:T(8,128)(2,1)} %broadcast_in_dim.46), calls=%async_computation.10 | async-start | bytes 262144 | tf_op jit(solution)/shard_map/all_to_all | solution.py:14
  165.3 2.9 %convolution_convert_fusion = bf16[128,4096]{1,0:T(8,128)(2,1)S(1)} fusion(bf16[512,128]{1,0:T(8,128)(2,1)S(1)} %get-tuple-element.24, bf16[512,4096]{1,0:T(8,128)(2,1)} %param.11), kind=kOutput, calls=%fused_computation.4 | convolution fusion | flops 537395200 | bytes 5373952 | tf_op jit(solution)/shard_map/dot_general | solution.py:133
  168.2 0.8 reshape.251
  169.0 1.4 copy.63
  170.4 5.1 %all-to-all-done.10 = bf16[8,64,128]{2,1,0:T(8,128)(2,1)S(1)} async-done(((bf16[8,64,128]{2,1,0:T(8,128)(2,1)}), bf16[8,64,128]{2,1,0:T(8,128)(2,1)S(1)}, u32[]{:S(2)}, u32[]{:S(2)}) %all-to-all-start.10) | async-done | bytes 131104 | tf_op jit(solution)/shard_map/all_to_all | solution.py:14
  175.5 10.5 %all-to-all-start.9 = ((bf16[32,2,64,128]{3,2,1,0:T(8,128)(2,1)}), bf16[32,2,64,128]{3,2,1,0:T(8,128)(2,1)S(1)}, u32[]{:S(2)}, u32[]{:S(2)}) async-start(bf16[32,2,64,128]{3,2,1,0:T(8,128)(2,1)} %bitcast.47), calls=%async_computation.9 | async-start | bytes 2097152 | tf_op jit(solution)/shard_map/all_to_all | solution.py:14
  186.2 0.9 convolution_convert_fusion.2
  187.1 15.5 %all-to-all-done.9 = bf16[32,2,64,128]{3,2,1,0:T(8,128)(2,1)S(1)} async-done(((bf16[32,2,64,128]{3,2,1,0:T(8,128)(2,1)}), bf16[32,2,64,128]{3,2,1,0:T(8,128)(2,1)S(1)}, u32[]{:S(2)}, u32[]{:S(2)}) %all-to-all-start.9) | async-done | bytes 1048608 | tf_op jit(solution)/shard_map/all_to_all | solution.py:14
  202.6 7.4 %all-to-all-start.3 = ((bf16[4,128,128]{2,1,0:T(8,128)(2,1)}), bf16[4,128,128]{2,1,0:T(8,128)(2,1)S(1)}, u32[]{:S(2)}, u32[]{:S(2)}) async-start(bf16[4,128,128]{2,1,0:T(8,128)(2,1)} %bitcast.26), calls=%async_computation.3 | async-start | bytes 262144 | tf_op jit(solution)/shard_map/all_to_all | solution.py:14
  211.3 11.0 %all-to-all-done.3 = bf16[4,128,128]{2,1,0:T(8,128)(2,1)S(1)} async-done(((bf16[4,128,128]{2,1,0:T(8,128)(2,1)}), bf16[4,128,128]{2,1,0:T(8,128)(2,1)S(1)}, u32[]{:S(2)}, u32[]{:S(2)}) %all-to-all-start.3) | async-done | bytes 131104 | tf_op jit(solution)/shard_map/all_to_all | solution.py:14
  222.3 5.9 %all-to-all-start.11 = ((bf16[16,24,128]{2,1,0:T(8,128)(2,1)}), bf16[16,24,128]{2,1,0:T(8,128)(2,1)S(1)}, u32[]{:S(2)}, u32[]{:S(2)}) async-start(bf16[16,24,128]{2,1,0:T(8,128)(2,1)} %bitcast.53), calls=%async_computation.11 | async-start | bytes 196608 | tf_op jit(solution)/shard_map/all_to_all | solution.py:14
  228.6 0.7 copy.53
  229.3 11.6 %all-to-all-done.11 = bf16[16,24,128]{2,1,0:T(8,128)(2,1)S(1)} async-done(((bf16[16,24,128]{2,1,0:T(8,128)(2,1)}), bf16[16,24,128]{2,1,0:T(8,128)(2,1)S(1)}, u32[]{:S(2)}, u32[]{:S(2)}) %all-to-all-start.11) | async-done | bytes 98336 | tf_op jit(solution)/shard_map/all_to_all | solution.py:14
  240.9 3.7 %all-to-all-start.4 = ((bf16[16,64,128]{2,1,0:T(8,128)(2,1)}), bf16[16,64,128]{2,1,0:T(8,128)(2,1)S(1)}, u32[]{:S(2)}, u32[]{:S(2)}) async-start(bf16[16,64,128]{2,1,0:T(8,128)(2,1)} %bitcast.28), calls=%async_computation.4 | async-start | bytes 524288 | tf_op jit(solution)/shard_map/all_to_all | solution.py:14
  244.8 15.5 %all-to-all-done.4 = bf16[16,64,128]{2,1,0:T(8,128)(2,1)S(1)} async-done(((bf16[16,64,128]{2,1,0:T(8,128)(2,1)}), bf16[16,64,128]{2,1,0:T(8,128)(2,1)S(1)}, u32[]{:S(2)}, u32[]{:S(2)}) %all-to-all-start.4) | async-done | bytes 262176 | tf_op jit(solution)/shard_map/all_to_all | solution.py:14
  260.3 0.7 broadcast_in_dim.47
  261.0 9.4 %all-to-all-start.12 = ((f32[16,24,128]{2,1,0:T(8,128)}), f32[16,24,128]{2,1,0:T(8,128)S(1)}, u32[]{:S(2)}, u32[]{:S(2)}) async-start(f32[16,24,128]{2,1,0:T(8,128)} %broadcast_in_dim.47), calls=%async_computation.12 | async-start | bytes 393216 | tf_op jit(solution)/shard_map/all_to_all | solution.py:14
  270.4 3.5 %fusion.3 = bf16[4,4096]{1,0:T(4,128)(2,1)} fusion(f32[4,4096]{1,0:T(4,128)S(1)} %reshape.249, bf16[512,4096]{1,0:T(8,128)(2,1)} %param.11, f32[4]{0:T(128)S(1)} %convert_divide_fusion, s32[512]{0:T(512)S(1)} %get-tuple-element.28, s32[512]{0:T(512)S(1)} %get-tuple-element.29, s32[4]{0:T(128)S(1)} %copy-done.1), kind=kOutput, calls=%fused_computation.7 | convolution fusion | flops 16832512 | bytes 4296736 | tf_op jit(solution)/shard_map/dot_general | solution.py:106
  275.2 9.8 %all-to-all-done.12 = f32[16,24,128]{2,1,0:T(8,128)S(1)} async-done(((f32[16,24,128]{2,1,0:T(8,128)}), f32[16,24,128]{2,1,0:T(8,128)S(1)}, u32[]{:S(2)}, u32[]{:S(2)}) %all-to-all-start.12) | async-done | bytes 196640 | tf_op jit(solution)/shard_map/all_to_all | solution.py:14
  285.7 0.7 copy.67
  (65 shorter events, 7.1 us)
Async XLA Ops:
  0.6 89.8 %copy-start = (s32[2,512]{1,0:T(2,128)S(1)}, s32[2,512]{1,0:T(2,128)}, u32[]{:S(2)}) copy-start(s32[2,512]{1,0:T(2,128)} %constant.84) | copy-start | bytes 12292
  0.6 61.0 %copy-start.2 = (s32[128]{0:T(128)S(1)}, s32[128]{0:T(128)}, u32[]{:S(2)}) copy-start(s32[128]{0:T(128)} %param.10) | copy-start | bytes 1540
  2.2 50.5 %all-to-all-start = ((bf16[16,64,128]{2,1,0:T(8,128)(2,1)}), bf16[16,64,128]{2,1,0:T(8,128)(2,1)S(1)}, u32[]{:S(2)}, u32[]{:S(2)}) async-start(bf16[16,64,128]{2,1,0:T(8,128)(2,1)} %bitcast.8), calls=%async_computation | async-start | bytes 524288 | tf_op jit(solution)/shard_map/all_to_all | solution.py:14
  20.2 28.1 %collective-permute-start = (bf16[384,128]{1,0:T(8,128)(2,1)S(1)}, bf16[384,128]{1,0:T(8,128)(2,1)S(1)}, u32[]{:S(2)}, u32[]{:S(2)}) collective-permute-start(bf16[384,128]{1,0:T(8,128)(2,1)S(1)} %constant_dynamic-update-slice_fusion), channel_id=1, source_target_pairs={{0,4},{4,0},{1,5},{5,1},{2,6},{6,2},{3,7},{7,3},{8,12},{12,8},{9,1... | collective-permute-start | bytes 294920 | tf_op jit(solution)/shard_map/ppermute | solution.py:22
  48.4 4.0 %collective-permute-start.1 = (bf16[2,128,128]{2,1,0:T(8,128)(2,1)S(1)}, bf16[2,128,128]{2,1,0:T(8,128)(2,1)S(1)}, u32[]{:S(2)}, u32[]{:S(2)}) collective-permute-start(bf16[2,128,128]{2,1,0:T(8,128)(2,1)S(1)} %get-tuple-element.23), channel_id=1, source_target_pairs={{0,32},{32,0},{1,33},{33,1},{2,34},{34,2},{3,35},{35,3},{4,36},{36... | collective-permute-start | bytes 196616 | tf_op jit(solution)/shard_map/ppermute | solution.py:22
  53.0 55.2 %copy-start.1 = (s32[4]{0:T(128)S(1)}, s32[4]{0:T(128)}, u32[]{:S(2)}) copy-start(s32[4]{0:T(128)} %param.12) | copy-start | bytes 52
  54.2 19.7 %all-to-all-start.1 = ((f32[32,8,640]{2,1,0:T(8,128)}), f32[32,8,640]{2,1,0:T(8,128)S(1)}, u32[]{:S(2)}, u32[]{:S(2)}) async-start(f32[32,8,640]{2,1,0:T(8,128)} %maximum_bitcast_fusion), calls=%async_computation.1 | async-start | bytes 1310720 | tf_op jit(solution)/shard_map/all_to_all | solution.py:14
  74.4 16.0 %collective-permute-start.2 = (f32[8,128]{0,1:T(8,128)S(1)}, f32[8,128]{0,1:T(8,128)S(1)}, u32[]{:S(2)}, u32[]{:S(2)}) collective-permute-start(f32[8,128]{0,1:T(8,128)S(1)} %broadcast_select_fusion), channel_id=1, source_target_pairs={{0,4},{4,0},{1,5},{5,1},{2,6},{6,2},{3,7},{7,3},{8,12},{12,8},{9,1... | collective-permute-start | bytes 12296 | tf_op jit(solution)/shard_map/ppermute | solution.py:22
  104.5 19.6 %all-to-all-start.5 = ((bf16[16,2,128,128]{3,2,1,0:T(8,128)(2,1)}), bf16[16,2,128,128]{3,2,1,0:T(8,128)(2,1)S(1)}, u32[]{:S(2)}, u32[]{:S(2)}) async-start(bf16[16,2,128,128]{3,2,1,0:T(8,128)(2,1)} %broadcast_in_dim.43), calls=%async_computation.5 | async-start | bytes 2097152 | tf_op jit(solution)/shard_map/all_to_all | solution.py:14
  124.1 12.6 %all-to-all-start.8 = ((f32[8,4,128]{2,1,0:T(4,128)}), f32[8,4,128]{2,1,0:T(4,128)S(1)}, u32[]{:S(2)}, u32[]{:S(2)}) async-start(f32[8,4,128]{2,1,0:T(4,128)} %fusion.14), calls=%async_computation.8 | async-start | bytes 32768 | tf_op jit(solution)/shard_map/all_to_all | solution.py:14
  141.1 10.7 %all-to-all-start.6 = ((bf16[16,4,128]{2,1,0:T(4,128)(2,1)}), bf16[16,4,128]{2,1,0:T(4,128)(2,1)S(1)}, u32[]{:S(2)}, u32[]{:S(2)}) async-start(bf16[16,4,128]{2,1,0:T(4,128)(2,1)} %broadcast_in_dim.44), calls=%async_computation.6 | async-start | bytes 32768 | tf_op jit(solution)/shard_map/all_to_all | solution.py:14
  161.9 13.6 %all-to-all-start.10 = ((bf16[8,64,128]{2,1,0:T(8,128)(2,1)}), bf16[8,64,128]{2,1,0:T(8,128)(2,1)S(1)}, u32[]{:S(2)}, u32[]{:S(2)}) async-start(bf16[8,64,128]{2,1,0:T(8,128)(2,1)} %broadcast_in_dim.46), calls=%async_computation.10 | async-start | bytes 262144 | tf_op jit(solution)/shard_map/all_to_all | solution.py:14
  175.5 27.1 %all-to-all-start.9 = ((bf16[32,2,64,128]{3,2,1,0:T(8,128)(2,1)}), bf16[32,2,64,128]{3,2,1,0:T(8,128)(2,1)S(1)}, u32[]{:S(2)}, u32[]{:S(2)}) async-start(bf16[32,2,64,128]{3,2,1,0:T(8,128)(2,1)} %bitcast.47), calls=%async_computation.9 | async-start | bytes 2097152 | tf_op jit(solution)/shard_map/all_to_all | solution.py:14
  202.6 19.8 %all-to-all-start.3 = ((bf16[4,128,128]{2,1,0:T(8,128)(2,1)}), bf16[4,128,128]{2,1,0:T(8,128)(2,1)S(1)}, u32[]{:S(2)}, u32[]{:S(2)}) async-start(bf16[4,128,128]{2,1,0:T(8,128)(2,1)} %bitcast.26), calls=%async_computation.3 | async-start | bytes 262144 | tf_op jit(solution)/shard_map/all_to_all | solution.py:14
  222.3 18.6 %all-to-all-start.11 = ((bf16[16,24,128]{2,1,0:T(8,128)(2,1)}), bf16[16,24,128]{2,1,0:T(8,128)(2,1)S(1)}, u32[]{:S(2)}, u32[]{:S(2)}) async-start(bf16[16,24,128]{2,1,0:T(8,128)(2,1)} %bitcast.53), calls=%async_computation.11 | async-start | bytes 196608 | tf_op jit(solution)/shard_map/all_to_all | solution.py:14
  240.9 19.4 %all-to-all-start.4 = ((bf16[16,64,128]{2,1,0:T(8,128)(2,1)}), bf16[16,64,128]{2,1,0:T(8,128)(2,1)S(1)}, u32[]{:S(2)}, u32[]{:S(2)}) async-start(bf16[16,64,128]{2,1,0:T(8,128)(2,1)} %bitcast.28), calls=%async_computation.4 | async-start | bytes 524288 | tf_op jit(solution)/shard_map/all_to_all | solution.py:14
  261.0 24.0 %all-to-all-start.12 = ((f32[16,24,128]{2,1,0:T(8,128)}), f32[16,24,128]{2,1,0:T(8,128)S(1)}, u32[]{:S(2)}, u32[]{:S(2)}) async-start(f32[16,24,128]{2,1,0:T(8,128)} %broadcast_in_dim.47), calls=%async_computation.12 | async-start | bytes 393216 | tf_op jit(solution)/shard_map/all_to_all | solution.py:14

commit v2 on v1

v2 whole, which is shorter than its diff:
```python
import jax
import jax.numpy as jnp
import numpy as np
from jax import lax
from jax.sharding import Mesh, PartitionSpec as P

inv_temp = 20.0
eps = 1e-06
bf16 = jnp.bfloat16
f32 = jnp.float32


def exchange(x, axes):
    return lax.all_to_all(x, axes, split_axis=0, concat_axis=0, tiled=False)


def spread(x, count):
    return jnp.broadcast_to(x[None], (count,) + x.shape)


def swap(x, axis):
    return lax.ppermute(x, axis, [(0, 1), (1, 0)])


def in_order(first, mine, other):
    return jnp.where(first, jnp.stack([mine, other]), jnp.stack([other, mine]))


def split2(v):
    high = v.astype(bf16)
    return high, (v - high.astype(f32)).astype(bf16)


def local(queries, passages, positive, hidden, lengths, w_down, w_up):
    zl_n, y_n, x_n = lax.axis_size("zl"), lax.axis_size("y"), lax.axis_size("x")
    c, y, h, x = (lax.axis_index(a) for a in ("c", "y", "h", "x"))
    plane = y_n * x_n
    rows, width = queries.shape
    pages, rank = lengths.shape[0], w_down.shape[1]
    tokens = hidden.shape[0]
    half = plane * pages
    cols = zl_n * half
    own = rows // plane

    part = [lax.dynamic_slice_in_dim(w, c * (w.shape[0] // 2), w.shape[0] // 2) for w in (w_down, w_up)]
    pack = jnp.concatenate([queries] + part, axis=0)
    both = in_order(h == 0, pack, swap(pack, "h"))
    q_mine, w_both = both[:, :rows], both[:, rows:]
    q_both = in_order(c == 0, q_mine, swap(q_mine, "c"))
    q_all = q_both.transpose(0, 2, 1, 3).reshape(2 * rows, 2 * width)

    p_sub = passages.reshape(y_n, 2, x_n * pages, width).transpose(1, 0, 2, 3)
    p_sub = p_sub.reshape(2, half, width)
    p_got = exchange(spread(p_sub, zl_n).reshape(zl_n * 2, half, width), ("zl", "h"))
    p_all = p_got.reshape(zl_n, 2, half, width).transpose(0, 2, 1, 3)
    p_all = p_all.reshape(cols, 2 * width)

    part = lax.dot_general(q_all, p_all, (((1,), (1,)), ((), ())), preferred_element_type=f32)
    q_own = jnp.where(c == 0, jnp.stack([queries, q_both[1, h]]), jnp.stack([q_both[0, h], queries]))
    q_own = q_own.reshape(2 * rows, width)
    side = lax.broadcasted_iota(jnp.int32, (1, width), 1) // (width // 2) == c
    q_side = jnp.where(side, q_own, jnp.zeros_like(q_own))
    qw_part = lax.dot_general(q_side, w_up, (((1,), (1,)), ((), ())), preferred_element_type=f32)
    sent = jnp.concatenate([part, qw_part], axis=1).reshape(2 * plane, own, cols + rank)
    got = exchange(sent, ("c", "y", "x"))
    got, w_both = lax.optimization_barrier((got, w_both))
    got = jnp.sum(got.reshape(2, plane, own, cols + rank), axis=1)
    scores = inv_temp * got[:, :, :cols]
    qw = got[0, :, cols:] + got[1, :, cols:]
    top = jnp.max(scores, axis=(0, 2))
    e = jnp.exp(scores - top[None, :, None])
    total = jnp.sum(e, axis=(0, 2))
    lane = lax.broadcasted_iota(jnp.int32, (own, rank), 1)
    stats = jnp.where(lane < rank // 2, top[:, None], total[:, None])
    stats = swap(jnp.concatenate([stats, qw], axis=0), "h")
    w_half = exchange(spread(w_both, plane), ("y", "x"))
    top_o, total_o = stats[:own, 0], stats[:own, rank // 2]
    qw = qw + stats[own:]
    top_a = jnp.maximum(top, top_o)
    scale = jnp.exp(top - top_a)
    z = total * scale + total_o * jnp.exp(top_o - top_a)
    probs = e * (scale / z)[None, :, None]
    k = np.arange(cols)
    base = k // half * (4 * half) + k % half // (x_n * pages) * (2 * x_n * pages) + k % (x_n * pages)
    base = np.stack([base, base + 2 * half]).astype(np.int32)
    target = lax.dynamic_slice(positive, ((y * x_n + x) * own,), (own,)) - h * (x_n * pages)
    onehot = (target[None, :, None] == base[:, None, :]).astype(f32)
    coeff_own = (probs - onehot).astype(bf16)

    sent = jnp.broadcast_to(qw.astype(bf16)[None], (2, own, rank))
    sent = jnp.concatenate([coeff_own, sent], axis=2)
    step = cols + rank
    sent = jnp.broadcast_to(sent[:, None], (2, plane, own, step))
    sent, w_half = lax.optimization_barrier((sent, w_half))
    got = exchange(sent.reshape(2 * plane, own, step), ("c", "y", "x"))

    w_all = in_order(c == 0, w_half, swap(w_half, "c")).reshape(2, y_n, x_n, 2, -1, rank)
    wd = w_all[:, :, :, :, : width // 2].transpose(1, 3, 2, 0, 4, 5).reshape(-1, rank)
    wu = w_all[:, :, :, :, width // 2 :].transpose(0, 4, 1, 3, 2, 5).reshape(rank, -1)
    xf = hidden.astype(f32)
    rs = lax.rsqrt(jnp.mean(xf * xf, axis=-1, keepdims=True) + eps)
    normed = (xf * rs).astype(bf16)
    pre = jnp.dot(normed, wd, preferred_element_type=f32)
    sig = jax.nn.sigmoid(pre)
    act = (pre * sig).astype(bf16)
    span = tokens // pages
    place = jnp.arange(tokens, dtype=jnp.int32)
    page_of, at = place // span, place % span
    mask = (page_of[None, :] == jnp.arange(pages)[:, None]) & (at[None, :] < lengths[:, None])
    mask = mask.astype(bf16)
    inv_len = 1.0 / lengths.astype(f32)
    x_mean = jnp.dot(mask, hidden, preferred_element_type=f32) * inv_len[:, None]
    pooled = (jnp.dot(mask, act, preferred_element_type=f32) * inv_len[:, None]).astype(bf16)
    weight = (at.reshape(pages, span) < lengths[:, None]).astype(f32) * inv_len[:, None]
    g = (sig * (1.0 + pre * (1.0 - sig)) * rs).reshape(pages, span, rank) * weight[:, :, None]

    got, pooled, g = lax.optimization_barrier((got, pooled, g))
    got = got.reshape(2 * rows, step)
    coeff, qw_all = got[:, :cols], got[:, cols:]

    c_mine = coeff.reshape(2 * rows, zl_n, plane, pages)
    c_mine = lax.dynamic_slice_in_dim(c_mine, y * x_n + x, 1, axis=2)[:, :, 0]
    dact_part = lax.dot_general(
        c_mine.reshape(2 * rows, zl_n * pages), qw_all, (((0,), (0,)), ((), ())), preferred_element_type=f32
    )
    high, low = split2(dact_part.reshape(zl_n, pages, rank))
    gq = jnp.dot(coeff, p_all, preferred_element_type=f32).reshape(2, rows, 2 * width)
    got = exchange(jnp.concatenate([high, low, spread(pooled, zl_n)], axis=1), ("zl",))
    got, x_mean = lax.optimization_barrier((got, x_mean))
    dact = inv_temp * jnp.sum(got[:, : 2 * pages].astype(f32).reshape(zl_n, 2, pages, rank), axis=(0, 1))
    pooled_zl = got[:, 2 * pages :].reshape(zl_n * pages, rank)

    dpre = (g * dact[:, None, :]).astype(bf16).reshape(tokens, rank)
    first, second = dpre[:, : rank // 2], dpre[:, rank // 2 :]
    turn = (((0,), (0,)), ((), ()))
    theirs = lax.dot_general(jnp.where(c == 0, second, first), hidden, turn, preferred_element_type=f32)
    theirs = swap(theirs.astype(bf16), "c")
    mine = lax.dot_general(jnp.where(c == 0, first, second), hidden, turn, preferred_element_type=f32)
    down = (mine + theirs.astype(f32)).astype(bf16)
    down = down.reshape(rank // 2, y_n, 2, x_n, width).transpose(1, 3, 2, 0, 4).reshape(plane, rank, width)
    sent = jnp.concatenate([down, spread(pooled_zl, plane)], axis=1)
    sent, gq = lax.optimization_barrier((sent, gq))
    got = exchange(sent, ("y", "x"))
    gq = jnp.where(c == 0, gq[0], gq[1]) + swap(jnp.where(c == 0, gq[1], gq[0]), "c")
    pooled_all = got[:, rank:].reshape(plane, zl_n, pages, rank).transpose(1, 0, 2, 3).reshape(cols, rank)
    down = jnp.sum(got[:, :rank].astype(f32), axis=0).astype(bf16)
    down = down.reshape(2, zl_n, rank // 2 // zl_n, width).transpose(1, 0, 2, 3)

    sub_embed = (x_mean + jnp.dot(pooled, wu, preferred_element_type=f32)).astype(bf16)

    gp = lax.dot_general(coeff, q_all, (((0,), (0,)), ((), ())), preferred_element_type=f32)
    gp = gp.astype(bf16).reshape(zl_n, half, 2, width).transpose(0, 2, 1, 3)
    u = (inv_temp * jnp.dot(coeff, pooled_all, preferred_element_type=f32)).astype(bf16)
    up_part = lax.dot_general(u, q_all, (((0,), (0,)), ((), ())), preferred_element_type=f32)
    up_part = up_part.astype(bf16).reshape(zl_n, rank // zl_n, 2, width).transpose(0, 2, 1, 3)
    sent = jnp.concatenate([down, up_part, gp], axis=2)
    sent, gq = lax.optimization_barrier((sent, gq))
    got = exchange(sent.reshape(zl_n * 2, -1, width), ("zl", "h"))
    gq_0, gq_1 = gq[:, :width], gq[:, width:]
    gq = jnp.where(h == 0, gq_0, gq_1) + swap(jnp.where(h == 0, gq_1, gq_0), "h")
    grad_queries = (inv_temp * gq).astype(bf16)
    got, grad_queries = lax.optimization_barrier((got, grad_queries))
    got = got.astype(f32)
    n = rank // 2 // zl_n
    step = n + rank // zl_n
    weights = jnp.sum(got[:, :step], axis=0)
    gp = jnp.sum(got[:, step:].reshape(zl_n, 2, half, width), axis=0) * inv_temp
    grad_passages = gp.reshape(2, y_n, x_n * pages, width).transpose(1, 0, 2, 3)
    grad_passages = grad_passages.reshape(-1, width).astype(bf16)
    got = exchange(spread(weights, zl_n * 2), ("zl", "c")).reshape(zl_n, 2, step, width)
    grad_down = got[:, :, :n].transpose(1, 0, 2, 3).reshape(rank, width).T
    grad_up = jnp.sum(got[:, :, n:], axis=1).reshape(rank, width)
    return (grad_queries, grad_passages, sub_embed, grad_down, grad_up)


def solution(mesh):
    dp, fsdp = ("zl", "c"), ("y", "h", "x")
    shape = (mesh.shape["dp"] // 2, 2, 4, 2, mesh.shape["fsdp"] // 8)
    inner = Mesh(mesh.devices.reshape(shape), dp + fsdp)
    both = dp + fsdp
    return jax.shard_map(
        local,
        mesh=inner,
        in_specs=(P(dp, fsdp), P(dp, fsdp), P(dp), P(both, None), P(both), P(fsdp, None), P(None, fsdp)),
        out_specs=(P(dp, fsdp), P(dp, fsdp), P(both, None), P(fsdp, None), P(None, fsdp)),
        check_vma=False,
    )
```

time: 288 us -> 218 us (0.76)
  waiting for transfers between devices: 136 us -> 81.7 us
  blocking collectives: 21.9 us -> 0 us
  other arithmetic: 6.92 us -> 11.6 us
    all_to_all x11 -> x8, waiting for transfers between devices: 108 us -> 54.3 us  [exchange(): return lax.all_to_all(x, axes, split_axis=0, concat_axis=0, tiled=False)]
    all_to_all x11 -> x8, starting transfers between devices: 74.8 us -> 48.9 us  [exchange(): return lax.all_to_all(x, axes, split_axis=0, concat_axis=0, tiled=False)]
    ppermute x3 -> x7, starting transfers between devices: 20.3 us -> 46.3 us  [swap(): return lax.ppermute(x, axis, [(0, 1), (1, 0)])]
    all_to_all x2 -> x0, blocking collectives: 21.9 us -> none  [exchange(): return lax.all_to_all(x, axes, split_axis=0, concat_axis=0, tiled=False)]
    dot_general x4 -> x5, matrix products: 4.13 us -> 8.44 us  [the longest x1 3.28 us: local(): lax.dot_general(jnp.where(c == 0, first, second), hidden, turn, preferred...]
    ppermute x3 -> x7, waiting for transfers between devices: 27.7 us -> 27.5 us  [swap(): return lax.ppermute(x, axis, [(0, 1), (1, 0)])]
  transfers between devices with their start and end apart: 14 -> 15, of which waited for: 13 -> 12; matrix products, arithmetic and copies ran while one was open for 7% -> 9% of each run, Pallas kernels for 0% -> 0%
where the time goes in v2:
time: 218 us; the launch traced here: 216 us
  starting transfers between devices  95.1 us (44%)
  waiting for transfers between devices  81.7 us (37%)
  matrix products  13.9 us (6%)
  local copies, waits for them, and re-layouts  12.6 us (6%)
  other arithmetic  11.6 us (5%)
    all_to_all x8, waiting for transfers between devices, exchange(): return lax.all_to_all(x, axes, split_axis=0, concat_axis=0, tiled=False)  54.3 us
    all_to_all x8, starting transfers between devices, exchange(): return lax.all_to_all(x, axes, split_axis=0, concat_axis=0, tiled=False)  48.9 us
    ppermute x7, starting transfers between devices, swap(): return lax.ppermute(x, axis, [(0, 1), (1, 0)])  46.3 us
    ppermute x7, waiting for transfers between devices, swap(): return lax.ppermute(x, axis, [(0, 1), (1, 0)])  27.5 us
  transfers between devices with their start and end apart: 15, of which 12 were waited for; matrix products, arithmetic and copies ran while one was open for 9% of the time, Pallas kernels for 0%

profile of v2, /device:TPU:1, one launch (start us, length us, event | category | flops | bytes accessed | tf_op | source)
XLA Modules:
  0.0 216.2 jit_solution(11833311083139179388)
XLA Ops:
  0.6 0.7 constant_dynamic-slice_fusion.1
  1.4 0.8 fusion.54
  2.2 16.3 %collective-permute-start = (bf16[256,128]{1,0:T(8,128)(2,1)S(1)}, bf16[256,128]{1,0:T(8,128)(2,1)S(1)}, u32[]{:S(2)}, u32[]{:S(2)}) collective-permute-start(bf16[256,128]{1,0:T(8,128)(2,1)S(1)} %get-tuple-element.72), channel_id=1, source_target_pairs={{0,4},{4,0},{1,5},{5,1},{2,6},{6,2},{3,7},{7,3},{8,12},{12,8},{9,1... | collective-permute-start | bytes 196616 | tf_op jit(solution)/shard_map/ppermute | solution.py:22
  18.4 0.8 copy.83
  19.2 0.7 broadcast_in_dim.45
  19.9 4.8 %all-to-all-start = ((bf16[16,64,128]{2,1,0:T(8,128)(2,1)}), bf16[16,64,128]{2,1,0:T(8,128)(2,1)S(1)}, u32[]{:S(2)}, u32[]{:S(2)}) async-start(bf16[16,64,128]{2,1,0:T(8,128)(2,1)} %bitcast.8), calls=%async_computation | async-start | bytes 524288 | tf_op jit(solution)/shard_map/all_to_all | solution.py:14
  24.9 3.1 %collective-permute-start.1 = (bf16[2,128,128]{2,1,0:T(8,128)(2,1)S(1)}, bf16[2,128,128]{2,1,0:T(8,128)(2,1)S(1)}, u32[]{:S(2)}, u32[]{:S(2)}) collective-permute-start(bf16[2,128,128]{2,1,0:T(8,128)(2,1)S(1)} %get-tuple-element.68), channel_id=1, source_target_pairs={{0,32},{32,0},{1,33},{33,1},{2,34},{34,2},{3,35},{35,3},{4,36},{36... | collective-permute-start | bytes 196616 | tf_op jit(solution)/shard_map/ppermute | solution.py:22
  28.0 0.9 collective-permute-done.1
  29.1 0.8 maximum_select_fusion.3
  30.0 0.9 fusion.59
  30.9 9.8 %all-to-all-done = bf16[16,64,128]{2,1,0:T(8,128)(2,1)S(1)} async-done(((bf16[16,64,128]{2,1,0:T(8,128)(2,1)}), bf16[16,64,128]{2,1,0:T(8,128)(2,1)S(1)}, u32[]{:S(2)}, u32[]{:S(2)}) %all-to-all-start) | async-done | bytes 262176 | tf_op jit(solution)/shard_map/all_to_all | solution.py:14
  41.3 0.9 maximum_bitcast_fusion
  42.2 12.2 %all-to-all-start.1 = ((f32[32,8,640]{2,1,0:T(8,128)}), f32[32,8,640]{2,1,0:T(8,128)S(1)}, u32[]{:S(2)}, u32[]{:S(2)}) async-start(f32[32,8,640]{2,1,0:T(8,128)} %maximum_bitcast_fusion), calls=%async_computation.1 | async-start | bytes 1310720 | tf_op jit(solution)/shard_map/all_to_all | solution.py:14
  54.4 12.3 %all-to-all-done.1 = f32[32,8,640]{2,1,0:T(8,128)S(1)} async-done(((f32[32,8,640]{2,1,0:T(8,128)}), f32[32,8,640]{2,1,0:T(8,128)S(1)}, u32[]{:S(2)}, u32[]{:S(2)}) %all-to-all-start.1) | async-done | bytes 655392 | tf_op jit(solution)/shard_map/all_to_all | solution.py:14
  66.8 1.2 broadcast_in_dim.52
  68.0 3.7 %all-to-all-start.2 = ((bf16[16,2,128,128]{3,2,1,0:T(8,128)(2,1)}), bf16[16,2,128,128]{3,2,1,0:T(8,128)(2,1)S(1)}, u32[]{:S(2)}, u32[]{:S(2)}) async-start(bf16[16,2,128,128]{3,2,1,0:T(8,128)(2,1)} %broadcast_in_dim.52), calls=%async_computation.2 | async-start | bytes 2097152 | tf_op jit(solution)/shard_map/all_to_all | solution.py:14
  72.0 3.3 %collective-permute-start.2 = (f32[16,128]{1,0:T(8,128)S(1)}, f32[16,128]{1,0:T(8,128)S(1)}, u32[]{:S(2)}, u32[]{:S(2)}) collective-permute-start(f32[16,128]{1,0:T(8,128)S(1)} %pad_maximum_fusion.5), channel_id=1, source_target_pairs={{0,4},{4,0},{1,5},{5,1},{2,6},{6,2},{3,7},{7,3},{8,12},{12,8},{9,1... | collective-permute-start | bytes 24584 | tf_op jit(solution)/shard_map/ppermute | solution.py:22
  75.4 9.7 %collective-permute-done.2 = f32[16,128]{1,0:T(8,128)S(1)} collective-permute-done((f32[16,128]{1,0:T(8,128)S(1)}, f32[16,128]{1,0:T(8,128)S(1)}, u32[]{:S(2)}, u32[]{:S(2)}) %collective-permute-start.2) | collective-permute-done | bytes 8224 | tf_op jit(solution)/shard_map/ppermute | solution.py:22
  85.5 2.1 all-to-all-done.2
  87.5 0.8 broadcast_in_dim.51
  88.3 4.7 %collective-permute-start.3 = (bf16[16,2,128,128]{3,2,1,0:T(8,128)(2,1)S(1)}, bf16[16,2,128,128]{3,2,1,0:T(8,128)(2,1)}, u32[]{:S(2)}, u32[]{:S(2)}) collective-permute-start(bf16[16,2,128,128]{3,2,1,0:T(8,128)(2,1)S(1)} %all-to-all-done.2), channel_id=1, source_target_pairs={{0,32},{32,0},{1,33},{33,1},{2,34},{34,2},{3,35},{35,3},{4,36},{36... | collective-permute-start | bytes 3145736 | tf_op jit(solution)/shard_map/ppermute | solution.py:22
  93.1 3.1 %fusion = f32[512]{0:T(512)S(1)} fusion(bf16[512,4096]{1,0:T(8,128)(2,1)} %param.11), kind=kLoop, calls=%fused_computation.2 | loop fusion | flops 6290944 | bytes 4196352 | tf_op jit(solution)/shard_map/reduce_sum | solution.py:101
  96.2 4.8 %all-to-all-start.3 = ((bf16[32,8,640]{2,1,0:T(8,128)(2,1)}), bf16[32,8,640]{2,1,0:T(8,128)(2,1)S(1)}, u32[]{:S(2)}, u32[]{:S(2)}) async-start(bf16[32,8,640]{2,1,0:T(8,128)(2,1)} %bitcast.18), calls=%async_computation.3 | async-start | bytes 655360 | tf_op jit(solution)/shard_map/all_to_all | solution.py:14
  101.0 1.9 maximum_select_fusion
  103.2 1.9 copy-done
  105.1 1.3 multiply_multiply_fusion
  106.8 3.1 %all-to-all-done.3 = bf16[32,8,640]{2,1,0:T(8,128)(2,1)S(1)} async-done(((bf16[32,8,640]{2,1,0:T(8,128)(2,1)}), bf16[32,8,640]{2,1,0:T(8,128)(2,1)S(1)}, u32[]{:S(2)}, u32[]{:S(2)}) %all-to-all-start.3) | async-done | bytes 327712 | tf_op jit(solution)/shard_map/all_to_all | solution.py:14
  110.9 3.7 %all-to-all-start.4 = ((bf16[8,12,128]{2,1,0:T(8,128)(2,1)}), bf16[8,12,128]{2,1,0:T(8,128)(2,1)S(1)}, u32[]{:S(2)}, u32[]{:S(2)}) async-start(bf16[8,12,128]{2,1,0:T(8,128)(2,1)} %copy.89), calls=%async_computation.4 | async-start | bytes 65536 | tf_op jit(solution)/shard_map/all_to_all | solution.py:14
  114.6 2.9 %convolution_multiply_fusion = f32[4,4096]{1,0:T(4,128)S(1)} fusion(bf16[512,4096]{1,0:T(8,128)(2,1)} %param.11, f32[4]{0:T(128)S(1)} %convert_divide_fusion, s32[512]{0:T(512)S(1)} %get-tuple-element.75, s32[512]{0:T(512)S(1)} %get-tuple-element.76, s32[4]{0:T(128)S(1)} %copy-done.4), kind=kOutput, calls=%fused_computation.6 | convolution fusion | flops 16799744 | bytes 4263968 | tf_op jit(solution)/shard_map/dot_general | solution.py:112
  117.5 6.6 %all-to-all-done.4 = bf16[8,12,128]{2,1,0:T(8,128)(2,1)S(1)} async-done(((bf16[8,12,128]{2,1,0:T(8,128)(2,1)}), bf16[8,12,128]{2,1,0:T(8,128)(2,1)S(1)}, u32[]{:S(2)}, u32[]{:S(2)}) %all-to-all-start.4) | async-done | bytes 24608 | tf_op jit(solution)/shard_map/all_to_all | solution.py:14
  124.2 3.1 %convolution_convert_fusion = bf16[64,4096]{1,0:T(8,128)(2,1)S(1)} fusion(bf16[512,4096]{1,0:T(8,128)(2,1)} %param.11, pred[]{:T(512)S(6)} %eq.55, bf16[512,128]{1,0:T(8,128)(2,1)S(1)} %bitcast.122), kind=kOutput, calls=%fused_computation.4 | convolution fusion | flops 268730368 | bytes 4980737 | tf_op jit(solution)/shard_map/dot_general | solution.py:136
  127.3 4.6 %collective-permute-start.4 = (bf16[64,4096]{1,0:T(8,128)(2,1)S(1)}, bf16[64,4096]{1,0:T(8,128)(2,1)}, u32[]{:S(2)}, u32[]{:S(2)}) collective-permute-start(bf16[64,4096]{1,0:T(8,128)(2,1)S(1)} %convolution_convert_fusion), channel_id=1, source_target_pairs={{0,32},{32,0},{1,33},{33,1},{2,34},{34,2},{3,35},{35,3},{4,36},{36... | collective-permute-start | bytes 1572872 | tf_op jit(solution)/shard_map/ppermute | solution.py:22
  132.3 1.2 collective-permute-done.4
  133.6 3.3 %add_convert_fusion = bf16[64,4096]{1,0:T(8,128)(2,1)S(1)} fusion(bf16[64,4096]{1,0:T(8,128)(2,1)} %collective-permute-done.4, bf16[512,4096]{1,0:T(8,128)(2,1)} %param.11, pred[]{:T(512)S(6)} %eq.55, bf16[512,128]{1,0:T(8,128)(2,1)S(1)} %bitcast.123), kind=kOutput, calls=%fused_computation.19 | convolution fusion | flops 269254656 | bytes 5505025 | tf_op jit(solution)/shard_map/dot_general | solution.py:138
  137.5 0.9 pad_maximum_fusion
  138.3 3.6 %all-to-all-start.5 = ((bf16[16,160,128]{2,1,0:T(8,128)(2,1)}), bf16[16,160,128]{2,1,0:T(8,128)(2,1)S(1)}, u32[]{:S(2)}, u32[]{:S(2)}) async-start(bf16[16,160,128]{2,1,0:T(8,128)(2,1)} %pad_maximum_fusion), calls=%async_computation.5 | async-start | bytes 1310720 | tf_op jit(solution)/shard_map/all_to_all | solution.py:14
  142.0 2.3 %collective-permute-start.5 = (f32[128,256]{1,0:T(8,128)S(1)}, f32[128,256]{1,0:T(8,128)S(1)}, u32[]{:S(2)}, u32[]{:S(2)}) collective-permute-start(f32[128,256]{1,0:T(8,128)S(1)} %select_bitcast_fusion), channel_id=1, source_target_pairs={{0,32},{32,0},{1,33},{33,1},{2,34},{34,2},{3,35},{35,3},{4,36},{36... | collective-permute-start | bytes 393224 | tf_op jit(solution)/shard_map/ppermute | solution.py:22
  145.3 9.0 %all-to-all-done.5 = bf16[16,160,128]{2,1,0:T(8,128)(2,1)S(1)} async-done(((bf16[16,160,128]{2,1,0:T(8,128)(2,1)}), bf16[16,160,128]{2,1,0:T(8,128)(2,1)S(1)}, u32[]{:S(2)}, u32[]{:S(2)}) %all-to-all-start.5) | async-done | bytes 655392 | tf_op jit(solution)/shard_map/all_to_all | solution.py:14
  154.9 0.8 pad_maximum_fusion.1
  155.7 8.3 %all-to-all-start.6 = ((bf16[16,88,128]{2,1,0:T(8,128)(2,1)}), bf16[16,88,128]{2,1,0:T(8,128)(2,1)S(1)}, u32[]{:S(2)}, u32[]{:S(2)}) async-start(bf16[16,88,128]{2,1,0:T(8,128)(2,1)} %bitcast.42), calls=%async_computation.6 | async-start | bytes 720896 | tf_op jit(solution)/shard_map/all_to_all | solution.py:14
  164.0 12.0 %collective-permute-start.6 = (f32[128,128]{1,0:T(8,128)S(1)}, f32[128,128]{1,0:T(8,128)S(1)}, u32[]{:S(2)}, u32[]{:S(2)}) collective-permute-start(f32[128,128]{1,0:T(8,128)S(1)} %slice_select_fusion), channel_id=1, source_target_pairs={{0,4},{4,0},{1,5},{5,1},{2,6},{6,2},{3,7},{7,3},{8,12},{12,8},{9,1... | collective-permute-start | bytes 196616 | tf_op jit(solution)/shard_map/ppermute | solution.py:22
  176.0 15.1 %collective-permute-done.6 = f32[128,128]{1,0:T(8,128)S(1)} collective-permute-done((f32[128,128]{1,0:T(8,128)S(1)}, f32[128,128]{1,0:T(8,128)S(1)}, u32[]{:S(2)}, u32[]{:S(2)}) %collective-permute-start.6) | collective-permute-done | bytes 65568 | tf_op jit(solution)/shard_map/ppermute | solution.py:22
  192.5 7.7 %all-to-all-start.7 = ((f32[16,24,128]{2,1,0:T(8,128)}), f32[16,24,128]{2,1,0:T(8,128)S(1)}, u32[]{:S(2)}, u32[]{:S(2)}) async-start(f32[16,24,128]{2,1,0:T(8,128)} %broadcast_in_dim.56), calls=%async_computation.7 | async-start | bytes 393216 | tf_op jit(solution)/shard_map/all_to_all | solution.py:14
  200.2 0.8 copy.96
  201.0 0.8 reshape.299
  201.8 0.9 fusion.2
  203.4 11.4 %all-to-all-done.7 = f32[16,24,128]{2,1,0:T(8,128)S(1)} async-done(((f32[16,24,128]{2,1,0:T(8,128)}), f32[16,24,128]{2,1,0:T(8,128)S(1)}, u32[]{:S(2)}, u32[]{:S(2)}) %all-to-all-start.7) | async-done | bytes 196640 | tf_op jit(solution)/shard_map/all_to_all | solution.py:14
  215.5 0.7 copy.98
  (90 shorter events, 8.7 us)
Async XLA Ops:
  2.2 22.7 %collective-permute-start = (bf16[256,128]{1,0:T(8,128)(2,1)S(1)}, bf16[256,128]{1,0:T(8,128)(2,1)S(1)}, u32[]{:S(2)}, u32[]{:S(2)}) collective-permute-start(bf16[256,128]{1,0:T(8,128)(2,1)S(1)} %get-tuple-element.72), channel_id=1, source_target_pairs={{0,4},{4,0},{1,5},{5,1},{2,6},{6,2},{3,7},{7,3},{8,12},{12,8},{9,1... | collective-permute-start | bytes 196616 | tf_op jit(solution)/shard_map/ppermute | solution.py:22
  19.9 20.8 %all-to-all-start = ((bf16[16,64,128]{2,1,0:T(8,128)(2,1)}), bf16[16,64,128]{2,1,0:T(8,128)(2,1)S(1)}, u32[]{:S(2)}, u32[]{:S(2)}) async-start(bf16[16,64,128]{2,1,0:T(8,128)(2,1)} %bitcast.8), calls=%async_computation | async-start | bytes 524288 | tf_op jit(solution)/shard_map/all_to_all | solution.py:14
  24.9 4.0 %collective-permute-start.1 = (bf16[2,128,128]{2,1,0:T(8,128)(2,1)S(1)}, bf16[2,128,128]{2,1,0:T(8,128)(2,1)S(1)}, u32[]{:S(2)}, u32[]{:S(2)}) collective-permute-start(bf16[2,128,128]{2,1,0:T(8,128)(2,1)S(1)} %get-tuple-element.68), channel_id=1, source_target_pairs={{0,32},{32,0},{1,33},{33,1},{2,34},{34,2},{3,35},{35,3},{4,36},{36... | collective-permute-start | bytes 196616 | tf_op jit(solution)/shard_map/ppermute | solution.py:22
  29.1 13.1 %copy-start.1 = (bf16[2,128,2,128]{3,2,1,0:T(2,128)(2,1)}, bf16[2,128,2,128]{3,2,1,0:T(2,128)(2,1)S(1)}, u32[]{:S(2)}) copy-start(bf16[2,128,2,128]{3,2,1,0:T(2,128)(2,1)S(1)} %copy.82) | copy-start | bytes 393220
  30.0 45.4 %copy-start.5 = (s32[128]{0:T(128)S(1)}, s32[128]{0:T(128)}, u32[]{:S(2)}) copy-start(s32[128]{0:T(128)} %param.10) | copy-start | bytes 1540
  30.0 55.3 %copy-start.3 = (s32[2,512]{1,0:T(2,128)S(1)}, s32[2,512]{1,0:T(2,128)}, u32[]{:S(2)}) copy-start(s32[2,512]{1,0:T(2,128)} %constant.103) | copy-start | bytes 12292
  40.7 52.3 %copy-start.4 = (s32[4]{0:T(128)S(1)}, s32[4]{0:T(128)}, u32[]{:S(2)}) copy-start(s32[4]{0:T(128)} %param.12) | copy-start | bytes 52
  42.2 24.5 %all-to-all-start.1 = ((f32[32,8,640]{2,1,0:T(8,128)}), f32[32,8,640]{2,1,0:T(8,128)S(1)}, u32[]{:S(2)}, u32[]{:S(2)}) async-start(f32[32,8,640]{2,1,0:T(8,128)} %maximum_bitcast_fusion), calls=%async_computation.1 | async-start | bytes 1310720 | tf_op jit(solution)/shard_map/all_to_all | solution.py:14
  68.0 19.5 %all-to-all-start.2 = ((bf16[16,2,128,128]{3,2,1,0:T(8,128)(2,1)}), bf16[16,2,128,128]{3,2,1,0:T(8,128)(2,1)S(1)}, u32[]{:S(2)}, u32[]{:S(2)}) async-start(bf16[16,2,128,128]{3,2,1,0:T(8,128)(2,1)} %broadcast_in_dim.52), calls=%async_computation.2 | async-start | bytes 2097152 | tf_op jit(solution)/shard_map/all_to_all | solution.py:14
  72.0 13.1 %collective-permute-start.2 = (f32[16,128]{1,0:T(8,128)S(1)}, f32[16,128]{1,0:T(8,128)S(1)}, u32[]{:S(2)}, u32[]{:S(2)}) collective-permute-start(f32[16,128]{1,0:T(8,128)S(1)} %pad_maximum_fusion.5), channel_id=1, source_target_pairs={{0,4},{4,0},{1,5},{5,1},{2,6},{6,2},{3,7},{7,3},{8,12},{12,8},{9,1... | collective-permute-start | bytes 24584 | tf_op jit(solution)/shard_map/ppermute | solution.py:22
  88.3 12.7 %collective-permute-start.3 = (bf16[16,2,128,128]{3,2,1,0:T(8,128)(2,1)S(1)}, bf16[16,2,128,128]{3,2,1,0:T(8,128)(2,1)}, u32[]{:S(2)}, u32[]{:S(2)}) collective-permute-start(bf16[16,2,128,128]{3,2,1,0:T(8,128)(2,1)S(1)} %all-to-all-done.2), channel_id=1, source_target_pairs={{0,32},{32,0},{1,33},{33,1},{2,34},{34,2},{3,35},{35,3},{4,36},{36... | collective-permute-start | bytes 3145736 | tf_op jit(solution)/shard_map/ppermute | solution.py:22
  96.2 13.7 %all-to-all-start.3 = ((bf16[32,8,640]{2,1,0:T(8,128)(2,1)}), bf16[32,8,640]{2,1,0:T(8,128)(2,1)S(1)}, u32[]{:S(2)}, u32[]{:S(2)}) async-start(bf16[32,8,640]{2,1,0:T(8,128)(2,1)} %bitcast.18), calls=%async_computation.3 | async-start | bytes 655360 | tf_op jit(solution)/shard_map/all_to_all | solution.py:14
  102.9 2.2 %copy-start = (bf16[512,4096]{1,0:T(8,128)(2,1)S(1)}, bf16[512,4096]{1,0:T(8,128)(2,1)}, u32[]{:S(2)}) copy-start(bf16[512,4096]{1,0:T(8,128)(2,1)} %param.11) | copy-start | bytes 12582916
  110.9 13.2 %all-to-all-start.4 = ((bf16[8,12,128]{2,1,0:T(8,128)(2,1)}), bf16[8,12,128]{2,1,0:T(8,128)(2,1)S(1)}, u32[]{:S(2)}, u32[]{:S(2)}) async-start(bf16[8,12,128]{2,1,0:T(8,128)(2,1)} %copy.89), calls=%async_computation.4 | async-start | bytes 65536 | tf_op jit(solution)/shard_map/all_to_all | solution.py:14
  127.3 6.2 %collective-permute-start.4 = (bf16[64,4096]{1,0:T(8,128)(2,1)S(1)}, bf16[64,4096]{1,0:T(8,128)(2,1)}, u32[]{:S(2)}, u32[]{:S(2)}) collective-permute-start(bf16[64,4096]{1,0:T(8,128)(2,1)S(1)} %convolution_convert_fusion), channel_id=1, source_target_pairs={{0,32},{32,0},{1,33},{33,1},{2,34},{34,2},{3,35},{35,3},{4,36},{36... | collective-permute-start | bytes 1572872 | tf_op jit(solution)/shard_map/ppermute | solution.py:22
  133.6 10.7 %copy-start.2 = (bf16[2,128,2,128]{3,2,1,0:T(2,128)(2,1)S(1)}, bf16[2,128,2,128]{3,2,1,0:T(2,128)(2,1)}, u32[]{:S(2)}) copy-start(bf16[2,128,2,128]{3,2,1,0:T(2,128)(2,1)} %copy-done.1) | copy-start | bytes 393220
  138.3 16.0 %all-to-all-start.5 = ((bf16[16,160,128]{2,1,0:T(8,128)(2,1)}), bf16[16,160,128]{2,1,0:T(8,128)(2,1)S(1)}, u32[]{:S(2)}, u32[]{:S(2)}) async-start(bf16[16,160,128]{2,1,0:T(8,128)(2,1)} %pad_maximum_fusion), calls=%async_computation.5 | async-start | bytes 1310720 | tf_op jit(solution)/shard_map/all_to_all | solution.py:14
  142.0 3.3 %collective-permute-start.5 = (f32[128,256]{1,0:T(8,128)S(1)}, f32[128,256]{1,0:T(8,128)S(1)}, u32[]{:S(2)}, u32[]{:S(2)}) collective-permute-start(f32[128,256]{1,0:T(8,128)S(1)} %select_bitcast_fusion), channel_id=1, source_target_pairs={{0,32},{32,0},{1,33},{33,1},{2,34},{34,2},{3,35},{35,3},{4,36},{36... | collective-permute-start | bytes 393224 | tf_op jit(solution)/shard_map/ppermute | solution.py:22
  155.7 36.0 %all-to-all-start.6 = ((bf16[16,88,128]{2,1,0:T(8,128)(2,1)}), bf16[16,88,128]{2,1,0:T(8,128)(2,1)S(1)}, u32[]{:S(2)}, u32[]{:S(2)}) async-start(bf16[16,88,128]{2,1,0:T(8,128)(2,1)} %bitcast.42), calls=%async_computation.6 | async-start | bytes 720896 | tf_op jit(solution)/shard_map/all_to_all | solution.py:14
  164.0 27.1 %collective-permute-start.6 = (f32[128,128]{1,0:T(8,128)S(1)}, f32[128,128]{1,0:T(8,128)S(1)}, u32[]{:S(2)}, u32[]{:S(2)}) collective-permute-start(f32[128,128]{1,0:T(8,128)S(1)} %slice_select_fusion), channel_id=1, source_target_pairs={{0,4},{4,0},{1,5},{5,1},{2,6},{6,2},{3,7},{7,3},{8,12},{12,8},{9,1... | collective-permute-start | bytes 196616 | tf_op jit(solution)/shard_map/ppermute | solution.py:22
  192.5 22.4 %all-to-all-start.7 = ((f32[16,24,128]{2,1,0:T(8,128)}), f32[16,24,128]{2,1,0:T(8,128)S(1)}, u32[]{:S(2)}, u32[]{:S(2)}) async-start(f32[16,24,128]{2,1,0:T(8,128)} %broadcast_in_dim.56), calls=%async_computation.7 | async-start | bytes 393216 | tf_op jit(solution)/shard_map/all_to_all | solution.py:14

commit v3 on v2

--- a/solution.py
+++ b/solution.py
@@ -31,6 +31,14 @@
     return high, (v - high.astype(f32)).astype(bf16)
 
 
+def halve(v, axis, name, bit):
+    mine = lax.axis_index(name) // bit % 2 == 0
+    low, high = lax.index_in_dim(v, 0, axis, False), lax.index_in_dim(v, 1, axis, False)
+    got = lax.ppermute(jnp.where(mine, high, low), name, [(i, i ^ bit) for i in range(4)])
+    kept = jnp.where(mine, low, high)
+    return jnp.where(mine, jnp.stack([kept, got], axis), jnp.stack([got, kept], axis))
+
+
 def local(queries, passages, positive, hidden, lengths, w_down, w_up):
     zl_n, y_n, x_n = lax.axis_size("zl"), lax.axis_size("y"), lax.axis_size("x")
     c, y, h, x = (lax.axis_index(a) for a in ("c", "y", "h", "x"))
@@ -42,10 +50,11 @@
     cols = zl_n * half
     own = rows // plane
 
-    part = [lax.dynamic_slice_in_dim(w, c * (w.shape[0] // 2), w.shape[0] // 2) for w in (w_down, w_up)]
-    pack = jnp.concatenate([queries] + part, axis=0)
-    both = in_order(h == 0, pack, swap(pack, "h"))
-    q_mine, w_both = both[:, :rows], both[:, rows:]
+    down_c = lax.dynamic_slice_in_dim(w_down, c * (width // 2), width // 2)
+    both = jnp.concatenate([queries, down_c, w_up], axis=0)
+    both = in_order(h == 0, both, swap(both, "h"))
+    q_mine, w_both = both[:, :rows], both[:, rows : rows + width // 2]
+    up2 = both[:, rows + width // 2 :]
     q_both = in_order(c == 0, q_mine, swap(q_mine, "c"))
     q_all = q_both.transpose(0, 2, 1, 3).reshape(2 * rows, 2 * width)
 
@@ -63,7 +72,9 @@
     qw_part = lax.dot_general(q_side, w_up, (((1,), (1,)), ((), ())), preferred_element_type=f32)
     sent = jnp.concatenate([part, qw_part], axis=1).reshape(2 * plane, own, cols + rank)
     got = exchange(sent, ("c", "y", "x"))
-    got, w_both = lax.optimization_barrier((got, w_both))
+    xf = hidden.astype(f32)
+    rs = lax.rsqrt(jnp.mean(xf * xf, axis=-1, keepdims=True) + eps)
+    got, w_both, rs = lax.optimization_barrier((got, w_both, rs))
     got = jnp.sum(got.reshape(2, plane, own, cols + rank), axis=1)
     scores = inv_temp * got[:, :, :cols]
     qw = got[0, :, cols:] + got[1, :, cols:]
@@ -94,11 +105,8 @@
     sent, w_half = lax.optimization_barrier((sent, w_half))
     got = exchange(sent.reshape(2 * plane, own, step), ("c", "y", "x"))
 
-    w_all = in_order(c == 0, w_half, swap(w_half, "c")).reshape(2, y_n, x_n, 2, -1, rank)
-    wd = w_all[:, :, :, :, : width // 2].transpose(1, 3, 2, 0, 4, 5).reshape(-1, rank)
-    wu = w_all[:, :, :, :, width // 2 :].transpose(0, 4, 1, 3, 2, 5).reshape(rank, -1)
-    xf = hidden.astype(f32)
-    rs = lax.rsqrt(jnp.mean(xf * xf, axis=-1, keepdims=True) + eps)
+    wd = in_order(c == 0, w_half, swap(w_half, "c")).reshape(2, y_n, x_n, 2, width // 2, rank)
+    wd = wd.transpose(1, 3, 2, 0, 4, 5).reshape(-1, rank)
     normed = (xf * rs).astype(bf16)
     pre = jnp.dot(normed, wd, preferred_element_type=f32)
     sig = jax.nn.sigmoid(pre)
@@ -131,22 +139,23 @@
     pooled_zl = got[:, 2 * pages :].reshape(zl_n * pages, rank)
 
     dpre = (g * dact[:, None, :]).astype(bf16).reshape(tokens, rank)
-    first, second = dpre[:, : rank // 2], dpre[:, rank // 2 :]
-    turn = (((0,), (0,)), ((), ()))
-    theirs = lax.dot_general(jnp.where(c == 0, second, first), hidden, turn, preferred_element_type=f32)
-    theirs = swap(theirs.astype(bf16), "c")
-    mine = lax.dot_general(jnp.where(c == 0, first, second), hidden, turn, preferred_element_type=f32)
-    down = (mine + theirs.astype(f32)).astype(bf16)
+    down = lax.dot_general(dpre, hidden, (((0,), (0,)), ((), ())), preferred_element_type=f32)
+    first, second = jnp.split(down.astype(bf16), 2)
+    theirs = swap(jnp.where(c == 0, second, first), "c")
+    down = (jnp.where(c == 0, first, second).astype(f32) + theirs.astype(f32)).astype(bf16)
     down = down.reshape(rank // 2, y_n, 2, x_n, width).transpose(1, 3, 2, 0, 4).reshape(plane, rank, width)
     sent = jnp.concatenate([down, spread(pooled_zl, plane)], axis=1)
     sent, gq = lax.optimization_barrier((sent, gq))
     got = exchange(sent, ("y", "x"))
-    gq = jnp.where(c == 0, gq[0], gq[1]) + swap(jnp.where(c == 0, gq[1], gq[0]), "c")
+    gq_0, gq_1 = gq[:, :, :width], gq[:, :, width:]
+    gq = jnp.where(h == 0, gq_0, gq_1) + swap(jnp.where(h == 0, gq_1, gq_0).astype(bf16), "h").astype(f32)
     pooled_all = got[:, rank:].reshape(plane, zl_n, pages, rank).transpose(1, 0, 2, 3).reshape(cols, rank)
     down = jnp.sum(got[:, :rank].astype(f32), axis=0).astype(bf16)
     down = down.reshape(2, zl_n, rank // 2 // zl_n, width).transpose(1, 0, 2, 3)
 
-    sub_embed = (x_mean + jnp.dot(pooled, wu, preferred_element_type=f32)).astype(bf16)
+    lift = lax.dynamic_index_in_dim(pooled_all.reshape(zl_n, half, rank), lax.axis_index("zl"), 0, False)
+    lift = jnp.einsum("pr,hrf->phf", lift, up2, preferred_element_type=f32)
+    lift = lift.reshape(2, 2, 2, 2, pages, 2 * width)
 
     gp = lax.dot_general(coeff, q_all, (((0,), (0,)), ((), ())), preferred_element_type=f32)
     gp = gp.astype(bf16).reshape(zl_n, half, 2, width).transpose(0, 2, 1, 3)
@@ -154,13 +163,15 @@
     up_part = lax.dot_general(u, q_all, (((0,), (0,)), ((), ())), preferred_element_type=f32)
     up_part = up_part.astype(bf16).reshape(zl_n, rank // zl_n, 2, width).transpose(0, 2, 1, 3)
     sent = jnp.concatenate([down, up_part, gp], axis=2)
-    sent, gq = lax.optimization_barrier((sent, gq))
+    sent, gq, lift = lax.optimization_barrier((sent, gq, lift))
     got = exchange(sent.reshape(zl_n * 2, -1, width), ("zl", "h"))
-    gq_0, gq_1 = gq[:, :width], gq[:, width:]
-    gq = jnp.where(h == 0, gq_0, gq_1) + swap(jnp.where(h == 0, gq_1, gq_0), "h")
+    lift = halve(halve(halve(lift, 2, "x", 2), 3, "x", 1), 0, "y", 2)
+    gq = jnp.where(c == 0, gq[0], gq[1]) + swap(jnp.where(c == 0, gq[1], gq[0]), "c")
     grad_queries = (inv_temp * gq).astype(bf16)
-    got, grad_queries = lax.optimization_barrier((got, grad_queries))
+    got, lift = lax.optimization_barrier((got, lift))
     got = got.astype(f32)
+    lift = halve(lift, 1, "y", 1).reshape(y_n, x_n, pages, 2, width)
+    sub_embed = (x_mean + lift.transpose(2, 0, 3, 1, 4).reshape(pages, -1)).astype(bf16)
     n = rank // 2 // zl_n
     step = n + rank // zl_n
     weights = jnp.sum(got[:, :step], axis=0)

time: 218 us -> 215 us (0.986)
  starting transfers between devices: 95.1 us -> 112 us
  waiting for transfers between devices: 81.7 us -> 68.3 us
  matrix products: 13.9 us -> 9.65 us
    ppermute x0 -> x4, starting transfers between devices: none -> 14.9 us  [halve(): lax.ppermute(jnp.where(mine, high, low), name, [(i, i ^ bit) for i in ran...]
    ppermute x7, waiting for transfers between devices: 27.5 us -> 14.1 us  [swap(): return lax.ppermute(x, axis, [(0, 1), (1, 0)])]
    all_to_all x8, starting transfers between devices: 48.9 us -> 56.2 us  [exchange(): return lax.all_to_all(x, axes, split_axis=0, concat_axis=0, tiled=False)]
    ppermute x7, starting transfers between devices: 46.3 us -> 40.5 us  [swap(): return lax.ppermute(x, axis, [(0, 1), (1, 0)])]
    all_to_all x8, waiting for transfers between devices: 54.3 us -> 49.2 us  [exchange(): return lax.all_to_all(x, axes, split_axis=0, concat_axis=0, tiled=False)]
    ppermute x0 -> x4, waiting for transfers between devices: none -> 5.03 us  [halve(): lax.ppermute(jnp.where(mine, high, low), name, [(i, i ^ bit) for i in ran...]
    dot_general x3 -> x2, matrix products: 7.29 us -> 3.06 us  [the longest x1 2.93 us: local(): lax.dot_general(dpre, hidden, (((0,), (0,)), ((), ())), preferred_element...]
  transfers between devices with their start and end apart: 15 -> 19, of which waited for: 12 -> 14; matrix products, arithmetic and copies ran while one was open for 9% -> 7% of each run, Pallas kernels for 0% -> 0%
where the time goes in v3:
time: 215 us; the launch traced here: 214 us
  starting transfers between devices  112 us (52%)
  waiting for transfers between devices  68.3 us (32%)
  other arithmetic  11.8 us (5%)
  local copies, waits for them, and re-layouts  10.9 us (5%)
  matrix products  9.65 us (4%)
    all_to_all x8, starting transfers between devices, exchange(): return lax.all_to_all(x, axes, split_axis=0, concat_axis=0, tiled=False)  56.2 us
    all_to_all x8, waiting for transfers between devices, exchange(): return lax.all_to_all(x, axes, split_axis=0, concat_axis=0, tiled=False)  49.2 us
    ppermute x7, starting transfers between devices, swap(): return lax.ppermute(x, axis, [(0, 1), (1, 0)])  40.5 us
    ppermute x4, starting transfers between devices, halve(): lax.ppermute(jnp.where(mine, high, low), name, [(i, i ^ bit) for i in ran...  14.9 us
    ppermute x7, waiting for transfers between devices, swap(): return lax.ppermute(x, axis, [(0, 1), (1, 0)])  14.1 us
    ppermute x4, waiting for transfers between devices, halve(): lax.ppermute(jnp.where(mine, high, low), name, [(i, i ^ bit) for i in ran...  5.03 us
  transfers between devices with their start and end apart: 19, of which 14 were waited for; matrix products, arithmetic and copies ran while one was open for 7% of the time, Pallas kernels for 0%

profile of v3, /device:TPU:1, one launch (start us, length us, event | category | flops | bytes accessed | tf_op | source)
XLA Modules:
  0.0 213.7 jit_solution(10061705520740848340)
XLA Ops:
  1.4 0.8 fusion.47
  2.2 16.3 %collective-permute-start = (bf16[320,128]{1,0:T(8,128)(2,1)S(1)}, bf16[320,128]{1,0:T(8,128)(2,1)S(1)}, u32[]{:S(2)}, u32[]{:S(2)}) collective-permute-start(bf16[320,128]{1,0:T(8,128)(2,1)S(1)} %get-tuple-element.79), channel_id=1, source_target_pairs={{0,4},{4,0},{1,5},{5,1},{2,6},{6,2},{3,7},{7,3},{8,12},{12,8},{9,1... | collective-permute-start | bytes 245768 | tf_op jit(solution)/shard_map/ppermute | solution.py:22
  18.5 0.8 copy.216
  20.0 4.8 %all-to-all-start = ((bf16[16,64,128]{2,1,0:T(8,128)(2,1)}), bf16[16,64,128]{2,1,0:T(8,128)(2,1)S(1)}, u32[]{:S(2)}, u32[]{:S(2)}) async-start(bf16[16,64,128]{2,1,0:T(8,128)(2,1)} %bitcast.8), calls=%async_computation | async-start | bytes 524288 | tf_op jit(solution)/shard_map/all_to_all | solution.py:14
  24.9 3.1 %collective-permute-start.1 = (bf16[2,128,128]{2,1,0:T(8,128)(2,1)S(1)}, bf16[2,128,128]{2,1,0:T(8,128)(2,1)S(1)}, u32[]{:S(2)}, u32[]{:S(2)}) collective-permute-start(bf16[2,128,128]{2,1,0:T(8,128)(2,1)S(1)} %get-tuple-element.75), channel_id=1, source_target_pairs={{0,32},{32,0},{1,33},{33,1},{2,34},{34,2},{3,35},{35,3},{4,36},{36... | collective-permute-start | bytes 196616 | tf_op jit(solution)/shard_map/ppermute | solution.py:22
  28.1 0.9 collective-permute-done.1
  29.2 0.8 maximum_select_fusion.3
  30.0 0.9 fusion.51
  31.0 9.8 %all-to-all-done = bf16[16,64,128]{2,1,0:T(8,128)(2,1)S(1)} async-done(((bf16[16,64,128]{2,1,0:T(8,128)(2,1)}), bf16[16,64,128]{2,1,0:T(8,128)(2,1)S(1)}, u32[]{:S(2)}, u32[]{:S(2)}) %all-to-all-start) | async-done | bytes 262176 | tf_op jit(solution)/shard_map/all_to_all | solution.py:14
  41.3 0.9 maximum_bitcast_fusion
  42.2 12.2 %all-to-all-start.1 = ((f32[32,8,640]{2,1,0:T(8,128)}), f32[32,8,640]{2,1,0:T(8,128)S(1)}, u32[]{:S(2)}, u32[]{:S(2)}) async-start(f32[32,8,640]{2,1,0:T(8,128)} %maximum_bitcast_fusion), calls=%async_computation.1 | async-start | bytes 1310720 | tf_op jit(solution)/shard_map/all_to_all | solution.py:14
  54.5 3.1 %fusion = f32[512]{0:T(512)S(1)} fusion(bf16[512,4096]{1,0:T(8,128)(2,1)} %param.11), kind=kLoop, calls=%fused_computation.2 | loop fusion | flops 6290944 | bytes 4196352 | tf_op jit(solution)/shard_map/reduce_sum | solution.py:76
  57.6 9.2 %all-to-all-done.1 = f32[32,8,640]{2,1,0:T(8,128)S(1)} async-done(((f32[32,8,640]{2,1,0:T(8,128)}), f32[32,8,640]{2,1,0:T(8,128)S(1)}, u32[]{:S(2)}, u32[]{:S(2)}) %all-to-all-start.1) | async-done | bytes 655392 | tf_op jit(solution)/shard_map/all_to_all | solution.py:14
  67.2 4.1 %collective-permute-start.2 = (f32[16,128]{1,0:T(8,128)S(1)}, f32[16,128]{1,0:T(8,128)S(1)}, u32[]{:S(2)}, u32[]{:S(2)}) collective-permute-start(f32[16,128]{1,0:T(8,128)S(1)} %pad_maximum_fusion.5), channel_id=1, source_target_pairs={{0,4},{4,0},{1,5},{5,1},{2,6},{6,2},{3,7},{7,3},{8,12},{12,8},{9,1... | collective-permute-start | bytes 24584 | tf_op jit(solution)/shard_map/ppermute | solution.py:22
  71.4 0.9 broadcast_in_dim.52
  72.3 3.7 %all-to-all-start.2 = ((bf16[16,2,64,128]{3,2,1,0:T(8,128)(2,1)}), bf16[16,2,64,128]{3,2,1,0:T(8,128)(2,1)S(1)}, u32[]{:S(2)}, u32[]{:S(2)}) async-start(bf16[16,2,64,128]{3,2,1,0:T(8,128)(2,1)} %broadcast_in_dim.52), calls=%async_computation.2 | async-start | bytes 1048576 | tf_op jit(solution)/shard_map/all_to_all | solution.py:14
  76.0 4.3 %collective-permute-done.2 = f32[16,128]{1,0:T(8,128)S(1)} collective-permute-done((f32[16,128]{1,0:T(8,128)S(1)}, f32[16,128]{1,0:T(8,128)S(1)}, u32[]{:S(2)}, u32[]{:S(2)}) %collective-permute-start.2) | collective-permute-done | bytes 8224 | tf_op jit(solution)/shard_map/ppermute | solution.py:22
  80.6 5.6 %all-to-all-done.2 = bf16[16,2,64,128]{3,2,1,0:T(8,128)(2,1)S(1)} async-done(((bf16[16,2,64,128]{3,2,1,0:T(8,128)(2,1)}), bf16[16,2,64,128]{3,2,1,0:T(8,128)(2,1)S(1)}, u32[]{:S(2)}, u32[]{:S(2)}) %all-to-all-start.2) | async-done | bytes 524320 | tf_op jit(solution)/shard_map/all_to_all | solution.py:14
  86.3 0.7 broadcast_in_dim.51
  87.0 4.1 %collective-permute-start.3 = (bf16[16,2,64,128]{3,2,1,0:T(8,128)(2,1)S(1)}, bf16[16,2,64,128]{3,2,1,0:T(8,128)(2,1)S(1)}, u32[]{:S(2)}, u32[]{:S(2)}) collective-permute-start(bf16[16,2,64,128]{3,2,1,0:T(8,128)(2,1)S(1)} %all-to-all-done.2), channel_id=1, source_target_pairs={{0,32},{32,0},{1,33},{33,1},{2,34},{34,2},{3,35},{35,3},{4,36},{36... | collective-permute-start | bytes 1572872 | tf_op jit(solution)/shard_map/ppermute | solution.py:22
  91.3 3.7 %all-to-all-start.3 = ((bf16[32,8,640]{2,1,0:T(8,128)(2,1)}), bf16[32,8,640]{2,1,0:T(8,128)(2,1)S(1)}, u32[]{:S(2)}, u32[]{:S(2)}) async-start(bf16[32,8,640]{2,1,0:T(8,128)(2,1)} %bitcast.19), calls=%async_computation.3 | async-start | bytes 655360 | tf_op jit(solution)/shard_map/all_to_all | solution.py:14
  95.2 1.9 copy-done.1
  97.1 1.3 multiply_multiply_fusion
  98.8 5.0 %all-to-all-done.3 = bf16[32,8,640]{2,1,0:T(8,128)(2,1)S(1)} async-done(((bf16[32,8,640]{2,1,0:T(8,128)(2,1)}), bf16[32,8,640]{2,1,0:T(8,128)(2,1)S(1)}, u32[]{:S(2)}, u32[]{:S(2)}) %all-to-all-start.3) | async-done | bytes 327712 | tf_op jit(solution)/shard_map/all_to_all | solution.py:14
  104.9 8.5 %all-to-all-start.4 = ((bf16[8,12,128]{2,1,0:T(8,128)(2,1)}), bf16[8,12,128]{2,1,0:T(8,128)(2,1)S(1)}, u32[]{:S(2)}, u32[]{:S(2)}) async-start(bf16[8,12,128]{2,1,0:T(8,128)(2,1)} %copy.222), calls=%async_computation.4 | async-start | bytes 65536 | tf_op jit(solution)/shard_map/all_to_all | solution.py:14
  113.4 2.9 %convolution_multiply_fusion = f32[4,4096]{1,0:T(4,128)S(1)} fusion(bf16[512,4096]{1,0:T(8,128)(2,1)} %param.11, f32[4]{0:T(128)S(1)} %convert_divide_fusion, s32[512]{0:T(512)S(1)} %get-tuple-element.82, s32[512]{0:T(512)S(1)} %get-tuple-element.83, s32[4]{0:T(128)S(1)} %copy-done.3), kind=kOutput, calls=%fused_computation.5 | convolution fusion | flops 16799744 | bytes 4263968 | tf_op jit(solution)/shard_map/dot_general | solution.py:120
  116.3 6.7 %all-to-all-done.4 = bf16[8,12,128]{2,1,0:T(8,128)(2,1)S(1)} async-done(((bf16[8,12,128]{2,1,0:T(8,128)(2,1)}), bf16[8,12,128]{2,1,0:T(8,128)(2,1)S(1)}, u32[]{:S(2)}, u32[]{:S(2)}) %all-to-all-start.4) | async-done | bytes 24608 | tf_op jit(solution)/shard_map/all_to_all | solution.py:14
  123.0 2.9 %convolution_convert_fusion = bf16[128,4096]{1,0:T(8,128)(2,1)S(1)} fusion(bf16[512,128]{1,0:T(8,128)(2,1)S(1)} %bitcast.193, bf16[512,4096]{1,0:T(8,128)(2,1)} %param.11), kind=kOutput, calls=%fused_computation.4 | convolution fusion | flops 537395200 | bytes 5373952 | tf_op jit(solution)/shard_map/dot_general | solution.py:142
  126.0 0.8 broadcast_select_fusion
  126.8 4.4 %collective-permute-start.4 = (bf16[64,4096]{1,0:T(8,128)(2,1)}, bf16[64,4096]{1,0:T(8,128)(2,1)S(1)}, u32[]{:S(2)}, u32[]{:S(2)}) collective-permute-start(bf16[64,4096]{1,0:T(8,128)(2,1)} %broadcast_select_fusion), channel_id=1, source_target_pairs={{0,32},{32,0},{1,33},{33,1},{2,34},{34,2},{3,35},{35,3},{4,36},{36... | collective-permute-start | bytes 1572872 | tf_op jit(solution)/shard_map/ppermute | solution.py:22
  131.9 1.1 collective-permute-done.4
  133.8 0.9 pad_maximum_fusion
  134.6 3.6 %all-to-all-start.5 = ((bf16[16,160,128]{2,1,0:T(8,128)(2,1)}), bf16[16,160,128]{2,1,0:T(8,128)(2,1)S(1)}, u32[]{:S(2)}, u32[]{:S(2)}) async-start(bf16[16,160,128]{2,1,0:T(8,128)(2,1)} %pad_maximum_fusion), calls=%async_computation.5 | async-start | bytes 1310720 | tf_op jit(solution)/shard_map/all_to_all | solution.py:14
  138.3 5.5 %collective-permute-start.5 = (bf16[2,128,128]{2,1,0:T(8,128)(2,1)S(1)}, bf16[2,128,128]{2,1,0:T(8,128)(2,1)S(1)}, u32[]{:S(2)}, u32[]{:S(2)}) collective-permute-start(bf16[2,128,128]{2,1,0:T(8,128)(2,1)S(1)} %select_convert_fusion), channel_id=1, source_target_pairs={{0,4},{4,0},{1,5},{5,1},{2,6},{6,2},{3,7},{7,3},{8,12},{12,8},{9,1... | collective-permute-start | bytes 196616 | tf_op jit(solution)/shard_map/ppermute | solution.py:22
  144.2 7.8 %collective-permute-done.5 = bf16[2,128,128]{2,1,0:T(8,128)(2,1)S(1)} collective-permute-done((bf16[2,128,128]{2,1,0:T(8,128)(2,1)S(1)}, bf16[2,128,128]{2,1,0:T(8,128)(2,1)S(1)}, u32[]{:S(2)}, u32[]{:S(2)}) %collective-permute-start.5) | collective-permute-done | bytes 65568 | tf_op jit(solution)/shard_map/ppermute | solution.py:22
  153.0 0.8 pad_maximum_fusion.1
  153.8 4.9 %collective-permute-start.7 = (f32[2,2,2,4,256]{4,3,2,1,0:T(4,128)S(1)}, f32[2,2,2,4,256]{4,3,2,1,0:T(4,128)S(1)}, u32[]{:S(2)}, u32[]{:S(2)}) collective-permute-start(f32[2,2,2,4,256]{4,3,2,1,0:T(4,128)S(1)} %fusion.22), channel_id=1, source_target_pairs={{0,2},{1,3},{2,0},{3,1},{4,6},{5,7},{6,4},{7,5},{8,10},{9,11},{10,... | collective-permute-start | bytes 98312 | tf_op jit(solution)/shard_map/ppermute | solution.py:37
  158.7 8.8 %all-to-all-start.6 = ((bf16[16,88,128]{2,1,0:T(8,128)(2,1)}), bf16[16,88,128]{2,1,0:T(8,128)(2,1)S(1)}, u32[]{:S(2)}, u32[]{:S(2)}) async-start(bf16[16,88,128]{2,1,0:T(8,128)(2,1)} %bitcast.50), calls=%async_computation.6 | async-start | bytes 720896 | tf_op jit(solution)/shard_map/all_to_all | solution.py:14
  167.6 3.0 %collective-permute-start.6 = (f32[128,128]{1,0:T(8,128)S(1)}, f32[128,128]{1,0:T(8,128)S(1)}, u32[]{:S(2)}, u32[]{:S(2)}) collective-permute-start(f32[128,128]{1,0:T(8,128)S(1)} %select_bitcast_fusion), channel_id=1, source_target_pairs={{0,32},{32,0},{1,33},{33,1},{2,34},{34,2},{3,35},{35,3},{4,36},{36... | collective-permute-start | bytes 196616 | tf_op jit(solution)/shard_map/ppermute | solution.py:22
  170.6 2.2 %collective-permute-start.8 = (f32[2,2,2,4,256]{4,3,1,0,2:T(4,128)S(1)}, f32[2,2,2,4,256]{4,3,1,0,2:T(4,128)S(1)}, u32[]{:S(2)}, u32[]{:S(2)}) collective-permute-start(f32[2,2,2,4,256]{4,3,1,0,2:T(4,128)S(1)} %select_bitcast_fusion.2), channel_id=1, source_target_pairs={{0,1},{1,0},{2,3},{3,2},{4,5},{5,4},{6,7},{7,6},{8,9},{9,8},{10,11... | collective-permute-start | bytes 98312 | tf_op jit(solution)/shard_map/ppermute | solution.py:37
  172.8 2.7 %collective-permute-done.8 = f32[2,2,2,4,256]{4,3,1,0,2:T(4,128)S(1)} collective-permute-done((f32[2,2,2,4,256]{4,3,1,0,2:T(4,128)S(1)}, f32[2,2,2,4,256]{4,3,1,0,2:T(4,128)S(1)}, u32[]{:S(2)}, u32[]{:S(2)}) %collective-permute-start.8) | collective-permute-done | bytes 32800 | tf_op jit(solution)/shard_map/ppermute | solution.py:37
  175.6 4.6 %collective-permute-start.9 = (f32[2,2,2,4,256]{4,3,0,1,2:T(4,128)S(1)}, f32[2,2,2,4,256]{4,3,0,1,2:T(4,128)S(1)}, u32[]{:S(2)}, u32[]{:S(2)}) collective-permute-start(f32[2,2,2,4,256]{4,3,0,1,2:T(4,128)S(1)} %select_bitcast_fusion.1), channel_id=1, source_target_pairs={{0,16},{8,24},{16,0},{24,8},{1,17},{9,25},{17,1},{25,9},{2,18},{10... | collective-permute-start | bytes 98312 | tf_op jit(solution)/shard_map/ppermute | solution.py:37
  180.9 1.1 collective-permute-done.9
  182.1 3.8 %all-to-all-done.6 = bf16[16,88,128]{2,1,0:T(8,128)(2,1)S(1)} async-done(((bf16[16,88,128]{2,1,0:T(8,128)(2,1)}), bf16[16,88,128]{2,1,0:T(8,128)(2,1)S(1)}, u32[]{:S(2)}, u32[]{:S(2)}) %all-to-all-start.6) | async-done | bytes 360480 | tf_op jit(solution)/shard_map/all_to_all | solution.py:14
  186.7 10.9 %all-to-all-start.7 = ((f32[16,24,128]{2,1,0:T(8,128)}), f32[16,24,128]{2,1,0:T(8,128)S(1)}, u32[]{:S(2)}, u32[]{:S(2)}) async-start(f32[16,24,128]{2,1,0:T(8,128)} %broadcast_in_dim.56), calls=%async_computation.7 | async-start | bytes 393216 | tf_op jit(solution)/shard_map/all_to_all | solution.py:14
  197.6 3.1 %collective-permute-start.10 = (f32[2,2,2,4,256]{4,3,1,2,0:T(4,128)S(1)}, f32[2,2,2,4,256]{4,3,1,2,0:T(4,128)S(1)}, u32[]{:S(2)}, u32[]{:S(2)}) collective-permute-start(f32[2,2,2,4,256]{4,3,1,2,0:T(4,128)S(1)} %fusion.21), channel_id=1, source_target_pairs={{0,8},{8,0},{16,24},{24,16},{1,9},{9,1},{17,25},{25,17},{2,10},{10... | collective-permute-start | bytes 98312 | tf_op jit(solution)/shard_map/ppermute | solution.py:37
  201.4 1.2 collective-permute-done.10
  203.3 8.9 %all-to-all-done.7 = f32[16,24,128]{2,1,0:T(8,128)S(1)} async-done(((f32[16,24,128]{2,1,0:T(8,128)}), f32[16,24,128]{2,1,0:T(8,128)S(1)}, u32[]{:S(2)}, u32[]{:S(2)}) %all-to-all-start.7) | async-done | bytes 196640 | tf_op jit(solution)/shard_map/all_to_all | solution.py:14
  (116 shorter events, 11.8 us)
Async XLA Ops:
  0.6 0.8 copy-start
  2.2 22.7 %collective-permute-start = (bf16[320,128]{1,0:T(8,128)(2,1)S(1)}, bf16[320,128]{1,0:T(8,128)(2,1)S(1)}, u32[]{:S(2)}, u32[]{:S(2)}) collective-permute-start(bf16[320,128]{1,0:T(8,128)(2,1)S(1)} %get-tuple-element.79), channel_id=1, source_target_pairs={{0,4},{4,0},{1,5},{5,1},{2,6},{6,2},{3,7},{7,3},{8,12},{12,8},{9,1... | collective-permute-start | bytes 245768 | tf_op jit(solution)/shard_map/ppermute | solution.py:22
  20.0 20.8 %all-to-all-start = ((bf16[16,64,128]{2,1,0:T(8,128)(2,1)}), bf16[16,64,128]{2,1,0:T(8,128)(2,1)S(1)}, u32[]{:S(2)}, u32[]{:S(2)}) async-start(bf16[16,64,128]{2,1,0:T(8,128)(2,1)} %bitcast.8), calls=%async_computation | async-start | bytes 524288 | tf_op jit(solution)/shard_map/all_to_all | solution.py:14
  24.9 4.0 %collective-permute-start.1 = (bf16[2,128,128]{2,1,0:T(8,128)(2,1)S(1)}, bf16[2,128,128]{2,1,0:T(8,128)(2,1)S(1)}, u32[]{:S(2)}, u32[]{:S(2)}) collective-permute-start(bf16[2,128,128]{2,1,0:T(8,128)(2,1)S(1)} %get-tuple-element.75), channel_id=1, source_target_pairs={{0,32},{32,0},{1,33},{33,1},{2,34},{34,2},{3,35},{35,3},{4,36},{36... | collective-permute-start | bytes 196616 | tf_op jit(solution)/shard_map/ppermute | solution.py:22
  41.0 30.2 %copy-start.4 = (s32[128]{0:T(128)S(1)}, s32[128]{0:T(128)}, u32[]{:S(2)}) copy-start(s32[128]{0:T(128)} %param.10) | copy-start | bytes 1540
  42.2 38.3 %copy-start.2 = (s32[2,512]{1,0:T(2,128)S(1)}, s32[2,512]{1,0:T(2,128)}, u32[]{:S(2)}) copy-start(s32[2,512]{1,0:T(2,128)} %constant.165) | copy-start | bytes 12292
  42.2 49.0 %copy-start.3 = (s32[4]{0:T(128)S(1)}, s32[4]{0:T(128)}, u32[]{:S(2)}) copy-start(s32[4]{0:T(128)} %param.12) | copy-start | bytes 52
  42.2 24.5 %all-to-all-start.1 = ((f32[32,8,640]{2,1,0:T(8,128)}), f32[32,8,640]{2,1,0:T(8,128)S(1)}, u32[]{:S(2)}, u32[]{:S(2)}) async-start(f32[32,8,640]{2,1,0:T(8,128)} %maximum_bitcast_fusion), calls=%async_computation.1 | async-start | bytes 1310720 | tf_op jit(solution)/shard_map/all_to_all | solution.py:14
  67.2 13.1 %collective-permute-start.2 = (f32[16,128]{1,0:T(8,128)S(1)}, f32[16,128]{1,0:T(8,128)S(1)}, u32[]{:S(2)}, u32[]{:S(2)}) collective-permute-start(f32[16,128]{1,0:T(8,128)S(1)} %pad_maximum_fusion.5), channel_id=1, source_target_pairs={{0,4},{4,0},{1,5},{5,1},{2,6},{6,2},{3,7},{7,3},{8,12},{12,8},{9,1... | collective-permute-start | bytes 24584 | tf_op jit(solution)/shard_map/ppermute | solution.py:22
  72.3 14.0 %all-to-all-start.2 = ((bf16[16,2,64,128]{3,2,1,0:T(8,128)(2,1)}), bf16[16,2,64,128]{3,2,1,0:T(8,128)(2,1)S(1)}, u32[]{:S(2)}, u32[]{:S(2)}) async-start(bf16[16,2,64,128]{3,2,1,0:T(8,128)(2,1)} %broadcast_in_dim.52), calls=%async_computation.2 | async-start | bytes 1048576 | tf_op jit(solution)/shard_map/all_to_all | solution.py:14
  87.0 7.9 %collective-permute-start.3 = (bf16[16,2,64,128]{3,2,1,0:T(8,128)(2,1)S(1)}, bf16[16,2,64,128]{3,2,1,0:T(8,128)(2,1)S(1)}, u32[]{:S(2)}, u32[]{:S(2)}) collective-permute-start(bf16[16,2,64,128]{3,2,1,0:T(8,128)(2,1)S(1)} %all-to-all-done.2), channel_id=1, source_target_pairs={{0,32},{32,0},{1,33},{33,1},{2,34},{34,2},{3,35},{35,3},{4,36},{36... | collective-permute-start | bytes 1572872 | tf_op jit(solution)/shard_map/ppermute | solution.py:22
  91.3 12.6 %all-to-all-start.3 = ((bf16[32,8,640]{2,1,0:T(8,128)(2,1)}), bf16[32,8,640]{2,1,0:T(8,128)(2,1)S(1)}, u32[]{:S(2)}, u32[]{:S(2)}) async-start(bf16[32,8,640]{2,1,0:T(8,128)(2,1)} %bitcast.19), calls=%async_computation.3 | async-start | bytes 655360 | tf_op jit(solution)/shard_map/all_to_all | solution.py:14
  94.9 2.2 %copy-start.1 = (bf16[512,4096]{1,0:T(8,128)(2,1)S(1)}, bf16[512,4096]{1,0:T(8,128)(2,1)}, u32[]{:S(2)}) copy-start(bf16[512,4096]{1,0:T(8,128)(2,1)} %param.11) | copy-start | bytes 12582916
  104.9 18.1 %all-to-all-start.4 = ((bf16[8,12,128]{2,1,0:T(8,128)(2,1)}), bf16[8,12,128]{2,1,0:T(8,128)(2,1)S(1)}, u32[]{:S(2)}, u32[]{:S(2)}) async-start(bf16[8,12,128]{2,1,0:T(8,128)(2,1)} %copy.222), calls=%async_computation.4 | async-start | bytes 65536 | tf_op jit(solution)/shard_map/all_to_all | solution.py:14
  126.8 6.1 %collective-permute-start.4 = (bf16[64,4096]{1,0:T(8,128)(2,1)}, bf16[64,4096]{1,0:T(8,128)(2,1)S(1)}, u32[]{:S(2)}, u32[]{:S(2)}) collective-permute-start(bf16[64,4096]{1,0:T(8,128)(2,1)} %broadcast_select_fusion), channel_id=1, source_target_pairs={{0,32},{32,0},{1,33},{33,1},{2,34},{34,2},{3,35},{35,3},{4,36},{36... | collective-permute-start | bytes 1572872 | tf_op jit(solution)/shard_map/ppermute | solution.py:22
  134.6 17.4 %all-to-all-start.5 = ((bf16[16,160,128]{2,1,0:T(8,128)(2,1)}), bf16[16,160,128]{2,1,0:T(8,128)(2,1)S(1)}, u32[]{:S(2)}, u32[]{:S(2)}) async-start(bf16[16,160,128]{2,1,0:T(8,128)(2,1)} %pad_maximum_fusion), calls=%async_computation.5 | async-start | bytes 1310720 | tf_op jit(solution)/shard_map/all_to_all | solution.py:14
  138.3 13.7 %collective-permute-start.5 = (bf16[2,128,128]{2,1,0:T(8,128)(2,1)S(1)}, bf16[2,128,128]{2,1,0:T(8,128)(2,1)S(1)}, u32[]{:S(2)}, u32[]{:S(2)}) collective-permute-start(bf16[2,128,128]{2,1,0:T(8,128)(2,1)S(1)} %select_convert_fusion), channel_id=1, source_target_pairs={{0,4},{4,0},{1,5},{5,1},{2,6},{6,2},{3,7},{7,3},{8,12},{12,8},{9,1... | collective-permute-start | bytes 196616 | tf_op jit(solution)/shard_map/ppermute | solution.py:22
  153.8 16.7 %collective-permute-start.7 = (f32[2,2,2,4,256]{4,3,2,1,0:T(4,128)S(1)}, f32[2,2,2,4,256]{4,3,2,1,0:T(4,128)S(1)}, u32[]{:S(2)}, u32[]{:S(2)}) collective-permute-start(f32[2,2,2,4,256]{4,3,2,1,0:T(4,128)S(1)} %fusion.22), channel_id=1, source_target_pairs={{0,2},{1,3},{2,0},{3,1},{4,6},{5,7},{6,4},{7,5},{8,10},{9,11},{10,... | collective-permute-start | bytes 98312 | tf_op jit(solution)/shard_map/ppermute | solution.py:37
  158.7 27.1 %all-to-all-start.6 = ((bf16[16,88,128]{2,1,0:T(8,128)(2,1)}), bf16[16,88,128]{2,1,0:T(8,128)(2,1)S(1)}, u32[]{:S(2)}, u32[]{:S(2)}) async-start(bf16[16,88,128]{2,1,0:T(8,128)(2,1)} %bitcast.50), calls=%async_computation.6 | async-start | bytes 720896 | tf_op jit(solution)/shard_map/all_to_all | solution.py:14
  167.6 12.7 %collective-permute-start.6 = (f32[128,128]{1,0:T(8,128)S(1)}, f32[128,128]{1,0:T(8,128)S(1)}, u32[]{:S(2)}, u32[]{:S(2)}) collective-permute-start(f32[128,128]{1,0:T(8,128)S(1)} %select_bitcast_fusion), channel_id=1, source_target_pairs={{0,32},{32,0},{1,33},{33,1},{2,34},{34,2},{3,35},{35,3},{4,36},{36... | collective-permute-start | bytes 196616 | tf_op jit(solution)/shard_map/ppermute | solution.py:22
  170.6 5.0 %collective-permute-start.8 = (f32[2,2,2,4,256]{4,3,1,0,2:T(4,128)S(1)}, f32[2,2,2,4,256]{4,3,1,0,2:T(4,128)S(1)}, u32[]{:S(2)}, u32[]{:S(2)}) collective-permute-start(f32[2,2,2,4,256]{4,3,1,0,2:T(4,128)S(1)} %select_bitcast_fusion.2), channel_id=1, source_target_pairs={{0,1},{1,0},{2,3},{3,2},{4,5},{5,4},{6,7},{7,6},{8,9},{9,8},{10,11... | collective-permute-start | bytes 98312 | tf_op jit(solution)/shard_map/ppermute | solution.py:37
  175.6 6.5 %collective-permute-start.9 = (f32[2,2,2,4,256]{4,3,0,1,2:T(4,128)S(1)}, f32[2,2,2,4,256]{4,3,0,1,2:T(4,128)S(1)}, u32[]{:S(2)}, u32[]{:S(2)}) collective-permute-start(f32[2,2,2,4,256]{4,3,0,1,2:T(4,128)S(1)} %select_bitcast_fusion.1), channel_id=1, source_target_pairs={{0,16},{8,24},{16,0},{24,8},{1,17},{9,25},{17,1},{25,9},{2,18},{10... | collective-permute-start | bytes 98312 | tf_op jit(solution)/shard_map/ppermute | solution.py:37
  186.7 25.5 %all-to-all-start.7 = ((f32[16,24,128]{2,1,0:T(8,128)}), f32[16,24,128]{2,1,0:T(8,128)S(1)}, u32[]{:S(2)}, u32[]{:S(2)}) async-start(f32[16,24,128]{2,1,0:T(8,128)} %broadcast_in_dim.56), calls=%async_computation.7 | async-start | bytes 393216 | tf_op jit(solution)/shard_map/all_to_all | solution.py:14
  197.6 5.0 %collective-permute-start.10 = (f32[2,2,2,4,256]{4,3,1,2,0:T(4,128)S(1)}, f32[2,2,2,4,256]{4,3,1,2,0:T(4,128)S(1)}, u32[]{:S(2)}, u32[]{:S(2)}) collective-permute-start(f32[2,2,2,4,256]{4,3,1,2,0:T(4,128)S(1)} %fusion.21), channel_id=1, source_target_pairs={{0,8},{8,0},{16,24},{24,16},{1,9},{9,1},{17,25},{25,17},{2,10},{10... | collective-permute-start | bytes 98312 | tf_op jit(solution)/shard_map/ppermute | solution.py:37

commit v4 on v3

--- a/solution.py
+++ b/solution.py
@@ -65,28 +65,26 @@
     p_all = p_all.reshape(cols, 2 * width)
 
     part = lax.dot_general(q_all, p_all, (((1,), (1,)), ((), ())), preferred_element_type=f32)
-    q_own = jnp.where(c == 0, jnp.stack([queries, q_both[1, h]]), jnp.stack([q_both[0, h], queries]))
-    q_own = q_own.reshape(2 * rows, width)
-    side = lax.broadcasted_iota(jnp.int32, (1, width), 1) // (width // 2) == c
-    q_side = jnp.where(side, q_own, jnp.zeros_like(q_own))
-    qw_part = lax.dot_general(q_side, w_up, (((1,), (1,)), ((), ())), preferred_element_type=f32)
-    sent = jnp.concatenate([part, qw_part], axis=1).reshape(2 * plane, own, cols + rank)
+    sent = part.reshape(2 * plane, own, cols)
     got = exchange(sent, ("c", "y", "x"))
     xf = hidden.astype(f32)
     rs = lax.rsqrt(jnp.mean(xf * xf, axis=-1, keepdims=True) + eps)
     got, w_both, rs = lax.optimization_barrier((got, w_both, rs))
-    got = jnp.sum(got.reshape(2, plane, own, cols + rank), axis=1)
-    scores = inv_temp * got[:, :, :cols]
-    qw = got[0, :, cols:] + got[1, :, cols:]
+    scores = inv_temp * jnp.sum(got.reshape(2, plane, own, cols), axis=1)
     top = jnp.max(scores, axis=(0, 2))
     e = jnp.exp(scores - top[None, :, None])
     total = jnp.sum(e, axis=(0, 2))
     lane = lax.broadcasted_iota(jnp.int32, (own, rank), 1)
     stats = jnp.where(lane < rank // 2, top[:, None], total[:, None])
-    stats = swap(jnp.concatenate([stats, qw], axis=0), "h")
-    w_half = exchange(spread(w_both, plane), ("y", "x"))
+    stats = swap(stats, "h")
+
+    up_c = jnp.where(c == 0, up2[:, : rank // 2], up2[:, rank // 2 :]).transpose(1, 0, 2).reshape(rank // 2, -1)
+    qw = lax.dot_general(q_all, up_c, (((1,), (1,)), ((), ())), preferred_element_type=f32)
+    qw = qw.reshape(2, plane, own, rank // 2).transpose(1, 2, 0, 3).reshape(plane, own, rank)
+    high, low = split2(qw)
+    sent = jnp.concatenate([spread(w_both.reshape(width, rank), plane), high, low], axis=1)
+    w_half = exchange(sent, ("y", "x"))
     top_o, total_o = stats[:own, 0], stats[:own, rank // 2]
-    qw = qw + stats[own:]
     top_a = jnp.maximum(top, top_o)
     scale = jnp.exp(top - top_a)
     z = total * scale + total_o * jnp.exp(top_o - top_a)
@@ -98,6 +96,8 @@
     onehot = (target[None, :, None] == base[:, None, :]).astype(f32)
     coeff_own = (probs - onehot).astype(bf16)
 
+    qw = jnp.sum(w_half[:, width:].astype(f32).reshape(plane, 2, own, rank), axis=(0, 1))
+    w_half = w_half[:, :width]
     sent = jnp.broadcast_to(qw.astype(bf16)[None], (2, own, rank))
     sent = jnp.concatenate([coeff_own, sent], axis=2)
     step = cols + rank
@@ -124,7 +124,8 @@
 
     got, pooled, g = lax.optimization_barrier((got, pooled, g))
     got = got.reshape(2 * rows, step)
-    coeff, qw_all = got[:, :cols], got[:, cols:]
+    coeff = got[:, :cols]
+    qw_all = got[:, cols:].reshape(2, plane, own, 2, rank // 2).transpose(3, 1, 2, 0, 4).reshape(2 * rows, rank)
 
     c_mine = coeff.reshape(2 * rows, zl_n, plane, pages)
     c_mine = lax.dynamic_slice_in_dim(c_mine, y * x_n + x, 1, axis=2)[:, :, 0]
@@ -163,10 +164,11 @@
     up_part = lax.dot_general(u, q_all, (((0,), (0,)), ((), ())), preferred_element_type=f32)
     up_part = up_part.astype(bf16).reshape(zl_n, rank // zl_n, 2, width).transpose(0, 2, 1, 3)
     sent = jnp.concatenate([down, up_part, gp], axis=2)
-    sent, gq, lift = lax.optimization_barrier((sent, gq, lift))
+    sent, gq = lax.optimization_barrier((sent, gq))
     got = exchange(sent.reshape(zl_n * 2, -1, width), ("zl", "h"))
+    gq = jnp.where(c == 0, gq[0], gq[1]) + swap(jnp.where(c == 0, gq[1], gq[0]), "c")
+    gq, lift = lax.optimization_barrier((gq, lift))
     lift = halve(halve(halve(lift, 2, "x", 2), 3, "x", 1), 0, "y", 2)
-    gq = jnp.where(c == 0, gq[0], gq[1]) + swap(jnp.where(c == 0, gq[1], gq[0]), "c")
     grad_queries = (inv_temp * gq).astype(bf16)
     got, lift = lax.optimization_barrier((got, lift))
     got = got.astype(f32)

time: 215 us -> 213 us (level)
    all_to_all x8, starting transfers between devices: 56.2 us -> 52.6 us  [exchange(): return lax.all_to_all(x, axes, split_axis=0, concat_axis=0, tiled=False)]
  transfers between devices with their start and end apart: 19 -> 19, of which waited for: 14 -> 15; matrix products, arithmetic and copies ran while one was open for 7% -> 7% of each run, Pallas kernels for 0% -> 0%
where the time goes in v4:
time: 213 us; the launch traced here: 212 us
  starting transfers between devices  111 us (52%)
  waiting for transfers between devices  68.5 us (32%)
  local copies, waits for them, and re-layouts  11.4 us (5%)
  other arithmetic  10.1 us (5%)
  matrix products  9.7 us (5%)
    all_to_all x8, starting transfers between devices, exchange(): return lax.all_to_all(x, axes, split_axis=0, concat_axis=0, tiled=False)  52.6 us
    all_to_all x8, waiting for transfers between devices, exchange(): return lax.all_to_all(x, axes, split_axis=0, concat_axis=0, tiled=False)  48.6 us
    ppermute x7, starting transfers between devices, swap(): return lax.ppermute(x, axis, [(0, 1), (1, 0)])  42.4 us
    ppermute x4, starting transfers between devices, halve(): lax.ppermute(jnp.where(mine, high, low), name, [(i, i ^ bit) for i in ran...  15.7 us
    ppermute x7, waiting for transfers between devices, swap(): return lax.ppermute(x, axis, [(0, 1), (1, 0)])  14.1 us
    ppermute x4, waiting for transfers between devices, halve(): lax.ppermute(jnp.where(mine, high, low), name, [(i, i ^ bit) for i in ran...  5.81 us
  transfers between devices with their start and end apart: 19, of which 15 were waited for; matrix products, arithmetic and copies ran while one was open for 7% of the time, Pallas kernels for 0%

profile of v4, /device:TPU:1, one launch (start us, length us, event | category | flops | bytes accessed | tf_op | source)
XLA Modules:
  0.0 211.9 jit_solution(2852587955357742880)
XLA Ops:
  0.7 0.7 copy-done
  1.4 0.8 fusion.39
  2.2 16.3 %collective-permute-start = (bf16[320,128]{1,0:T(8,128)(2,1)S(1)}, bf16[320,128]{1,0:T(8,128)(2,1)S(1)}, u32[]{:S(2)}, u32[]{:S(2)}) collective-permute-start(bf16[320,128]{1,0:T(8,128)(2,1)S(1)} %get-tuple-element.76), channel_id=1, source_target_pairs={{0,4},{4,0},{1,5},{5,1},{2,6},{6,2},{3,7},{7,3},{8,12},{12,8},{9,1... | collective-permute-start | bytes 245768 | tf_op jit(solution)/shard_map/ppermute | solution.py:22
  18.5 0.8 copy.190
  19.2 0.7 broadcast_in_dim.37
  20.0 4.8 %all-to-all-start = ((bf16[16,64,128]{2,1,0:T(8,128)(2,1)}), bf16[16,64,128]{2,1,0:T(8,128)(2,1)S(1)}, u32[]{:S(2)}, u32[]{:S(2)}) async-start(bf16[16,64,128]{2,1,0:T(8,128)(2,1)} %bitcast.8), calls=%async_computation | async-start | bytes 524288 | tf_op jit(solution)/shard_map/all_to_all | solution.py:14
  24.8 3.1 %fusion = f32[512]{0:T(512)S(1)} fusion(bf16[512,4096]{1,0:T(8,128)(2,1)} %param.11), kind=kLoop, calls=%fused_computation.2 | loop fusion | flops 6290944 | bytes 4196352 | tf_op jit(solution)/shard_map/reduce_sum | solution.py:71
  28.0 3.1 %collective-permute-start.1 = (bf16[2,128,128]{2,1,0:T(8,128)(2,1)S(1)}, bf16[2,128,128]{2,1,0:T(8,128)(2,1)S(1)}, u32[]{:S(2)}, u32[]{:S(2)}) collective-permute-start(bf16[2,128,128]{2,1,0:T(8,128)(2,1)S(1)} %get-tuple-element.72), channel_id=1, source_target_pairs={{0,32},{32,0},{1,33},{33,1},{2,34},{34,2},{3,35},{35,3},{4,36},{36... | collective-permute-start | bytes 196616 | tf_op jit(solution)/shard_map/ppermute | solution.py:22
  31.2 0.9 collective-permute-done.1
  32.3 8.4 %all-to-all-done = bf16[16,64,128]{2,1,0:T(8,128)(2,1)S(1)} async-done(((bf16[16,64,128]{2,1,0:T(8,128)(2,1)}), bf16[16,64,128]{2,1,0:T(8,128)(2,1)S(1)}, u32[]{:S(2)}, u32[]{:S(2)}) %all-to-all-start) | async-done | bytes 262176 | tf_op jit(solution)/shard_map/all_to_all | solution.py:14
  41.2 1.1 fusion.44
  42.3 12.1 %all-to-all-start.1 = ((f32[32,8,512]{2,1,0:T(8,128)}), f32[32,8,512]{2,1,0:T(8,128)S(1)}, u32[]{:S(2)}, u32[]{:S(2)}) async-start(f32[32,8,512]{2,1,0:T(8,128)} %fusion.44), calls=%async_computation.1 | async-start | bytes 1048576 | tf_op jit(solution)/shard_map/all_to_all | solution.py:14
  55.0 10.5 %all-to-all-done.1 = f32[32,8,512]{2,1,0:T(8,128)S(1)} async-done(((f32[32,8,512]{2,1,0:T(8,128)}), f32[32,8,512]{2,1,0:T(8,128)S(1)}, u32[]{:S(2)}, u32[]{:S(2)}) %all-to-all-start.1) | async-done | bytes 524320 | tf_op jit(solution)/shard_map/all_to_all | solution.py:14
  66.0 4.1 %collective-permute-start.2 = (f32[8,128]{0,1:T(8,128)S(1)}, f32[8,128]{0,1:T(8,128)S(1)}, u32[]{:S(2)}, u32[]{:S(2)}) collective-permute-start(f32[8,128]{0,1:T(8,128)S(1)} %broadcast_select_fusion.1), channel_id=1, source_target_pairs={{0,4},{4,0},{1,5},{5,1},{2,6},{6,2},{3,7},{7,3},{8,12},{12,8},{9,1... | collective-permute-start | bytes 12296 | tf_op jit(solution)/shard_map/ppermute | solution.py:22
  70.2 0.9 pad_maximum_fusion.1
  71.1 3.6 %all-to-all-start.2 = ((bf16[16,144,128]{2,1,0:T(8,128)(2,1)}), bf16[16,144,128]{2,1,0:T(8,128)(2,1)S(1)}, u32[]{:S(2)}, u32[]{:S(2)}) async-start(bf16[16,144,128]{2,1,0:T(8,128)(2,1)} %pad_maximum_fusion.1), calls=%async_computation.2 | async-start | bytes 1179648 | tf_op jit(solution)/shard_map/all_to_all | solution.py:14
  74.7 5.0 %collective-permute-done.2 = f32[8,128]{0,1:T(8,128)S(1)} collective-permute-done((f32[8,128]{0,1:T(8,128)S(1)}, f32[8,128]{0,1:T(8,128)S(1)}, u32[]{:S(2)}, u32[]{:S(2)}) %collective-permute-start.2) | collective-permute-done | bytes 4128 | tf_op jit(solution)/shard_map/ppermute | solution.py:22
  79.8 5.8 %all-to-all-done.2 = bf16[16,144,128]{2,1,0:T(8,128)(2,1)S(1)} async-done(((bf16[16,144,128]{2,1,0:T(8,128)(2,1)}), bf16[16,144,128]{2,1,0:T(8,128)(2,1)S(1)}, u32[]{:S(2)}, u32[]{:S(2)}) %all-to-all-start.2) | async-done | bytes 589856 | tf_op jit(solution)/shard_map/all_to_all | solution.py:14
  85.7 0.7 broadcast_in_dim.43
  86.4 4.1 %collective-permute-start.3 = (bf16[16,128,128]{2,1,0:T(8,128)(2,1)S(1)}, bf16[16,128,128]{2,1,0:T(8,128)(2,1)S(1)}, u32[]{:S(2)}, u32[]{:S(2)}) collective-permute-start(bf16[16,128,128]{2,1,0:T(8,128)(2,1)S(1)} %slice.135), channel_id=1, source_target_pairs={{0,32},{32,0},{1,33},{33,1},{2,34},{34,2},{3,35},{35,3},{4,36},{36... | collective-permute-start | bytes 1572872 | tf_op jit(solution)/shard_map/ppermute | solution.py:22
  90.7 3.7 %all-to-all-start.3 = ((bf16[32,8,640]{2,1,0:T(8,128)(2,1)}), bf16[32,8,640]{2,1,0:T(8,128)(2,1)S(1)}, u32[]{:S(2)}, u32[]{:S(2)}) async-start(bf16[32,8,640]{2,1,0:T(8,128)(2,1)} %bitcast.20), calls=%async_computation.3 | async-start | bytes 655360 | tf_op jit(solution)/shard_map/all_to_all | solution.py:14
  94.6 1.9 copy-done.1
  96.5 1.3 multiply_multiply_fusion
  98.2 5.0 %all-to-all-done.3 = bf16[32,8,640]{2,1,0:T(8,128)(2,1)S(1)} async-done(((bf16[32,8,640]{2,1,0:T(8,128)(2,1)}), bf16[32,8,640]{2,1,0:T(8,128)(2,1)S(1)}, u32[]{:S(2)}, u32[]{:S(2)}) %all-to-all-start.3) | async-done | bytes 327712 | tf_op jit(solution)/shard_map/all_to_all | solution.py:14
  104.7 8.5 %all-to-all-start.4 = ((bf16[8,12,128]{2,1,0:T(8,128)(2,1)}), bf16[8,12,128]{2,1,0:T(8,128)(2,1)S(1)}, u32[]{:S(2)}, u32[]{:S(2)}) async-start(bf16[8,12,128]{2,1,0:T(8,128)(2,1)} %copy.199), calls=%async_computation.4 | async-start | bytes 65536 | tf_op jit(solution)/shard_map/all_to_all | solution.py:14
  113.2 2.9 %convolution_multiply_fusion = f32[4,4096]{1,0:T(4,128)S(1)} fusion(bf16[512,4096]{1,0:T(8,128)(2,1)} %param.11, f32[4]{0:T(128)S(1)} %convert_divide_fusion, s32[512]{0:T(512)S(1)} %get-tuple-element.79, s32[512]{0:T(512)S(1)} %get-tuple-element.80, s32[4]{0:T(128)S(1)} %copy-done.4), kind=kOutput, calls=%fused_computation.5 | convolution fusion | flops 16799744 | bytes 4263968 | tf_op jit(solution)/shard_map/dot_general | solution.py:120
  116.0 6.7 %all-to-all-done.4 = bf16[8,12,128]{2,1,0:T(8,128)(2,1)S(1)} async-done(((bf16[8,12,128]{2,1,0:T(8,128)(2,1)}), bf16[8,12,128]{2,1,0:T(8,128)(2,1)S(1)}, u32[]{:S(2)}, u32[]{:S(2)}) %all-to-all-start.4) | async-done | bytes 24608 | tf_op jit(solution)/shard_map/all_to_all | solution.py:14
  122.8 2.9 %convolution_convert_fusion = bf16[128,4096]{1,0:T(8,128)(2,1)S(1)} fusion(bf16[512,128]{1,0:T(8,128)(2,1)S(1)} %bitcast.186, bf16[512,4096]{1,0:T(8,128)(2,1)} %param.11), kind=kOutput, calls=%fused_computation.4 | convolution fusion | flops 537395200 | bytes 5373952 | tf_op jit(solution)/shard_map/dot_general | solution.py:143
  125.8 4.4 %collective-permute-start.4 = (bf16[64,4096]{1,0:T(8,128)(2,1)S(1)}, bf16[64,4096]{1,0:T(8,128)(2,1)S(1)}, u32[]{:S(2)}, u32[]{:S(2)}) collective-permute-start(bf16[64,4096]{1,0:T(8,128)(2,1)S(1)} %broadcast_select_fusion), channel_id=1, source_target_pairs={{0,32},{32,0},{1,33},{33,1},{2,34},{34,2},{3,35},{35,3},{4,36},{36... | collective-permute-start | bytes 1572872 | tf_op jit(solution)/shard_map/ppermute | solution.py:22
  130.3 0.7 copy.208
  132.6 0.9 pad_maximum_fusion
  133.5 3.7 %all-to-all-start.5 = ((bf16[16,160,128]{2,1,0:T(8,128)(2,1)}), bf16[16,160,128]{2,1,0:T(8,128)(2,1)S(1)}, u32[]{:S(2)}, u32[]{:S(2)}) async-start(bf16[16,160,128]{2,1,0:T(8,128)(2,1)} %pad_maximum_fusion), calls=%async_computation.5 | async-start | bytes 1310720 | tf_op jit(solution)/shard_map/all_to_all | solution.py:14
  137.2 5.5 %collective-permute-start.5 = (bf16[2,128,128]{2,1,0:T(8,128)(2,1)S(1)}, bf16[2,128,128]{2,1,0:T(8,128)(2,1)S(1)}, u32[]{:S(2)}, u32[]{:S(2)}) collective-permute-start(bf16[2,128,128]{2,1,0:T(8,128)(2,1)S(1)} %select_convert_fusion), channel_id=1, source_target_pairs={{0,4},{4,0},{1,5},{5,1},{2,6},{6,2},{3,7},{7,3},{8,12},{12,8},{9,1... | collective-permute-start | bytes 196616 | tf_op jit(solution)/shard_map/ppermute | solution.py:22
  143.1 7.8 %collective-permute-done.5 = bf16[2,128,128]{2,1,0:T(8,128)(2,1)S(1)} collective-permute-done((bf16[2,128,128]{2,1,0:T(8,128)(2,1)S(1)}, bf16[2,128,128]{2,1,0:T(8,128)(2,1)S(1)}, u32[]{:S(2)}, u32[]{:S(2)}) %collective-permute-start.5) | collective-permute-done | bytes 65568 | tf_op jit(solution)/shard_map/ppermute | solution.py:22
  151.8 0.8 pad_maximum_fusion.2
  152.5 4.8 %collective-permute-start.6 = (f32[128,128]{1,0:T(8,128)S(1)}, f32[128,128]{1,0:T(8,128)S(1)}, u32[]{:S(2)}, u32[]{:S(2)}) collective-permute-start(f32[128,128]{1,0:T(8,128)S(1)} %select_bitcast_fusion), channel_id=1, source_target_pairs={{0,32},{32,0},{1,33},{33,1},{2,34},{34,2},{3,35},{35,3},{4,36},{36... | collective-permute-start | bytes 196616 | tf_op jit(solution)/shard_map/ppermute | solution.py:22
  157.4 6.6 %all-to-all-start.6 = ((bf16[16,88,128]{2,1,0:T(8,128)(2,1)}), bf16[16,88,128]{2,1,0:T(8,128)(2,1)S(1)}, u32[]{:S(2)}, u32[]{:S(2)}) async-start(bf16[16,88,128]{2,1,0:T(8,128)(2,1)} %bitcast.51), calls=%async_computation.6 | async-start | bytes 720896 | tf_op jit(solution)/shard_map/all_to_all | solution.py:14
  164.3 4.7 %collective-permute-start.7 = (f32[2,2,2,4,256]{4,3,2,1,0:T(4,128)S(1)}, f32[2,2,2,4,256]{4,3,2,1,0:T(4,128)S(1)}, u32[]{:S(2)}, u32[]{:S(2)}) collective-permute-start(f32[2,2,2,4,256]{4,3,2,1,0:T(4,128)S(1)} %fusion.16), channel_id=1, source_target_pairs={{0,2},{1,3},{2,0},{3,1},{4,6},{5,7},{6,4},{7,5},{8,10},{9,11},{10,... | collective-permute-start | bytes 98312 | tf_op jit(solution)/shard_map/ppermute | solution.py:37
  169.6 1.2 collective-permute-done.7
  170.8 3.1 %collective-permute-start.8 = (f32[2,2,2,4,256]{4,3,1,0,2:T(4,128)S(1)}, f32[2,2,2,4,256]{4,3,1,0,2:T(4,128)S(1)}, u32[]{:S(2)}, u32[]{:S(2)}) collective-permute-start(f32[2,2,2,4,256]{4,3,1,0,2:T(4,128)S(1)} %select_bitcast_fusion.2), channel_id=1, source_target_pairs={{0,1},{1,0},{2,3},{3,2},{4,5},{5,4},{6,7},{7,6},{8,9},{9,8},{10,11... | collective-permute-start | bytes 98312 | tf_op jit(solution)/shard_map/ppermute | solution.py:37
  174.0 1.8 collective-permute-done.8
  175.8 4.7 %collective-permute-start.9 = (f32[2,2,2,4,256]{4,3,0,1,2:T(4,128)S(1)}, f32[2,2,2,4,256]{4,3,0,1,2:T(4,128)S(1)}, u32[]{:S(2)}, u32[]{:S(2)}) collective-permute-start(f32[2,2,2,4,256]{4,3,0,1,2:T(4,128)S(1)} %select_bitcast_fusion.1), channel_id=1, source_target_pairs={{0,16},{8,24},{16,0},{24,8},{1,17},{9,25},{17,1},{25,9},{2,18},{10... | collective-permute-start | bytes 98312 | tf_op jit(solution)/shard_map/ppermute | solution.py:37
  180.5 1.7 collective-permute-done.9
  182.3 3.2 %all-to-all-done.6 = bf16[16,88,128]{2,1,0:T(8,128)(2,1)S(1)} async-done(((bf16[16,88,128]{2,1,0:T(8,128)(2,1)}), bf16[16,88,128]{2,1,0:T(8,128)(2,1)S(1)}, u32[]{:S(2)}, u32[]{:S(2)}) %all-to-all-start.6) | async-done | bytes 360480 | tf_op jit(solution)/shard_map/all_to_all | solution.py:14
  186.3 9.5 %all-to-all-start.7 = ((f32[16,24,128]{2,1,0:T(8,128)}), f32[16,24,128]{2,1,0:T(8,128)S(1)}, u32[]{:S(2)}, u32[]{:S(2)}) async-start(f32[16,24,128]{2,1,0:T(8,128)} %broadcast_in_dim.47), calls=%async_computation.7 | async-start | bytes 393216 | tf_op jit(solution)/shard_map/all_to_all | solution.py:14
  195.8 3.2 %collective-permute-start.10 = (f32[2,2,2,4,256]{4,3,1,2,0:T(4,128)S(1)}, f32[2,2,2,4,256]{4,3,1,2,0:T(4,128)S(1)}, u32[]{:S(2)}, u32[]{:S(2)}) collective-permute-start(f32[2,2,2,4,256]{4,3,1,2,0:T(4,128)S(1)} %fusion.15), channel_id=1, source_target_pairs={{0,8},{8,0},{16,24},{24,16},{1,9},{9,1},{17,25},{25,17},{2,10},{10... | collective-permute-start | bytes 98312 | tf_op jit(solution)/shard_map/ppermute | solution.py:37
  199.7 1.1 collective-permute-done.10
  201.6 8.9 %all-to-all-done.7 = f32[16,24,128]{2,1,0:T(8,128)S(1)} async-done(((f32[16,24,128]{2,1,0:T(8,128)}), f32[16,24,128]{2,1,0:T(8,128)S(1)}, u32[]{:S(2)}, u32[]{:S(2)}) %all-to-all-start.7) | async-done | bytes 196640 | tf_op jit(solution)/shard_map/all_to_all | solution.py:14
  (124 shorter events, 11.4 us)
Async XLA Ops:
  0.6 0.8 copy-start
  2.2 25.8 %collective-permute-start = (bf16[320,128]{1,0:T(8,128)(2,1)S(1)}, bf16[320,128]{1,0:T(8,128)(2,1)S(1)}, u32[]{:S(2)}, u32[]{:S(2)}) collective-permute-start(bf16[320,128]{1,0:T(8,128)(2,1)S(1)} %get-tuple-element.76), channel_id=1, source_target_pairs={{0,4},{4,0},{1,5},{5,1},{2,6},{6,2},{3,7},{7,3},{8,12},{12,8},{9,1... | collective-permute-start | bytes 245768 | tf_op jit(solution)/shard_map/ppermute | solution.py:22
  20.0 20.8 %all-to-all-start = ((bf16[16,64,128]{2,1,0:T(8,128)(2,1)}), bf16[16,64,128]{2,1,0:T(8,128)(2,1)S(1)}, u32[]{:S(2)}, u32[]{:S(2)}) async-start(bf16[16,64,128]{2,1,0:T(8,128)(2,1)} %bitcast.8), calls=%async_computation | async-start | bytes 524288 | tf_op jit(solution)/shard_map/all_to_all | solution.py:14
  28.0 4.0 %collective-permute-start.1 = (bf16[2,128,128]{2,1,0:T(8,128)(2,1)S(1)}, bf16[2,128,128]{2,1,0:T(8,128)(2,1)S(1)}, u32[]{:S(2)}, u32[]{:S(2)}) collective-permute-start(bf16[2,128,128]{2,1,0:T(8,128)(2,1)S(1)} %get-tuple-element.72), channel_id=1, source_target_pairs={{0,32},{32,0},{1,33},{33,1},{2,34},{34,2},{3,35},{35,3},{4,36},{36... | collective-permute-start | bytes 196616 | tf_op jit(solution)/shard_map/ppermute | solution.py:22
  32.2 42.4 %copy-start.5 = (s32[128]{0:T(128)S(1)}, s32[128]{0:T(128)}, u32[]{:S(2)}) copy-start(s32[128]{0:T(128)} %param.10) | copy-start | bytes 1540
  32.2 47.5 %copy-start.3 = (s32[2,512]{1,0:T(2,128)S(1)}, s32[2,512]{1,0:T(2,128)}, u32[]{:S(2)}) copy-start(s32[2,512]{1,0:T(2,128)} %constant.150) | copy-start | bytes 12292
  41.2 49.3 %copy-start.4 = (s32[4]{0:T(128)S(1)}, s32[4]{0:T(128)}, u32[]{:S(2)}) copy-start(s32[4]{0:T(128)} %param.12) | copy-start | bytes 52
  42.3 23.2 %all-to-all-start.1 = ((f32[32,8,512]{2,1,0:T(8,128)}), f32[32,8,512]{2,1,0:T(8,128)S(1)}, u32[]{:S(2)}, u32[]{:S(2)}) async-start(f32[32,8,512]{2,1,0:T(8,128)} %fusion.44), calls=%async_computation.1 | async-start | bytes 1048576 | tf_op jit(solution)/shard_map/all_to_all | solution.py:14
  66.0 13.7 %collective-permute-start.2 = (f32[8,128]{0,1:T(8,128)S(1)}, f32[8,128]{0,1:T(8,128)S(1)}, u32[]{:S(2)}, u32[]{:S(2)}) collective-permute-start(f32[8,128]{0,1:T(8,128)S(1)} %broadcast_select_fusion.1), channel_id=1, source_target_pairs={{0,4},{4,0},{1,5},{5,1},{2,6},{6,2},{3,7},{7,3},{8,12},{12,8},{9,1... | collective-permute-start | bytes 12296 | tf_op jit(solution)/shard_map/ppermute | solution.py:22
  71.1 14.5 %all-to-all-start.2 = ((bf16[16,144,128]{2,1,0:T(8,128)(2,1)}), bf16[16,144,128]{2,1,0:T(8,128)(2,1)S(1)}, u32[]{:S(2)}, u32[]{:S(2)}) async-start(bf16[16,144,128]{2,1,0:T(8,128)(2,1)} %pad_maximum_fusion.1), calls=%async_computation.2 | async-start | bytes 1179648 | tf_op jit(solution)/shard_map/all_to_all | solution.py:14
  86.4 7.9 %collective-permute-start.3 = (bf16[16,128,128]{2,1,0:T(8,128)(2,1)S(1)}, bf16[16,128,128]{2,1,0:T(8,128)(2,1)S(1)}, u32[]{:S(2)}, u32[]{:S(2)}) collective-permute-start(bf16[16,128,128]{2,1,0:T(8,128)(2,1)S(1)} %slice.135), channel_id=1, source_target_pairs={{0,32},{32,0},{1,33},{33,1},{2,34},{34,2},{3,35},{35,3},{4,36},{36... | collective-permute-start | bytes 1572872 | tf_op jit(solution)/shard_map/ppermute | solution.py:22
  90.7 12.6 %all-to-all-start.3 = ((bf16[32,8,640]{2,1,0:T(8,128)(2,1)}), bf16[32,8,640]{2,1,0:T(8,128)(2,1)S(1)}, u32[]{:S(2)}, u32[]{:S(2)}) async-start(bf16[32,8,640]{2,1,0:T(8,128)(2,1)} %bitcast.20), calls=%async_computation.3 | async-start | bytes 655360 | tf_op jit(solution)/shard_map/all_to_all | solution.py:14
  94.3 2.2 %copy-start.1 = (bf16[512,4096]{1,0:T(8,128)(2,1)S(1)}, bf16[512,4096]{1,0:T(8,128)(2,1)}, u32[]{:S(2)}) copy-start(bf16[512,4096]{1,0:T(8,128)(2,1)} %param.11) | copy-start | bytes 12582916
  104.7 18.1 %all-to-all-start.4 = ((bf16[8,12,128]{2,1,0:T(8,128)(2,1)}), bf16[8,12,128]{2,1,0:T(8,128)(2,1)S(1)}, u32[]{:S(2)}, u32[]{:S(2)}) async-start(bf16[8,12,128]{2,1,0:T(8,128)(2,1)} %copy.199), calls=%async_computation.4 | async-start | bytes 65536 | tf_op jit(solution)/shard_map/all_to_all | solution.py:14
  125.8 5.9 %collective-permute-start.4 = (bf16[64,4096]{1,0:T(8,128)(2,1)S(1)}, bf16[64,4096]{1,0:T(8,128)(2,1)S(1)}, u32[]{:S(2)}, u32[]{:S(2)}) collective-permute-start(bf16[64,4096]{1,0:T(8,128)(2,1)S(1)} %broadcast_select_fusion), channel_id=1, source_target_pairs={{0,32},{32,0},{1,33},{33,1},{2,34},{34,2},{3,35},{35,3},{4,36},{36... | collective-permute-start | bytes 1572872 | tf_op jit(solution)/shard_map/ppermute | solution.py:22
  133.4 30.6 %copy-start.2 = (bf16[2,128,128]{2,1,0:T(8,128)(2,1)S(1)}, bf16[2,128,128]{2,1,0:T(8,128)(2,1)}, u32[]{:S(2)}) copy-start(bf16[2,128,128]{2,1,0:T(8,128)(2,1)} %copy.208) | copy-start | bytes 196612
  133.5 17.5 %all-to-all-start.5 = ((bf16[16,160,128]{2,1,0:T(8,128)(2,1)}), bf16[16,160,128]{2,1,0:T(8,128)(2,1)S(1)}, u32[]{:S(2)}, u32[]{:S(2)}) async-start(bf16[16,160,128]{2,1,0:T(8,128)(2,1)} %pad_maximum_fusion), calls=%async_computation.5 | async-start | bytes 1310720 | tf_op jit(solution)/shard_map/all_to_all | solution.py:14
  137.2 13.7 %collective-permute-start.5 = (bf16[2,128,128]{2,1,0:T(8,128)(2,1)S(1)}, bf16[2,128,128]{2,1,0:T(8,128)(2,1)S(1)}, u32[]{:S(2)}, u32[]{:S(2)}) collective-permute-start(bf16[2,128,128]{2,1,0:T(8,128)(2,1)S(1)} %select_convert_fusion), channel_id=1, source_target_pairs={{0,4},{4,0},{1,5},{5,1},{2,6},{6,2},{3,7},{7,3},{8,12},{12,8},{9,1... | collective-permute-start | bytes 196616 | tf_op jit(solution)/shard_map/ppermute | solution.py:22
  152.5 11.7 %collective-permute-start.6 = (f32[128,128]{1,0:T(8,128)S(1)}, f32[128,128]{1,0:T(8,128)S(1)}, u32[]{:S(2)}, u32[]{:S(2)}) collective-permute-start(f32[128,128]{1,0:T(8,128)S(1)} %select_bitcast_fusion), channel_id=1, source_target_pairs={{0,32},{32,0},{1,33},{33,1},{2,34},{34,2},{3,35},{35,3},{4,36},{36... | collective-permute-start | bytes 196616 | tf_op jit(solution)/shard_map/ppermute | solution.py:22
  157.4 28.0 %all-to-all-start.6 = ((bf16[16,88,128]{2,1,0:T(8,128)(2,1)}), bf16[16,88,128]{2,1,0:T(8,128)(2,1)S(1)}, u32[]{:S(2)}, u32[]{:S(2)}) async-start(bf16[16,88,128]{2,1,0:T(8,128)(2,1)} %bitcast.51), calls=%async_computation.6 | async-start | bytes 720896 | tf_op jit(solution)/shard_map/all_to_all | solution.py:14
  164.3 6.5 %collective-permute-start.7 = (f32[2,2,2,4,256]{4,3,2,1,0:T(4,128)S(1)}, f32[2,2,2,4,256]{4,3,2,1,0:T(4,128)S(1)}, u32[]{:S(2)}, u32[]{:S(2)}) collective-permute-start(f32[2,2,2,4,256]{4,3,2,1,0:T(4,128)S(1)} %fusion.16), channel_id=1, source_target_pairs={{0,2},{1,3},{2,0},{3,1},{4,6},{5,7},{6,4},{7,5},{8,10},{9,11},{10,... | collective-permute-start | bytes 98312 | tf_op jit(solution)/shard_map/ppermute | solution.py:37
  170.8 5.0 %collective-permute-start.8 = (f32[2,2,2,4,256]{4,3,1,0,2:T(4,128)S(1)}, f32[2,2,2,4,256]{4,3,1,0,2:T(4,128)S(1)}, u32[]{:S(2)}, u32[]{:S(2)}) collective-permute-start(f32[2,2,2,4,256]{4,3,1,0,2:T(4,128)S(1)} %select_bitcast_fusion.2), channel_id=1, source_target_pairs={{0,1},{1,0},{2,3},{3,2},{4,5},{5,4},{6,7},{7,6},{8,9},{9,8},{10,11... | collective-permute-start | bytes 98312 | tf_op jit(solution)/shard_map/ppermute | solution.py:37
  175.8 6.5 %collective-permute-start.9 = (f32[2,2,2,4,256]{4,3,0,1,2:T(4,128)S(1)}, f32[2,2,2,4,256]{4,3,0,1,2:T(4,128)S(1)}, u32[]{:S(2)}, u32[]{:S(2)}) collective-permute-start(f32[2,2,2,4,256]{4,3,0,1,2:T(4,128)S(1)} %select_bitcast_fusion.1), channel_id=1, source_target_pairs={{0,16},{8,24},{16,0},{24,8},{1,17},{9,25},{17,1},{25,9},{2,18},{10... | collective-permute-start | bytes 98312 | tf_op jit(solution)/shard_map/ppermute | solution.py:37
  186.3 24.2 %all-to-all-start.7 = ((f32[16,24,128]{2,1,0:T(8,128)}), f32[16,24,128]{2,1,0:T(8,128)S(1)}, u32[]{:S(2)}, u32[]{:S(2)}) async-start(f32[16,24,128]{2,1,0:T(8,128)} %broadcast_in_dim.47), calls=%async_computation.7 | async-start | bytes 393216 | tf_op jit(solution)/shard_map/all_to_all | solution.py:14
  195.8 5.0 %collective-permute-start.10 = (f32[2,2,2,4,256]{4,3,1,2,0:T(4,128)S(1)}, f32[2,2,2,4,256]{4,3,1,2,0:T(4,128)S(1)}, u32[]{:S(2)}, u32[]{:S(2)}) collective-permute-start(f32[2,2,2,4,256]{4,3,1,2,0:T(4,128)S(1)} %fusion.15), channel_id=1, source_target_pairs={{0,8},{8,0},{16,24},{24,16},{1,9},{9,1},{17,25},{25,17},{2,10},{10... | collective-permute-start | bytes 98312 | tf_op jit(solution)/shard_map/ppermute | solution.py:37

commit v5 on v4

--- a/solution.py
+++ b/solution.py
@@ -164,7 +164,6 @@
     up_part = lax.dot_general(u, q_all, (((0,), (0,)), ((), ())), preferred_element_type=f32)
     up_part = up_part.astype(bf16).reshape(zl_n, rank // zl_n, 2, width).transpose(0, 2, 1, 3)
     sent = jnp.concatenate([down, up_part, gp], axis=2)
-    sent, gq = lax.optimization_barrier((sent, gq))
     got = exchange(sent.reshape(zl_n * 2, -1, width), ("zl", "h"))
     gq = jnp.where(c == 0, gq[0], gq[1]) + swap(jnp.where(c == 0, gq[1], gq[0]), "c")
     gq, lift = lax.optimization_barrier((gq, lift))

time: 213 us -> 216 us (1.014)
  waiting for transfers between devices: 68.5 us -> 74.2 us
  starting transfers between devices: 111 us -> 108 us
    ppermute x4, starting transfers between devices: 15.7 us -> 9.96 us  [halve(): lax.ppermute(jnp.where(mine, high, low), name, [(i, i ^ bit) for i in ran...]
    all_to_all x8, waiting for transfers between devices: 48.6 us -> 53 us  [exchange(): return lax.all_to_all(x, axes, split_axis=0, concat_axis=0, tiled=False)]
    ppermute x4, waiting for transfers between devices: 5.81 us -> 9.22 us  [halve(): lax.ppermute(jnp.where(mine, high, low), name, [(i, i ^ bit) for i in ran...]
    all_to_all x8, starting transfers between devices: 52.6 us -> 55.6 us  [exchange(): return lax.all_to_all(x, axes, split_axis=0, concat_axis=0, tiled=False)]
  transfers between devices with their start and end apart: 19 -> 19, of which waited for: 15 -> 16; matrix products, arithmetic and copies ran while one was open for 7% -> 7% of each run, Pallas kernels for 0% -> 0%
where the time goes in v5:
time: 216 us; the launch traced here: 214 us
  starting transfers between devices  108 us (50%)
  waiting for transfers between devices  74.2 us (34%)
  local copies, waits for them, and re-layouts  10.7 us (5%)
  other arithmetic  10.1 us (5%)
  matrix products  9.7 us (4%)
    all_to_all x8, starting transfers between devices, exchange(): return lax.all_to_all(x, axes, split_axis=0, concat_axis=0, tiled=False)  55.6 us
    all_to_all x8, waiting for transfers between devices, exchange(): return lax.all_to_all(x, axes, split_axis=0, concat_axis=0, tiled=False)  53 us
    ppermute x7, starting transfers between devices, swap(): return lax.ppermute(x, axis, [(0, 1), (1, 0)])  42.4 us
    ppermute x7, waiting for transfers between devices, swap(): return lax.ppermute(x, axis, [(0, 1), (1, 0)])  12 us
    ppermute x4, starting transfers between devices, halve(): lax.ppermute(jnp.where(mine, high, low), name, [(i, i ^ bit) for i in ran...  9.96 us
    ppermute x4, waiting for transfers between devices, halve(): lax.ppermute(jnp.where(mine, high, low), name, [(i, i ^ bit) for i in ran...  9.22 us
  transfers between devices with their start and end apart: 19, of which 16 were waited for; matrix products, arithmetic and copies ran while one was open for 7% of the time, Pallas kernels for 0%

profile of v5, /device:TPU:1, one launch (start us, length us, event | category | flops | bytes accessed | tf_op | source)
XLA Modules:
  0.0 214.3 jit_solution(1383447050905916648)
XLA Ops:
  0.7 0.7 copy-done
  1.4 0.8 fusion.39
  2.2 16.3 %collective-permute-start = (bf16[320,128]{1,0:T(8,128)(2,1)S(1)}, bf16[320,128]{1,0:T(8,128)(2,1)S(1)}, u32[]{:S(2)}, u32[]{:S(2)}) collective-permute-start(bf16[320,128]{1,0:T(8,128)(2,1)S(1)} %get-tuple-element.72), channel_id=1, source_target_pairs={{0,4},{4,0},{1,5},{5,1},{2,6},{6,2},{3,7},{7,3},{8,12},{12,8},{9,1... | collective-permute-start | bytes 245768 | tf_op jit(solution)/shard_map/ppermute | solution.py:22
  18.5 0.8 copy.190
  19.2 0.7 broadcast_in_dim.37
  20.0 4.8 %all-to-all-start = ((bf16[16,64,128]{2,1,0:T(8,128)(2,1)}), bf16[16,64,128]{2,1,0:T(8,128)(2,1)S(1)}, u32[]{:S(2)}, u32[]{:S(2)}) async-start(bf16[16,64,128]{2,1,0:T(8,128)(2,1)} %bitcast.8), calls=%async_computation | async-start | bytes 524288 | tf_op jit(solution)/shard_map/all_to_all | solution.py:14
  24.8 3.1 %fusion = f32[512]{0:T(512)S(1)} fusion(bf16[512,4096]{1,0:T(8,128)(2,1)} %param.11), kind=kLoop, calls=%fused_computation.2 | loop fusion | flops 6290944 | bytes 4196352 | tf_op jit(solution)/shard_map/reduce_sum | solution.py:71
  28.0 3.1 %collective-permute-start.1 = (bf16[2,128,128]{2,1,0:T(8,128)(2,1)S(1)}, bf16[2,128,128]{2,1,0:T(8,128)(2,1)S(1)}, u32[]{:S(2)}, u32[]{:S(2)}) collective-permute-start(bf16[2,128,128]{2,1,0:T(8,128)(2,1)S(1)} %get-tuple-element.68), channel_id=1, source_target_pairs={{0,32},{32,0},{1,33},{33,1},{2,34},{34,2},{3,35},{35,3},{4,36},{36... | collective-permute-start | bytes 196616 | tf_op jit(solution)/shard_map/ppermute | solution.py:22
  31.2 0.9 collective-permute-done.1
  32.3 8.4 %all-to-all-done = bf16[16,64,128]{2,1,0:T(8,128)(2,1)S(1)} async-done(((bf16[16,64,128]{2,1,0:T(8,128)(2,1)}), bf16[16,64,128]{2,1,0:T(8,128)(2,1)S(1)}, u32[]{:S(2)}, u32[]{:S(2)}) %all-to-all-start) | async-done | bytes 262176 | tf_op jit(solution)/shard_map/all_to_all | solution.py:14
  41.2 1.1 fusion.44
  42.3 12.1 %all-to-all-start.1 = ((f32[32,8,512]{2,1,0:T(8,128)}), f32[32,8,512]{2,1,0:T(8,128)S(1)}, u32[]{:S(2)}, u32[]{:S(2)}) async-start(f32[32,8,512]{2,1,0:T(8,128)} %fusion.44), calls=%async_computation.1 | async-start | bytes 1048576 | tf_op jit(solution)/shard_map/all_to_all | solution.py:14
  55.0 10.5 %all-to-all-done.1 = f32[32,8,512]{2,1,0:T(8,128)S(1)} async-done(((f32[32,8,512]{2,1,0:T(8,128)}), f32[32,8,512]{2,1,0:T(8,128)S(1)}, u32[]{:S(2)}, u32[]{:S(2)}) %all-to-all-start.1) | async-done | bytes 524320 | tf_op jit(solution)/shard_map/all_to_all | solution.py:14
  66.0 4.1 %collective-permute-start.2 = (f32[8,128]{0,1:T(8,128)S(1)}, f32[8,128]{0,1:T(8,128)S(1)}, u32[]{:S(2)}, u32[]{:S(2)}) collective-permute-start(f32[8,128]{0,1:T(8,128)S(1)} %broadcast_select_fusion.1), channel_id=1, source_target_pairs={{0,4},{4,0},{1,5},{5,1},{2,6},{6,2},{3,7},{7,3},{8,12},{12,8},{9,1... | collective-permute-start | bytes 12296 | tf_op jit(solution)/shard_map/ppermute | solution.py:22
  70.2 0.9 pad_maximum_fusion.1
  71.0 3.6 %all-to-all-start.2 = ((bf16[16,144,128]{2,1,0:T(8,128)(2,1)}), bf16[16,144,128]{2,1,0:T(8,128)(2,1)S(1)}, u32[]{:S(2)}, u32[]{:S(2)}) async-start(bf16[16,144,128]{2,1,0:T(8,128)(2,1)} %pad_maximum_fusion.1), calls=%async_computation.2 | async-start | bytes 1179648 | tf_op jit(solution)/shard_map/all_to_all | solution.py:14
  74.7 5.0 %collective-permute-done.2 = f32[8,128]{0,1:T(8,128)S(1)} collective-permute-done((f32[8,128]{0,1:T(8,128)S(1)}, f32[8,128]{0,1:T(8,128)S(1)}, u32[]{:S(2)}, u32[]{:S(2)}) %collective-permute-start.2) | collective-permute-done | bytes 4128 | tf_op jit(solution)/shard_map/ppermute | solution.py:22
  79.8 5.7 %all-to-all-done.2 = bf16[16,144,128]{2,1,0:T(8,128)(2,1)S(1)} async-done(((bf16[16,144,128]{2,1,0:T(8,128)(2,1)}), bf16[16,144,128]{2,1,0:T(8,128)(2,1)S(1)}, u32[]{:S(2)}, u32[]{:S(2)}) %all-to-all-start.2) | async-done | bytes 589856 | tf_op jit(solution)/shard_map/all_to_all | solution.py:14
  85.6 0.7 broadcast_in_dim.43
  86.4 4.1 %collective-permute-start.3 = (bf16[16,128,128]{2,1,0:T(8,128)(2,1)S(1)}, bf16[16,128,128]{2,1,0:T(8,128)(2,1)S(1)}, u32[]{:S(2)}, u32[]{:S(2)}) collective-permute-start(bf16[16,128,128]{2,1,0:T(8,128)(2,1)S(1)} %slice.135), channel_id=1, source_target_pairs={{0,32},{32,0},{1,33},{33,1},{2,34},{34,2},{3,35},{35,3},{4,36},{36... | collective-permute-start | bytes 1572872 | tf_op jit(solution)/shard_map/ppermute | solution.py:22
  90.7 3.7 %all-to-all-start.3 = ((bf16[32,8,640]{2,1,0:T(8,128)(2,1)}), bf16[32,8,640]{2,1,0:T(8,128)(2,1)S(1)}, u32[]{:S(2)}, u32[]{:S(2)}) async-start(bf16[32,8,640]{2,1,0:T(8,128)(2,1)} %bitcast.20), calls=%async_computation.3 | async-start | bytes 655360 | tf_op jit(solution)/shard_map/all_to_all | solution.py:14
  94.6 1.9 copy-done.1
  96.5 1.3 multiply_multiply_fusion
  98.2 5.0 %all-to-all-done.3 = bf16[32,8,640]{2,1,0:T(8,128)(2,1)S(1)} async-done(((bf16[32,8,640]{2,1,0:T(8,128)(2,1)}), bf16[32,8,640]{2,1,0:T(8,128)(2,1)S(1)}, u32[]{:S(2)}, u32[]{:S(2)}) %all-to-all-start.3) | async-done | bytes 327712 | tf_op jit(solution)/shard_map/all_to_all | solution.py:14
  104.7 8.5 %all-to-all-start.4 = ((bf16[8,12,128]{2,1,0:T(8,128)(2,1)}), bf16[8,12,128]{2,1,0:T(8,128)(2,1)S(1)}, u32[]{:S(2)}, u32[]{:S(2)}) async-start(bf16[8,12,128]{2,1,0:T(8,128)(2,1)} %copy.199), calls=%async_computation.4 | async-start | bytes 65536 | tf_op jit(solution)/shard_map/all_to_all | solution.py:14
  113.2 2.9 %convolution_multiply_fusion = f32[4,4096]{1,0:T(4,128)S(1)} fusion(bf16[512,4096]{1,0:T(8,128)(2,1)} %param.11, f32[4]{0:T(128)S(1)} %convert_divide_fusion, s32[512]{0:T(512)S(1)} %get-tuple-element.75, s32[512]{0:T(512)S(1)} %get-tuple-element.76, s32[4]{0:T(128)S(1)} %copy-done.3), kind=kOutput, calls=%fused_computation.5 | convolution fusion | flops 16799744 | bytes 4263968 | tf_op jit(solution)/shard_map/dot_general | solution.py:120
  116.0 6.7 %all-to-all-done.4 = bf16[8,12,128]{2,1,0:T(8,128)(2,1)S(1)} async-done(((bf16[8,12,128]{2,1,0:T(8,128)(2,1)}), bf16[8,12,128]{2,1,0:T(8,128)(2,1)S(1)}, u32[]{:S(2)}, u32[]{:S(2)}) %all-to-all-start.4) | async-done | bytes 24608 | tf_op jit(solution)/shard_map/all_to_all | solution.py:14
  122.8 2.9 %convolution_convert_fusion = bf16[128,4096]{1,0:T(8,128)(2,1)S(1)} fusion(bf16[512,128]{1,0:T(8,128)(2,1)S(1)} %bitcast.186, bf16[512,4096]{1,0:T(8,128)(2,1)} %param.11), kind=kOutput, calls=%fused_computation.4 | convolution fusion | flops 537395200 | bytes 5373952 | tf_op jit(solution)/shard_map/dot_general | solution.py:143
  125.8 4.4 %collective-permute-start.4 = (bf16[64,4096]{1,0:T(8,128)(2,1)S(1)}, bf16[64,4096]{1,0:T(8,128)(2,1)S(1)}, u32[]{:S(2)}, u32[]{:S(2)}) collective-permute-start(bf16[64,4096]{1,0:T(8,128)(2,1)S(1)} %broadcast_select_fusion), channel_id=1, source_target_pairs={{0,32},{32,0},{1,33},{33,1},{2,34},{34,2},{3,35},{35,3},{4,36},{36... | collective-permute-start | bytes 1572872 | tf_op jit(solution)/shard_map/ppermute | solution.py:22
  130.5 1.3 collective-permute-done.4
  132.5 0.9 pad_maximum_fusion
  133.4 5.5 %collective-permute-start.5 = (bf16[2,128,128]{2,1,0:T(8,128)(2,1)S(1)}, bf16[2,128,128]{2,1,0:T(8,128)(2,1)S(1)}, u32[]{:S(2)}, u32[]{:S(2)}) collective-permute-start(bf16[2,128,128]{2,1,0:T(8,128)(2,1)S(1)} %select_convert_fusion), channel_id=1, source_target_pairs={{0,4},{4,0},{1,5},{5,1},{2,6},{6,2},{3,7},{7,3},{8,12},{12,8},{9,1... | collective-permute-start | bytes 196616 | tf_op jit(solution)/shard_map/ppermute | solution.py:22
  139.1 3.6 %all-to-all-start.5 = ((bf16[16,160,128]{2,1,0:T(8,128)(2,1)}), bf16[16,160,128]{2,1,0:T(8,128)(2,1)S(1)}, u32[]{:S(2)}, u32[]{:S(2)}) async-start(bf16[16,160,128]{2,1,0:T(8,128)(2,1)} %pad_maximum_fusion), calls=%async_computation.5 | async-start | bytes 1310720 | tf_op jit(solution)/shard_map/all_to_all | solution.py:14
  142.8 4.4 %collective-permute-done.5 = bf16[2,128,128]{2,1,0:T(8,128)(2,1)S(1)} collective-permute-done((bf16[2,128,128]{2,1,0:T(8,128)(2,1)S(1)}, bf16[2,128,128]{2,1,0:T(8,128)(2,1)S(1)}, u32[]{:S(2)}, u32[]{:S(2)}) %collective-permute-start.5) | collective-permute-done | bytes 65568 | tf_op jit(solution)/shard_map/ppermute | solution.py:22
  147.2 4.8 %collective-permute-start.6 = (f32[128,128]{1,0:T(8,128)S(1)}, f32[128,128]{1,0:T(8,128)S(1)}, u32[]{:S(2)}, u32[]{:S(2)}) collective-permute-start(f32[128,128]{1,0:T(8,128)S(1)} %select_bitcast_fusion), channel_id=1, source_target_pairs={{0,32},{32,0},{1,33},{33,1},{2,34},{34,2},{3,35},{35,3},{4,36},{36... | collective-permute-start | bytes 196616 | tf_op jit(solution)/shard_map/ppermute | solution.py:22
  152.9 1.9 all-to-all-done.5
  155.3 3.5 %collective-permute-start.7 = (f32[2,2,2,4,256]{4,3,2,1,0:T(4,128)S(1)}, f32[2,2,2,4,256]{4,3,2,1,0:T(4,128)S(1)}, u32[]{:S(2)}, u32[]{:S(2)}) collective-permute-start(f32[2,2,2,4,256]{4,3,2,1,0:T(4,128)S(1)} %fusion.16), channel_id=1, source_target_pairs={{0,2},{1,3},{2,0},{3,1},{4,6},{5,7},{6,4},{7,5},{8,10},{9,11},{10,... | collective-permute-start | bytes 98312 | tf_op jit(solution)/shard_map/ppermute | solution.py:37
  159.4 0.8 pad_maximum_fusion.2
  160.2 8.0 %all-to-all-start.6 = ((bf16[16,88,128]{2,1,0:T(8,128)(2,1)}), bf16[16,88,128]{2,1,0:T(8,128)(2,1)S(1)}, u32[]{:S(2)}, u32[]{:S(2)}) async-start(bf16[16,88,128]{2,1,0:T(8,128)(2,1)} %bitcast.51), calls=%async_computation.6 | async-start | bytes 720896 | tf_op jit(solution)/shard_map/all_to_all | solution.py:14
  168.8 1.9 collective-permute-start.8
  170.8 3.0 %collective-permute-done.8 = f32[2,2,2,4,256]{4,3,1,0,2:T(4,128)S(1)} collective-permute-done((f32[2,2,2,4,256]{4,3,1,0,2:T(4,128)S(1)}, f32[2,2,2,4,256]{4,3,1,0,2:T(4,128)S(1)}, u32[]{:S(2)}, u32[]{:S(2)}) %collective-permute-start.8) | collective-permute-done | bytes 32800 | tf_op jit(solution)/shard_map/ppermute | solution.py:37
  173.8 2.6 %collective-permute-start.9 = (f32[2,2,2,4,256]{4,3,0,1,2:T(4,128)S(1)}, f32[2,2,2,4,256]{4,3,0,1,2:T(4,128)S(1)}, u32[]{:S(2)}, u32[]{:S(2)}) collective-permute-start(f32[2,2,2,4,256]{4,3,0,1,2:T(4,128)S(1)} %select_bitcast_fusion.1), channel_id=1, source_target_pairs={{0,16},{8,24},{16,0},{24,8},{1,17},{9,25},{17,1},{25,9},{2,18},{10... | collective-permute-start | bytes 98312 | tf_op jit(solution)/shard_map/ppermute | solution.py:37
  176.4 3.8 %collective-permute-done.9 = f32[2,2,2,4,256]{4,3,0,1,2:T(4,128)S(1)} collective-permute-done((f32[2,2,2,4,256]{4,3,0,1,2:T(4,128)S(1)}, f32[2,2,2,4,256]{4,3,0,1,2:T(4,128)S(1)}, u32[]{:S(2)}, u32[]{:S(2)}) %collective-permute-start.9) | collective-permute-done | bytes 32800 | tf_op jit(solution)/shard_map/ppermute | solution.py:37
  180.3 5.7 %all-to-all-done.6 = bf16[16,88,128]{2,1,0:T(8,128)(2,1)S(1)} async-done(((bf16[16,88,128]{2,1,0:T(8,128)(2,1)}), bf16[16,88,128]{2,1,0:T(8,128)(2,1)S(1)}, u32[]{:S(2)}, u32[]{:S(2)}) %all-to-all-start.6) | async-done | bytes 360480 | tf_op jit(solution)/shard_map/all_to_all | solution.py:14
  186.9 11.4 %all-to-all-start.7 = ((f32[16,24,128]{2,1,0:T(8,128)}), f32[16,24,128]{2,1,0:T(8,128)S(1)}, u32[]{:S(2)}, u32[]{:S(2)}) async-start(f32[16,24,128]{2,1,0:T(8,128)} %broadcast_in_dim.47), calls=%async_computation.7 | async-start | bytes 393216 | tf_op jit(solution)/shard_map/all_to_all | solution.py:14
  198.2 1.9 collective-permute-start.10
  200.8 2.4 %collective-permute-done.10 = f32[2,2,2,4,256]{4,3,1,2,0:T(4,128)S(1)} collective-permute-done((f32[2,2,2,4,256]{4,3,1,2,0:T(4,128)S(1)}, f32[2,2,2,4,256]{4,3,1,2,0:T(4,128)S(1)}, u32[]{:S(2)}, u32[]{:S(2)}) %collective-permute-start.10) | collective-permute-done | bytes 32800 | tf_op jit(solution)/shard_map/ppermute | solution.py:37
  204.0 8.9 %all-to-all-done.7 = f32[16,24,128]{2,1,0:T(8,128)S(1)} async-done(((f32[16,24,128]{2,1,0:T(8,128)}), f32[16,24,128]{2,1,0:T(8,128)S(1)}, u32[]{:S(2)}, u32[]{:S(2)}) %all-to-all-start.7) | async-done | bytes 196640 | tf_op jit(solution)/shard_map/all_to_all | solution.py:14
  (122 shorter events, 11.6 us)
Async XLA Ops:
  0.6 0.8 copy-start
  2.2 25.8 %collective-permute-start = (bf16[320,128]{1,0:T(8,128)(2,1)S(1)}, bf16[320,128]{1,0:T(8,128)(2,1)S(1)}, u32[]{:S(2)}, u32[]{:S(2)}) collective-permute-start(bf16[320,128]{1,0:T(8,128)(2,1)S(1)} %get-tuple-element.72), channel_id=1, source_target_pairs={{0,4},{4,0},{1,5},{5,1},{2,6},{6,2},{3,7},{7,3},{8,12},{12,8},{9,1... | collective-permute-start | bytes 245768 | tf_op jit(solution)/shard_map/ppermute | solution.py:22
  20.0 20.8 %all-to-all-start = ((bf16[16,64,128]{2,1,0:T(8,128)(2,1)}), bf16[16,64,128]{2,1,0:T(8,128)(2,1)S(1)}, u32[]{:S(2)}, u32[]{:S(2)}) async-start(bf16[16,64,128]{2,1,0:T(8,128)(2,1)} %bitcast.8), calls=%async_computation | async-start | bytes 524288 | tf_op jit(solution)/shard_map/all_to_all | solution.py:14
  28.0 4.0 %collective-permute-start.1 = (bf16[2,128,128]{2,1,0:T(8,128)(2,1)S(1)}, bf16[2,128,128]{2,1,0:T(8,128)(2,1)S(1)}, u32[]{:S(2)}, u32[]{:S(2)}) collective-permute-start(bf16[2,128,128]{2,1,0:T(8,128)(2,1)S(1)} %get-tuple-element.68), channel_id=1, source_target_pairs={{0,32},{32,0},{1,33},{33,1},{2,34},{34,2},{3,35},{35,3},{4,36},{36... | collective-permute-start | bytes 196616 | tf_op jit(solution)/shard_map/ppermute | solution.py:22
  32.2 42.4 %copy-start.4 = (s32[128]{0:T(128)S(1)}, s32[128]{0:T(128)}, u32[]{:S(2)}) copy-start(s32[128]{0:T(128)} %param.10) | copy-start | bytes 1540
  32.2 47.5 %copy-start.2 = (s32[2,512]{1,0:T(2,128)S(1)}, s32[2,512]{1,0:T(2,128)}, u32[]{:S(2)}) copy-start(s32[2,512]{1,0:T(2,128)} %constant.150) | copy-start | bytes 12292
  41.2 49.3 %copy-start.3 = (s32[4]{0:T(128)S(1)}, s32[4]{0:T(128)}, u32[]{:S(2)}) copy-start(s32[4]{0:T(128)} %param.12) | copy-start | bytes 52
  42.3 23.2 %all-to-all-start.1 = ((f32[32,8,512]{2,1,0:T(8,128)}), f32[32,8,512]{2,1,0:T(8,128)S(1)}, u32[]{:S(2)}, u32[]{:S(2)}) async-start(f32[32,8,512]{2,1,0:T(8,128)} %fusion.44), calls=%async_computation.1 | async-start | bytes 1048576 | tf_op jit(solution)/shard_map/all_to_all | solution.py:14
  66.0 13.7 %collective-permute-start.2 = (f32[8,128]{0,1:T(8,128)S(1)}, f32[8,128]{0,1:T(8,128)S(1)}, u32[]{:S(2)}, u32[]{:S(2)}) collective-permute-start(f32[8,128]{0,1:T(8,128)S(1)} %broadcast_select_fusion.1), channel_id=1, source_target_pairs={{0,4},{4,0},{1,5},{5,1},{2,6},{6,2},{3,7},{7,3},{8,12},{12,8},{9,1... | collective-permute-start | bytes 12296 | tf_op jit(solution)/shard_map/ppermute | solution.py:22
  71.0 14.5 %all-to-all-start.2 = ((bf16[16,144,128]{2,1,0:T(8,128)(2,1)}), bf16[16,144,128]{2,1,0:T(8,128)(2,1)S(1)}, u32[]{:S(2)}, u32[]{:S(2)}) async-start(bf16[16,144,128]{2,1,0:T(8,128)(2,1)} %pad_maximum_fusion.1), calls=%async_computation.2 | async-start | bytes 1179648 | tf_op jit(solution)/shard_map/all_to_all | solution.py:14
  86.4 7.9 %collective-permute-start.3 = (bf16[16,128,128]{2,1,0:T(8,128)(2,1)S(1)}, bf16[16,128,128]{2,1,0:T(8,128)(2,1)S(1)}, u32[]{:S(2)}, u32[]{:S(2)}) collective-permute-start(bf16[16,128,128]{2,1,0:T(8,128)(2,1)S(1)} %slice.135), channel_id=1, source_target_pairs={{0,32},{32,0},{1,33},{33,1},{2,34},{34,2},{3,35},{35,3},{4,36},{36... | collective-permute-start | bytes 1572872 | tf_op jit(solution)/shard_map/ppermute | solution.py:22
  90.7 12.6 %all-to-all-start.3 = ((bf16[32,8,640]{2,1,0:T(8,128)(2,1)}), bf16[32,8,640]{2,1,0:T(8,128)(2,1)S(1)}, u32[]{:S(2)}, u32[]{:S(2)}) async-start(bf16[32,8,640]{2,1,0:T(8,128)(2,1)} %bitcast.20), calls=%async_computation.3 | async-start | bytes 655360 | tf_op jit(solution)/shard_map/all_to_all | solution.py:14
  94.3 2.2 %copy-start.1 = (bf16[512,4096]{1,0:T(8,128)(2,1)S(1)}, bf16[512,4096]{1,0:T(8,128)(2,1)}, u32[]{:S(2)}) copy-start(bf16[512,4096]{1,0:T(8,128)(2,1)} %param.11) | copy-start | bytes 12582916
  104.7 18.1 %all-to-all-start.4 = ((bf16[8,12,128]{2,1,0:T(8,128)(2,1)}), bf16[8,12,128]{2,1,0:T(8,128)(2,1)S(1)}, u32[]{:S(2)}, u32[]{:S(2)}) async-start(bf16[8,12,128]{2,1,0:T(8,128)(2,1)} %copy.199), calls=%async_computation.4 | async-start | bytes 65536 | tf_op jit(solution)/shard_map/all_to_all | solution.py:14
  125.8 5.9 %collective-permute-start.4 = (bf16[64,4096]{1,0:T(8,128)(2,1)S(1)}, bf16[64,4096]{1,0:T(8,128)(2,1)S(1)}, u32[]{:S(2)}, u32[]{:S(2)}) collective-permute-start(bf16[64,4096]{1,0:T(8,128)(2,1)S(1)} %broadcast_select_fusion), channel_id=1, source_target_pairs={{0,32},{32,0},{1,33},{33,1},{2,34},{34,2},{3,35},{35,3},{4,36},{36... | collective-permute-start | bytes 1572872 | tf_op jit(solution)/shard_map/ppermute | solution.py:22
  133.4 13.7 %collective-permute-start.5 = (bf16[2,128,128]{2,1,0:T(8,128)(2,1)S(1)}, bf16[2,128,128]{2,1,0:T(8,128)(2,1)S(1)}, u32[]{:S(2)}, u32[]{:S(2)}) collective-permute-start(bf16[2,128,128]{2,1,0:T(8,128)(2,1)S(1)} %select_convert_fusion), channel_id=1, source_target_pairs={{0,4},{4,0},{1,5},{5,1},{2,6},{6,2},{3,7},{7,3},{8,12},{12,8},{9,1... | collective-permute-start | bytes 196616 | tf_op jit(solution)/shard_map/ppermute | solution.py:22
  139.1 15.7 %all-to-all-start.5 = ((bf16[16,160,128]{2,1,0:T(8,128)(2,1)}), bf16[16,160,128]{2,1,0:T(8,128)(2,1)S(1)}, u32[]{:S(2)}, u32[]{:S(2)}) async-start(bf16[16,160,128]{2,1,0:T(8,128)(2,1)} %pad_maximum_fusion), calls=%async_computation.5 | async-start | bytes 1310720 | tf_op jit(solution)/shard_map/all_to_all | solution.py:14
  147.2 5.7 %collective-permute-start.6 = (f32[128,128]{1,0:T(8,128)S(1)}, f32[128,128]{1,0:T(8,128)S(1)}, u32[]{:S(2)}, u32[]{:S(2)}) collective-permute-start(f32[128,128]{1,0:T(8,128)S(1)} %select_bitcast_fusion), channel_id=1, source_target_pairs={{0,32},{32,0},{1,33},{33,1},{2,34},{34,2},{3,35},{35,3},{4,36},{36... | collective-permute-start | bytes 196616 | tf_op jit(solution)/shard_map/ppermute | solution.py:22
  155.3 13.5 %collective-permute-start.7 = (f32[2,2,2,4,256]{4,3,2,1,0:T(4,128)S(1)}, f32[2,2,2,4,256]{4,3,2,1,0:T(4,128)S(1)}, u32[]{:S(2)}, u32[]{:S(2)}) collective-permute-start(f32[2,2,2,4,256]{4,3,2,1,0:T(4,128)S(1)} %fusion.16), channel_id=1, source_target_pairs={{0,2},{1,3},{2,0},{3,1},{4,6},{5,7},{6,4},{7,5},{8,10},{9,11},{10,... | collective-permute-start | bytes 98312 | tf_op jit(solution)/shard_map/ppermute | solution.py:37
  160.2 25.8 %all-to-all-start.6 = ((bf16[16,88,128]{2,1,0:T(8,128)(2,1)}), bf16[16,88,128]{2,1,0:T(8,128)(2,1)S(1)}, u32[]{:S(2)}, u32[]{:S(2)}) async-start(bf16[16,88,128]{2,1,0:T(8,128)(2,1)} %bitcast.51), calls=%async_computation.6 | async-start | bytes 720896 | tf_op jit(solution)/shard_map/all_to_all | solution.py:14
  168.8 5.0 %collective-permute-start.8 = (f32[2,2,2,4,256]{4,3,1,0,2:T(4,128)S(1)}, f32[2,2,2,4,256]{4,3,1,0,2:T(4,128)S(1)}, u32[]{:S(2)}, u32[]{:S(2)}) collective-permute-start(f32[2,2,2,4,256]{4,3,1,0,2:T(4,128)S(1)} %select_bitcast_fusion.2), channel_id=1, source_target_pairs={{0,1},{1,0},{2,3},{3,2},{4,5},{5,4},{6,7},{7,6},{8,9},{9,8},{10,11... | collective-permute-start | bytes 98312 | tf_op jit(solution)/shard_map/ppermute | solution.py:37
  173.8 6.5 %collective-permute-start.9 = (f32[2,2,2,4,256]{4,3,0,1,2:T(4,128)S(1)}, f32[2,2,2,4,256]{4,3,0,1,2:T(4,128)S(1)}, u32[]{:S(2)}, u32[]{:S(2)}) collective-permute-start(f32[2,2,2,4,256]{4,3,0,1,2:T(4,128)S(1)} %select_bitcast_fusion.1), channel_id=1, source_target_pairs={{0,16},{8,24},{16,0},{24,8},{1,17},{9,25},{17,1},{25,9},{2,18},{10... | collective-permute-start | bytes 98312 | tf_op jit(solution)/shard_map/ppermute | solution.py:37
  186.9 26.0 %all-to-all-start.7 = ((f32[16,24,128]{2,1,0:T(8,128)}), f32[16,24,128]{2,1,0:T(8,128)S(1)}, u32[]{:S(2)}, u32[]{:S(2)}) async-start(f32[16,24,128]{2,1,0:T(8,128)} %broadcast_in_dim.47), calls=%async_computation.7 | async-start | bytes 393216 | tf_op jit(solution)/shard_map/all_to_all | solution.py:14
  198.2 5.0 %collective-permute-start.10 = (f32[2,2,2,4,256]{4,3,1,2,0:T(4,128)S(1)}, f32[2,2,2,4,256]{4,3,1,2,0:T(4,128)S(1)}, u32[]{:S(2)}, u32[]{:S(2)}) collective-permute-start(f32[2,2,2,4,256]{4,3,1,2,0:T(4,128)S(1)} %fusion.15), channel_id=1, source_target_pairs={{0,8},{8,0},{16,24},{24,16},{1,9},{9,1},{17,25},{25,17},{2,10},{10... | collective-permute-start | bytes 98312 | tf_op jit(solution)/shard_map/ppermute | solution.py:37
